TPU v7x, 32 devices: a whole 2x2x4 slice. The times are simulated.
32 devices in a mesh: slab: 4 (over y, core), trace: 8 (over z, x).
Axes of the slice: x: 2, y: 2, z: 4, core: 2. Of those that a mesh axis runs over, the one named last changes fastest.
Arguments:
- near_tiles: float32 [4, 2, 2, 768, 6144], P('slab', None, None, None, 'trace'), may hold values from -0.078125 to 0.078125
- near_side: int32 [4, 8], P('slab', 'trace'), may hold values from -1 to 1, as said below
- skeleton: int32 [4, 8, 64], P('slab', 'trace'), may hold values from 0 to 767, as said below
- far_coupling: float32 [4, 2, 512, 512], P('slab', None, 'trace'), may hold values from -0.125 to 0.125
- far_basis: float32 [4, 2, 64, 6144], P('slab', None, None, 'trace'), may hold values from -0.5 to 0.5
- sources: float32 [4, 2, 1, 16, 6144], P('slab', None, None, None, 'trace'), may hold values from -200 to 200
Outputs:
- traces: float32 [4, 2, 1, 16, 6144], P('slab', None, None, None, 'trace')
Inputs may be any that keep to these rules, and one draw needn't show every extreme that they name: `near_side`: each entry is -1 or 1, so that the second near tile lies in a block next to the row's own block; it is 1 for the first block and -1 for the last. `skeleton`: the 64 positions of one block are distinct.
All inputs are finite; a program needn't handle non-finite values.
Results may differ from a plain program's by a relative error of at most 0.0001.
Values sent between devices are 32-bit elements; how exact they have to be, the bound alone decides.
No kernel may reach another device: no remote copies, remote signals or barrier semaphores. Data moves between devices by JAX's collectives and lax.ppermute only.
A program may use at most 128 MiB of HBM per device.

v0:
```python
import jax
import jax.numpy as jnp
from jax import lax
from jax.sharding import PartitionSpec as P

exact_mode = lax.Precision.HIGHEST
small_eps = 1e-06


def extended(block, sides, width):
    for axis, dim in sides:
        count = lax.axis_size(axis)
        forward = [(i, i + 1) for i in range(count - 1)]
        backward = [(target, source) for source, target in forward]
        low = lax.ppermute(
            lax.slice_in_dim(block, block.shape[dim] - width, None, axis=dim), axis, forward
        )
        high = lax.ppermute(lax.slice_in_dim(block, 0, width, axis=dim), axis, backward)
        block = jnp.concatenate([low, block, high], axis=dim)
    return block


def from_behind(x, axis, by):
    size = lax.axis_size(axis)
    pairs = [(i, i + by) for i in range(size) if 0 <= i + by < size]
    return lax.ppermute(x, axis, pairs)


def real_block(part_re, part_im):
    upper = jnp.concatenate([part_re, part_im], axis=1)
    lower = jnp.concatenate([-part_im, part_re], axis=1)
    return jnp.concatenate([upper, lower], axis=0)


def build_mats(tile_set, coupling, basis):
    near_mat = jnp.concatenate(
        [real_block(tile_set[0, 0], tile_set[0, 1]), real_block(tile_set[1, 0], tile_set[1, 1])],
        axis=0,
    )
    coef_mat = real_block(coupling[0].T, coupling[1].T)
    basis_mat = real_block(basis[0], basis[1])
    return (near_mat, coef_mat, basis_mat)


def apply_operator(trace_in, mats, offset, skel_index):
    near_mat, coef_mat, basis_mat = mats
    width = trace_in.shape[2]
    padded = extended(trace_in, (("trace", 2),), width)
    beside_in = lax.dynamic_slice_in_dim(padded, (1 + offset) * width, width, axis=2)
    stacked_in = jnp.concatenate([trace_in[0], trace_in[1], beside_in[0], beside_in[1]], axis=1)
    near_out = jnp.dot(stacked_in, near_mat, precision=exact_mode)
    picked = jnp.take(trace_in, skel_index, axis=2)
    gathered = lax.all_gather(picked, "trace", axis=2, tiled=True)
    rank_count = picked.shape[2]
    block_here = lax.axis_index("trace")
    owner_ids = jnp.arange(gathered.shape[2], dtype=jnp.int32) // rank_count
    keep_mask = ((owner_ids != block_here) & (owner_ids != block_here + offset)).astype(jnp.float32)
    masked = gathered * keep_mask
    coef_out = jnp.dot(
        jnp.concatenate([masked[0], masked[1]], axis=1), coef_mat, precision=exact_mode
    )
    far_out = jnp.dot(coef_out, basis_mat, precision=exact_mode)
    total = near_out + far_out
    return jnp.stack([total[:, :width], total[:, width:]])


def on_device(near_tiles, near_side, skeleton, far_coupling, far_basis, sources):
    mats = build_mats(near_tiles[0], far_coupling[0], far_basis[0])
    offset = near_side[0, 0]
    skel_index = skeleton[0, 0]
    local_src = sources[0]
    batches = local_src.shape[1]
    shots = local_src.shape[2]
    width = local_src.shape[3]
    slab_count = lax.axis_size("slab")
    all_src = local_src.reshape(2, batches * shots, width)
    trace_in = jnp.zeros_like(all_src)
    updated = all_src
    for step_idx in range(slab_count):
        updated = apply_operator(trace_in, mats, offset, skel_index) + all_src
        if step_idx + 1 < slab_count:
            trace_in = from_behind(updated, "slab", 1)
    finished = updated.reshape(2, batches, shots, width)
    partial_sum = jnp.sum(finished * finished, axis=(0, 3))
    total_sum = lax.psum(partial_sum, "trace")
    mean_square = total_sum / (2 * width * lax.axis_size("trace"))
    normed = finished / jnp.sqrt(mean_square + small_eps)[None, :, :, None]
    return normed[None]


def solution(mesh):
    placed = (
        P("slab", None, None, None, "trace"),
        P("slab", "trace"),
        P("slab", "trace", None),
        P("slab", None, "trace", None),
        P("slab", None, None, "trace"),
        P("slab", None, None, None, "trace"),
    )
    return jax.shard_map(
        on_device,
        mesh=mesh,
        in_specs=placed,
        out_specs=P("slab", None, None, None, "trace"),
        check_vma=False,
    )
```

profile of v0, /device:TPU:4, one launch (start us, length us, event | category | flops | bytes accessed | tf_op | source)
XLA Modules:
  0.0 294.6 jit_solution(4480945173706273481)
XLA Ops:
  0.0 4.3 %collective-permute-start = (f32[2,16,768]{2,1,0:T(8,128)S(1)}, f32[2,16,768]{2,1,0:T(8,128)}, u32[]{:S(2)}, u32[]{:S(2)}) collective-permute-start(f32[2,16,768]{2,1,0:T(8,128)S(1)} %broadcast_in_dim.11), channel_id=1, source_target_pairs={{0,1},{1,2},{2,3},{3,4},{4,5},{5,6},{6,7},{8,9},{9,10},{10,11},{11... | collective-permute-start | bytes 294920 | tf_op jit(solution)/shard_map/ppermute | solution.py:15
  4.3 1.3 collective-permute-start.1
  5.6 0.7 compare_select_fusion
  6.3 0.7 compare_and_fusion
  6.9 1.7 slice_bitcast_fusion.6
  8.6 1.6 fusion.76
  10.2 1.8 slice_bitcast_fusion.4
  12.0 0.9 fusion.77
  12.9 7.0 %slice_bitcast_fusion.2 = (f32[768,768]{1,0:T(8,128)S(1)}, f32[768,768]{1,0:T(8,128)}, f32[768,768]{1,0:T(8,128)}, f32[768,768]{1,0:T(8,128)}) fusion(f32[2,2,768,768]{3,2,1,0:T(8,128)} %bitcast.117), kind=kLoop, calls=%fused_computation.7 | loop fusion | bytes 18874368 | tf_op jit(solution)/shard_map/squeeze | solution.py:37
  20.0 2.5 fusion.78
  22.7 0.7 gather_fusion
  23.5 33.0 %all_gather.12 = f32[2,16,512]{1,0,2:T(2,128)S(1)} all-gather(f32[2,16,64]{1,0,2:T(2,128)S(1)} %select_bitcast_fusion.3), channel_id=1, replica_groups=mesh['slab'=4,'trace'=8] {'trace'}, dimensions={2}, use_global_device_ids=true | all-gather | bytes 73728 | tf_op jit(solution)/shard_map/all_gather | solution.py:53
  57.2 0.6 broadcast_multiply_fusion.3
  58.4 1.6 fusion.44
  60.0 16.2 %maximum_maximum_fusion = f32[3072,1536]{1,0:T(8,128)} fusion(f32[768,768]{1,0:T(8,128)} %get-tuple-element.8, f32[768,768]{1,0:T(8,128)} %get-tuple-element.11, f32[768,768]{1,0:T(8,128)} %get-tuple-element.7, f32[768,768]{1,0:T(8,128)} %get-tuple-element.9, f32[768,768]{1,0:T(8,128)} %get-tuple-element.10, f32[768,768]{1,0:T(8,128)S(1)} %get-tuple-element.6), kind=kLoop, calls=%fused_computation.4 | loop fusion | flops 33030144 | bytes 33030144 | tf_op jit(solution)/shard_map/concatenate | solution.py:36
  76.8 0.9 fusion.36
  77.8 12.1 %convolution_add_fusion.3 = f32[16,1536]{1,0:T(8,128)S(1)} fusion(f32[16,1536]{1,0:T(8,128)S(1)} %fusion.28, f32[3072,1536]{1,0:T(8,128)} %maximum_maximum_fusion, f32[16,768]{1,0:T(8,128)S(1)} %get-tuple-element.47, f32[16,768]{1,0:T(8,128)S(1)} %get-tuple-element.46, f32[3072]{0:T(1024)S(1)} %pad.55.clone), kind=kOutput, calls=%fused_computation.12 | convolution fusion | flops 906092544 | bytes 19181568 | tf_op jit(solution)/shard_map/dot_general | solution.py:51
  90.0 1.9 collective-permute-start.2
  91.9 4.0 %collective-permute-done.2 = f32[2,16,768]{2,1,0:T(8,128)S(1)} collective-permute-done((f32[2,16,768]{2,1,0:T(8,128)S(1)}, f32[2,16,768]{2,1,0:T(8,128)S(1)}, u32[]{:S(2)}, u32[]{:S(2)}) %collective-permute-start.2) | collective-permute-done | bytes 98336 | tf_op jit(solution)/shard_map/ppermute | solution.py:26
  96.3 0.7 gather_fusion.1
  97.1 31.5 %all_gather.13 = f32[2,16,512]{1,0,2:T(2,128)S(1)} all-gather(f32[2,16,64]{1,0,2:T(2,128)S(1)} %select_bitcast_fusion.2), channel_id=1, replica_groups=mesh['slab'=4,'trace'=8] {'trace'}, dimensions={2}, use_global_device_ids=true | all-gather | bytes 73728 | tf_op jit(solution)/shard_map/all_gather | solution.py:53
  128.6 0.6 broadcast_multiply_fusion.2
  130.4 3.5 %collective-permute-start.3 = (f32[2,16,768]{2,1,0:T(8,128)S(1)}, f32[2,16,768]{2,1,0:T(8,128)S(1)}, u32[]{:S(2)}, u32[]{:S(2)}) collective-permute-start(f32[2,16,768]{2,1,0:T(8,128)S(1)} %collective-permute-done.2), channel_id=1, source_target_pairs={{0,1},{1,2},{2,3},{3,4},{4,5},{5,6},{6,7},{8,9},{9,10},{10,11},{11... | collective-permute-start | bytes 294920 | tf_op jit(solution)/shard_map/ppermute | solution.py:15
  133.9 1.5 collective-permute-start.4
  136.1 4.3 %collective-permute-done.4 = f32[2,16,768]{2,1,0:T(8,128)S(1)} collective-permute-done((f32[2,16,768]{2,1,0:T(8,128)S(1)}, f32[2,16,768]{2,1,0:T(8,128)S(1)}, u32[]{:S(2)}, u32[]{:S(2)}) %collective-permute-start.4) | collective-permute-done | bytes 98336 | tf_op jit(solution)/shard_map/ppermute | solution.py:18
  140.5 12.1 %convolution_add_fusion.2 = f32[16,1536]{1,0:T(8,128)S(1)} fusion(f32[16,1536]{1,0:T(8,128)S(1)} %fusion.27, f32[3072,1536]{1,0:T(8,128)} %maximum_maximum_fusion, f32[16,768]{1,0:T(8,128)S(1)} %get-tuple-element.43, f32[16,768]{1,0:T(8,128)S(1)} %get-tuple-element.42, f32[16,768]{1,0:T(8,128)S(1)} %get-tuple-element.41, f32[16,768]{1,0:T(8,128)S(1)} %get-tuple-element.40), kind=kOutput, calls=%fused_computation.11 | convolution fusion | flops 906141696 | bytes 19267584 | tf_op jit(solution)/shard_map/dot_general | solution.py:51
  152.6 1.9 collective-permute-start.5
  154.6 4.0 %collective-permute-done.5 = f32[2,16,768]{2,1,0:T(8,128)S(1)} collective-permute-done((f32[2,16,768]{2,1,0:T(8,128)S(1)}, f32[2,16,768]{2,1,0:T(8,128)S(1)}, u32[]{:S(2)}, u32[]{:S(2)}) %collective-permute-start.5) | collective-permute-done | bytes 98336 | tf_op jit(solution)/shard_map/ppermute | solution.py:26
  159.0 0.7 gather_fusion.2
  159.8 31.5 %all_gather.14 = f32[2,16,512]{1,0,2:T(2,128)S(1)} all-gather(f32[2,16,64]{1,0,2:T(2,128)S(1)} %select_bitcast_fusion.1), channel_id=1, replica_groups=mesh['slab'=4,'trace'=8] {'trace'}, dimensions={2}, use_global_device_ids=true | all-gather | bytes 73728 | tf_op jit(solution)/shard_map/all_gather | solution.py:53
  191.3 0.6 broadcast_multiply_fusion.1
  192.6 0.5 fusion.42
  193.1 1.6 collective-permute-start.6
  194.7 1.3 collective-permute-start.7
  196.9 4.3 %collective-permute-done.7 = f32[2,16,768]{2,1,0:T(8,128)S(1)} collective-permute-done((f32[2,16,768]{2,1,0:T(8,128)S(1)}, f32[2,16,768]{2,1,0:T(8,128)S(1)}, u32[]{:S(2)}, u32[]{:S(2)}) %collective-permute-start.7) | collective-permute-done | bytes 98336 | tf_op jit(solution)/shard_map/ppermute | solution.py:18
  201.2 12.1 %convolution_add_fusion.1 = f32[16,1536]{1,0:T(8,128)S(1)} fusion(f32[16,1536]{1,0:T(8,128)S(1)} %fusion.26, f32[3072,1536]{1,0:T(8,128)} %maximum_maximum_fusion, f32[16,768]{1,0:T(8,128)S(1)} %get-tuple-element.37, f32[16,768]{1,0:T(8,128)S(1)} %get-tuple-element.36, f32[16,768]{1,0:T(8,128)S(1)} %get-tuple-element.35, f32[16,768]{1,0:T(8,128)S(1)} %get-tuple-element.34), kind=kOutput, calls=%fused_computation.10 | convolution fusion | flops 906141696 | bytes 19267584 | tf_op jit(solution)/shard_map/dot_general | solution.py:51
  213.4 1.9 collective-permute-start.8
  215.4 4.0 %collective-permute-done.8 = f32[2,16,768]{2,1,0:T(8,128)S(1)} collective-permute-done((f32[2,16,768]{2,1,0:T(8,128)S(1)}, f32[2,16,768]{2,1,0:T(8,128)S(1)}, u32[]{:S(2)}, u32[]{:S(2)}) %collective-permute-start.8) | collective-permute-done | bytes 98336 | tf_op jit(solution)/shard_map/ppermute | solution.py:26
  219.8 0.7 gather_fusion.3
  220.6 31.6 %all_gather.15 = f32[2,16,512]{1,0,2:T(2,128)S(1)} all-gather(f32[2,16,64]{1,0,2:T(2,128)S(1)} %select_bitcast_fusion), channel_id=1, replica_groups=mesh['slab'=4,'trace'=8] {'trace'}, dimensions={2}, use_global_device_ids=true | all-gather | bytes 73728 | tf_op jit(solution)/shard_map/all_gather | solution.py:53
  252.2 0.6 broadcast_multiply_fusion
  253.4 0.5 fusion.41
  253.9 1.3 collective-permute-start.10
  255.2 4.8 %collective-permute-start.9 = (f32[2,16,768]{2,1,0:T(8,128)S(1)}, f32[2,16,768]{2,1,0:T(8,128)S(1)}, u32[]{:S(2)}, u32[]{:S(2)}) collective-permute-start(f32[2,16,768]{2,1,0:T(8,128)S(1)} %collective-permute-done.8), channel_id=1, source_target_pairs={{0,1},{1,2},{2,3},{3,4},{4,5},{5,6},{6,7},{8,9},{9,10},{10,11},{11... | collective-permute-start | bytes 294920 | tf_op jit(solution)/shard_map/ppermute | solution.py:15
  260.5 1.5 collective-permute-done.9
  262.0 12.1 %convolution_add_fusion = f32[16,1536]{1,0:T(8,128)S(1)} fusion(f32[16,1536]{1,0:T(8,128)S(1)} %fusion.25, f32[3072,1536]{1,0:T(8,128)} %maximum_maximum_fusion, f32[16,768]{1,0:T(8,128)S(1)} %get-tuple-element.31, f32[16,768]{1,0:T(8,128)S(1)} %get-tuple-element.30, f32[16,768]{1,0:T(8,128)S(1)} %get-tuple-element.29, f32[16,768]{1,0:T(8,128)S(1)} %get-tuple-element.28), kind=kOutput, calls=%fused_computation.9 | convolution fusion | flops 906141696 | bytes 19267584 | tf_op jit(solution)/shard_map/dot_general | solution.py:51
  274.3 19.5 %psum.7 = f32[1,16]{1,0:T(1,128)S(1)} all-reduce(f32[1,16]{1,0:T(1,128)S(1)} %bitcast.129), channel_id=1, replica_groups=mesh['slab'=4,'trace'=8] {'trace'}, use_global_device_ids=true, to_apply=%region_1.3 | all-reduce | flops 16 | bytes 128 | tf_op jit(solution)/shard_map/psum | solution.py:85
  293.9 0.7 fusion.38
  (73 shorter events, 7.9 us)
Async XLA Ops:
  0.0 20.0 %slice-start = ((s8[9437184]{0:T(1024)(128)(4,1)}), s8[4194304]{0:T(1024)(128)(4,1)S(1)}, s32[]{:S(2)}) async-start(s8[9437184]{0:T(1024)(128)(4,1)} %bitcast.118), calls=%async_computation | async-start | bytes 8388608
  0.0 76.8 %collective-permute-start = (f32[2,16,768]{2,1,0:T(8,128)S(1)}, f32[2,16,768]{2,1,0:T(8,128)}, u32[]{:S(2)}, u32[]{:S(2)}) collective-permute-start(f32[2,16,768]{2,1,0:T(8,128)S(1)} %broadcast_in_dim.11), channel_id=1, source_target_pairs={{0,1},{1,2},{2,3},{3,4},{4,5},{5,6},{6,7},{8,9},{9,10},{10,11},{11... | collective-permute-start | bytes 294920 | tf_op jit(solution)/shard_map/ppermute | solution.py:15
  4.3 72.5 %collective-permute-start.1 = (f32[2,16,768]{2,1,0:T(8,128)S(1)}, f32[2,16,768]{2,1,0:T(8,128)}, u32[]{:S(2)}, u32[]{:S(2)}) collective-permute-start(f32[2,16,768]{2,1,0:T(8,128)S(1)} %broadcast_in_dim.11), channel_id=1, source_target_pairs={{1,0},{2,1},{3,2},{4,3},{5,4},{6,5},{7,6},{9,8},{10,9},{11,10},{12... | collective-permute-start | bytes 294920 | tf_op jit(solution)/shard_map/ppermute | solution.py:18
  12.9 7.0 %slice-start.1 = ((s8[9437184]{0:T(1024)(128)(4,1)}), s8[4194304]{0:T(1024)(128)(4,1)S(1)}, s32[]{:S(2)}) async-start(s8[9437184]{0:T(1024)(128)(4,1)} %bitcast.118), calls=%async_computation.1 | async-start | bytes 8388608
  12.9 7.0 %slice-start.2 = ((s8[9437184]{0:T(1024)(128)(4,1)}), s8[1048576]{0:T(1024)(128)(4,1)S(1)}, s32[]{:S(2)}) async-start(s8[9437184]{0:T(1024)(128)(4,1)} %bitcast.118), calls=%async_computation.2 | async-start | bytes 2097152
  23.4 52.9 %copy-start.1 = (f32[64,768]{1,0:T(8,128)S(1)}, f32[64,768]{1,0:T(8,128)}, u32[]{:S(2)}) copy-start(f32[64,768]{1,0:T(8,128)} %get-tuple-element.20) | copy-start | bytes 589828
  58.3 18.0 %copy-start.2 = (f32[64,768]{1,0:T(8,128)S(1)}, f32[64,768]{1,0:T(8,128)}, u32[]{:S(2)}) copy-start(f32[64,768]{1,0:T(8,128)} %get-tuple-element.21) | copy-start | bytes 589828
  76.3 13.7 %copy-start = (f32[1,2,1,16,768]{4,3,2,1,0:T(8,128)S(1)}, f32[1,2,1,16,768]{4,3,2,1,0:T(8,128)}, u32[]{:S(2)}) copy-start(f32[1,2,1,16,768]{4,3,2,1,0:T(8,128)} %param.13) | copy-start | bytes 294916
  76.3 53.6 %copy-start.3 = (f32[512,64]{0,1:T(8,128)S(1)}, f32[512,64]{0,1:T(8,128)}, u32[]{:S(2)}) copy-start(f32[512,64]{0,1:T(8,128)} %fusion.76) | copy-start | bytes 393220
  76.3 53.6 %copy-start.4 = (f32[512,64]{0,1:T(8,128)S(1)}, f32[512,64]{0,1:T(8,128)}, u32[]{:S(2)}) copy-start(f32[512,64]{0,1:T(8,128)} %get-tuple-element.22) | copy-start | bytes 393220
  76.3 53.6 %copy-start.5 = (f32[512,64]{0,1:T(8,128)S(1)}, f32[512,64]{0,1:T(8,128)}, u32[]{:S(2)}) copy-start(f32[512,64]{0,1:T(8,128)} %get-tuple-element.23) | copy-start | bytes 393220
  90.0 5.9 %collective-permute-start.2 = (f32[2,16,768]{2,1,0:T(8,128)S(1)}, f32[2,16,768]{2,1,0:T(8,128)S(1)}, u32[]{:S(2)}, u32[]{:S(2)}) collective-permute-start(f32[2,16,768]{2,1,0:T(8,128)S(1)} %maximum_add_fusion), channel_id=1, source_target_pairs={{0,8},{8,16},{16,24},{1,9},{9,17},{17,25},{2,10},{10,18},{18,26},{... | collective-permute-start | bytes 294920 | tf_op jit(solution)/shard_map/ppermute | solution.py:26
  130.4 5.7 %collective-permute-start.3 = (f32[2,16,768]{2,1,0:T(8,128)S(1)}, f32[2,16,768]{2,1,0:T(8,128)S(1)}, u32[]{:S(2)}, u32[]{:S(2)}) collective-permute-start(f32[2,16,768]{2,1,0:T(8,128)S(1)} %collective-permute-done.2), channel_id=1, source_target_pairs={{0,1},{1,2},{2,3},{3,4},{4,5},{5,6},{6,7},{8,9},{9,10},{10,11},{11... | collective-permute-start | bytes 294920 | tf_op jit(solution)/shard_map/ppermute | solution.py:15
  133.9 6.5 %collective-permute-start.4 = (f32[2,16,768]{2,1,0:T(8,128)S(1)}, f32[2,16,768]{2,1,0:T(8,128)S(1)}, u32[]{:S(2)}, u32[]{:S(2)}) collective-permute-start(f32[2,16,768]{2,1,0:T(8,128)S(1)} %collective-permute-done.2), channel_id=1, source_target_pairs={{1,0},{2,1},{3,2},{4,3},{5,4},{6,5},{7,6},{9,8},{10,9},{11,10},{12... | collective-permute-start | bytes 294920 | tf_op jit(solution)/shard_map/ppermute | solution.py:18
  152.6 5.9 %collective-permute-start.5 = (f32[2,16,768]{2,1,0:T(8,128)S(1)}, f32[2,16,768]{2,1,0:T(8,128)S(1)}, u32[]{:S(2)}, u32[]{:S(2)}) collective-permute-start(f32[2,16,768]{2,1,0:T(8,128)S(1)} %maximum_add_fusion.1), channel_id=1, source_target_pairs={{0,8},{8,16},{16,24},{1,9},{9,17},{17,25},{2,10},{10,18},{18,26},{... | collective-permute-start | bytes 294920 | tf_op jit(solution)/shard_map/ppermute | solution.py:26
  193.1 3.8 %collective-permute-start.6 = (f32[2,16,768]{2,1,0:T(8,128)S(1)}, f32[2,16,768]{2,1,0:T(8,128)S(1)}, u32[]{:S(2)}, u32[]{:S(2)}) collective-permute-start(f32[2,16,768]{2,1,0:T(8,128)S(1)} %collective-permute-done.5), channel_id=1, source_target_pairs={{0,1},{1,2},{2,3},{3,4},{4,5},{5,6},{6,7},{8,9},{9,10},{10,11},{11... | collective-permute-start | bytes 294920 | tf_op jit(solution)/shard_map/ppermute | solution.py:15
  194.7 6.5 %collective-permute-start.7 = (f32[2,16,768]{2,1,0:T(8,128)S(1)}, f32[2,16,768]{2,1,0:T(8,128)S(1)}, u32[]{:S(2)}, u32[]{:S(2)}) collective-permute-start(f32[2,16,768]{2,1,0:T(8,128)S(1)} %collective-permute-done.5), channel_id=1, source_target_pairs={{1,0},{2,1},{3,2},{4,3},{5,4},{6,5},{7,6},{9,8},{10,9},{11,10},{12... | collective-permute-start | bytes 294920 | tf_op jit(solution)/shard_map/ppermute | solution.py:18
  213.4 5.9 %collective-permute-start.8 = (f32[2,16,768]{2,1,0:T(8,128)S(1)}, f32[2,16,768]{2,1,0:T(8,128)S(1)}, u32[]{:S(2)}, u32[]{:S(2)}) collective-permute-start(f32[2,16,768]{2,1,0:T(8,128)S(1)} %maximum_add_fusion.2), channel_id=1, source_target_pairs={{0,8},{8,16},{16,24},{1,9},{9,17},{17,25},{2,10},{10,18},{18,26},{... | collective-permute-start | bytes 294920 | tf_op jit(solution)/shard_map/ppermute | solution.py:26
  253.9 6.6 %collective-permute-start.10 = (f32[2,16,768]{2,1,0:T(8,128)S(1)}, f32[2,16,768]{2,1,0:T(8,128)S(1)}, u32[]{:S(2)}, u32[]{:S(2)}) collective-permute-start(f32[2,16,768]{2,1,0:T(8,128)S(1)} %collective-permute-done.8), channel_id=1, source_target_pairs={{1,0},{2,1},{3,2},{4,3},{5,4},{6,5},{7,6},{9,8},{10,9},{11,10},{12... | collective-permute-start | bytes 294920 | tf_op jit(solution)/shard_map/ppermute | solution.py:18
  255.2 6.8 %collective-permute-start.9 = (f32[2,16,768]{2,1,0:T(8,128)S(1)}, f32[2,16,768]{2,1,0:T(8,128)S(1)}, u32[]{:S(2)}, u32[]{:S(2)}) collective-permute-start(f32[2,16,768]{2,1,0:T(8,128)S(1)} %collective-permute-done.8), channel_id=1, source_target_pairs={{0,1},{1,2},{2,3},{3,4},{4,5},{5,6},{6,7},{8,9},{9,10},{10,11},{11... | collective-permute-start | bytes 294920 | tf_op jit(solution)/shard_map/ppermute | solution.py:15
where the time goes:
time: 295 us
  blocking collectives  147 us (50%)
  matrix products  53.6 us (18%)
  other arithmetic  27.5 us (9%)
  starting transfers between devices  25.3 us (9%)
  waiting for transfers between devices  22.8 us (8%)
  local copies, waits for them, and re-layouts  17.2 us (6%)
    all_gather x4, blocking collectives, apply_operator(): gathered = lax.all_gather(picked, 'trace', axis=2, tiled=True)  128 us
    dot_general x4, matrix products, apply_operator(): near_out = jnp.dot(stacked_in, near_mat, precision=exact_mode)  48.6 us
    psum x1, blocking collectives, on_device(): total_sum = lax.psum(partial_sum, 'trace')  19.5 us
    concatenate x1, other arithmetic, build_mats(): jnp.concatenate([real_block(tile_set[0, 0], tile_set[0, 1]), real_block(t...  16.2 us
    ppermute x4, starting transfers between devices, extended(): lax.ppermute(lax.slice_in_dim(block, block.shape[dim] - width, None, axis...  14.2 us
    ppermute x3, waiting for transfers between devices, from_behind(): return lax.ppermute(x, axis, pairs)  12 us
    ppermute x4, waiting for transfers between devices, extended(): lax.ppermute(lax.slice_in_dim(block, 0, width, axis=dim), axis, backward)  8.64 us
    squeeze x1, local copies, waits for them, and re-layouts, build_mats(): tile_set[0, 1]  7 us
  transfers between devices with their start and end apart: 11, of which 8 were waited for; matrix products, arithmetic and copies ran while one was open for 13% of the time, Pallas kernels for 0%

commit v1 on v0

v1 whole, which is shorter than its diff:
```python
import jax
import jax.numpy as jnp
from jax import lax
from jax.experimental import pallas as pl
from jax.experimental.pallas import tpu as pltpu
from jax.sharding import PartitionSpec as P

f32 = jnp.float32
bf16 = jnp.bfloat16
small_eps = 1e-06
both_axes = ("slab", "trace")
in_vmem = pl.BlockSpec(memory_space=pltpu.VMEM)
in_smem = pl.BlockSpec(memory_space=pltpu.SMEM)
vmem_room = pltpu.CompilerParams(vmem_limit_bytes=20 << 20)


def two_parts(x):
    high = x.astype(bf16)
    return high, (x - high.astype(f32)).astype(bf16)


def three_parts(x):
    high = x.astype(bf16)
    rest = x - high.astype(f32)
    middle = rest.astype(bf16)
    return high, middle, (rest - middle.astype(f32)).astype(bf16)


def dot(a, b):
    return jnp.dot(a, b, preferred_element_type=f32)


def times(stacked, high, weight_high, weight_low):
    rows = high.shape[0]
    both = dot(stacked, weight_high)
    return both[:rows] + both[rows:] + dot(high, weight_low)


def complex_times(x, weights):
    high, low = two_parts(x)
    stacked = jnp.concatenate([high, low], axis=0)
    by_re = times(stacked, high, *weights[0])
    by_im = times(stacked, high, *weights[1])
    half = x.shape[0] // 2
    return by_re[:half] - by_im[half:], by_im[:half] + by_re[half:]


def pick(x, skel_row):
    width = x.shape[1]
    count = skel_row.shape[1]
    rows = lax.broadcasted_iota(jnp.int32, (width, count), 0)
    chosen = jnp.where(rows == skel_row, 1.0, 0.0).astype(bf16)
    parts = three_parts(x)
    n = x.shape[0]
    out = dot(jnp.concatenate(parts, axis=0), chosen)
    return out[:n] + (out[n : 2 * n] + out[2 * n :])


def put_state(state_ref, small_ref, x, skel_row):
    n, width = x.shape
    half = n // 2
    rank = skel_row.shape[1]
    chosen = pick(x, skel_row)
    state_ref[:, :width] = x
    state_ref[:, width:] = jnp.concatenate(
        [chosen, jnp.zeros((n, state_ref.shape[1] - width - rank), f32)], axis=1
    )
    small_ref[...] = jnp.concatenate([chosen[:half], chosen[half:]], axis=1)


def first_kernel(skel_ref, src_ref, state_ref, small_ref):
    put_state(state_ref, small_ref, src_ref[...], skel_ref[...])


def split_kernel(tiles_ref, high_ref, low_ref):
    plane = pl.program_id(0)
    high, low = two_parts(tiles_ref[0])
    high_ref[plane] = high
    low_ref[plane] = low


def far_split_kernel(side_ref, coupling_ref, basis_ref, coef_ref, base_ref):
    blocks = lax.axis_size("trace")
    here = lax.axis_index("trace")
    _, rank, total = coupling_ref.shape
    turned = lax.rem((blocks - here) * rank, total)
    position = lax.broadcasted_iota(jnp.int32, (rank, total), 1)
    ahead = side_ref[0, 0] > 0
    start = jnp.where(ahead, rank, total - rank)
    keep = (position < start) | (position >= start + rank)
    for part in range(2):
        rolled = jnp.where(keep, pltpu.roll(coupling_ref[part], turned, 1), 0.0)
        high, low = two_parts(rolled.T)
        coef_ref[part, 0] = high
        coef_ref[part, 1] = low
        high, low = two_parts(basis_ref[part])
        base_ref[part, 0] = high
        base_ref[part, 1] = low


def near_kernel(step, side_ref, own_ref, before_ref, after_ref, src_ref, high_ref, low_ref, out_ref):
    @pl.when(lax.axis_index("slab") == step)
    def _():
        n, width = src_ref.shape
        half = n // 2
        ahead = side_ref[0, 0] > 0
        beside = jnp.where(ahead, after_ref[:, :width], before_ref[:, :width])
        total_re, total_im = src_ref[:half], src_ref[half:]
        for slot, x in ((0, own_ref[:, :width]), (1, beside)):
            weights = [(high_ref[2 * slot + p], low_ref[2 * slot + p]) for p in range(2)]
            re, im = complex_times(x, weights)
            total_re += re
            total_im += im
        out_ref[:half] = total_re
        out_ref[half:] = total_im


def far_kernel(step, skel_ref, old_ref, near_ref, before_ref, after_ref, *refs):
    *small_refs, coef_ref, base_ref, state_ref, small_ref = refs
    active = lax.axis_index("slab") == step

    @pl.when(active)
    def _():
        n, width = near_ref.shape
        half = n // 2
        rank = skel_ref.shape[1]
        pieces = [after_ref[:, width : width + rank]]
        for ref in small_refs:
            pieces.append(jnp.concatenate([ref[:, :rank], ref[:, rank:]], axis=0))
        pieces.append(before_ref[:, width : width + rank])
        values = jnp.concatenate(pieces, axis=1)
        weights = [(coef_ref[p, 0, rank:], coef_ref[p, 1, rank:]) for p in range(2)]
        coef = jnp.concatenate(complex_times(values, weights), axis=0)
        weights = [(base_ref[p, 0], base_ref[p, 1]) for p in range(2)]
        far = jnp.concatenate(complex_times(coef, weights), axis=0)
        put_state(state_ref, small_ref, near_ref[...] + far, skel_ref[...])

    @pl.when(jnp.logical_not(active))
    def _():
        width = near_ref.shape[1]
        rank = skel_ref.shape[1]
        half = near_ref.shape[0] // 2
        state_ref[...] = old_ref[...]
        small_ref[...] = jnp.concatenate(
            [old_ref[:half, width : width + rank], old_ref[half:, width : width + rank]], axis=1
        )


def energy_kernel(state_ref, out_ref):
    half = state_ref.shape[0] // 2
    width = state_ref.shape[1] - 128
    x = state_ref[:, :width]
    squares = x * x
    each = jnp.sum(squares[:half] + squares[half:], axis=1, keepdims=True)
    lanes = jnp.broadcast_to(each, (half, 128)).T
    out_ref[...] = jnp.broadcast_to(lanes[:1], out_ref.shape)


def norm_kernel(count, state_ref, sums_ref, out_ref):
    half = state_ref.shape[0] // 2
    width = out_ref.shape[-1]
    total = jnp.sum(sums_ref[...], axis=0, keepdims=True)
    scale = jnp.broadcast_to(1.0 / jnp.sqrt(total / count + small_eps), (128, half)).T[:, :1]
    out_ref[0] = state_ref[:half, :width] * scale
    out_ref[1] = state_ref[half:, :width] * scale


def ring_pairs(step, shift, slabs, blocks):
    pairs = []
    for place in range(slabs):
        source = (step - 1 + place) % slabs
        target = (source + 1) % slabs
        move = shift if place == 0 else 0
        pairs += [
            (source * blocks + c, target * blocks + (c + move) % blocks) for c in range(blocks)
        ]
    return pairs


def on_device(near_tiles, near_side, skeleton, far_coupling, far_basis, sources):
    slabs = lax.axis_size("slab")
    blocks = lax.axis_size("trace")
    _, slots, parts, tile, width = near_tiles.shape
    _, _, batches, shots, _ = sources.shape
    rank = skeleton.shape[2]
    rows = batches * shots
    n = parts * rows
    wide = width + 128

    src = sources.reshape(n, width)
    tiles = near_tiles.reshape(slots * parts, tile, width)
    skel_here = skeleton.reshape(1, rank)
    skel_next = lax.ppermute(
        skel_here, "slab", [((s + 1) % slabs, s) for s in range(slabs)]
    )
    state_type = jax.ShapeDtypeStruct((n, wide), f32)
    small_type = jax.ShapeDtypeStruct((rows, parts * rank), f32)
    state, small = pl.pallas_call(
        first_kernel,
        out_shape=(state_type, small_type),
        in_specs=[in_vmem] * 2,
        out_specs=[in_vmem] * 2,
        compiler_params=vmem_room,
        name="first",
    )(skel_next, src)
    halves = jax.ShapeDtypeStruct(tiles.shape, bf16)
    tiles_high, tiles_low = pl.pallas_call(
        split_kernel,
        grid=(slots * parts,),
        out_shape=(halves, halves),
        in_specs=[pl.BlockSpec((1, tile, width), lambda i: (i, 0, 0))],
        out_specs=[in_vmem] * 2,
        compiler_params=vmem_room,
        name="split_tiles",
    )(tiles)
    coef, base = pl.pallas_call(
        far_split_kernel,
        out_shape=(
            jax.ShapeDtypeStruct((parts, 2, blocks * rank, rank), bf16),
            jax.ShapeDtypeStruct((parts, 2, rank, width), bf16),
        ),
        in_specs=[in_smem, in_vmem, in_vmem],
        out_specs=[in_vmem] * 2,
        compiler_params=vmem_room,
        name="split_far",
    )(near_side, far_coupling[0], far_basis[0])

    for step in range(1, slabs):

        def send(x, shift):
            return lax.ppermute(x, both_axes, ring_pairs(step, shift, slabs, blocks))

        own = send(state, 0)
        before = send(state, 1)
        after = send(state, blocks - 1)
        smalls = [send(small, shift) for shift in range(blocks - 2, 1, -1)]
        near = pl.pallas_call(
            lambda *refs, step=step: near_kernel(step, *refs),
            out_shape=jax.ShapeDtypeStruct((n, width), f32),
            in_specs=[in_smem] + [in_vmem] * 6,
            out_specs=in_vmem,
            compiler_params=vmem_room,
            name="near",
        )(near_side, own, before, after, src, tiles_high, tiles_low)
        state, small = pl.pallas_call(
            lambda *refs, step=step: far_kernel(step, *refs),
            out_shape=(state_type, small_type),
            in_specs=[in_vmem] * (7 + len(smalls)),
            out_specs=[in_vmem] * 2,
            compiler_params=vmem_room,
            name="far",
        )(skel_next, state, near, before, after, *smalls, coef, base)

    partial = pl.pallas_call(
        energy_kernel,
        out_shape=jax.ShapeDtypeStruct((blocks, rows), f32),
        in_specs=[in_vmem],
        out_specs=in_vmem,
        compiler_params=vmem_room,
        name="energy",
    )(state)
    sums = lax.all_to_all(partial, "trace", 0, 0)
    normed = pl.pallas_call(
        lambda *refs: norm_kernel(float(parts * width * blocks), *refs),
        out_shape=jax.ShapeDtypeStruct((parts, rows, width), f32),
        in_specs=[in_vmem] * 2,
        out_specs=in_vmem,
        compiler_params=vmem_room,
        name="norm",
    )(state, sums)
    return normed.reshape(sources.shape)


def solution(mesh):
    placed = (
        P("slab", None, None, None, "trace"),
        P("slab", "trace"),
        P("slab", "trace", None),
        P("slab", None, "trace", None),
        P("slab", None, None, "trace"),
        P("slab", None, None, None, "trace"),
    )
    return jax.shard_map(
        on_device,
        mesh=mesh,
        in_specs=placed,
        out_specs=P("slab", None, None, None, "trace"),
        check_vma=False,
    )
```

time: 295 us -> 56.4 us (0.19)
  the two profiles are of different devices: /device:TPU:4 before, /device:TPU:0 now
where the time goes in v1:
time: 56.4 us; the launch traced here: 56.2 us
  starting transfers between devices  24.6 us (44%)
  waiting for transfers between devices  12.6 us (22%)
  blocking collectives  9.7 us (17%)
  local copies, waits for them, and re-layouts  4.58 us (8%)
  Pallas kernels  3.85 us (7%)
  between operations  0.8 us (1%)
    ppermute x24, starting transfers between devices, send(): return lax.ppermute(x, both_axes, ring_pairs(step, shift, slabs, blocks))  22.2 us
    ppermute x24, waiting for transfers between devices, send(): return lax.ppermute(x, both_axes, ring_pairs(step, shift, slabs, blocks))  11.2 us
    all_to_all x1, blocking collectives, on_device(): sums = lax.all_to_all(partial, 'trace', 0, 0)  9.7 us
    unnamed x10, local copies, waits for them, and re-layouts  4.58 us
    ppermute x1, starting transfers between devices, on_device(): lax.ppermute(skel_here, 'slab', [((s + 1) % slabs, s) for s in range(slab...  2.41 us
    ppermute x1, waiting for transfers between devices, on_device(): lax.ppermute(skel_here, 'slab', [((s + 1) % slabs, s) for s in range(slab...  1.43 us
    pallas_call x1, Pallas kernels, on_device(): pl.pallas_call(split_kernel, grid=(slots * parts,), out_shape=(halves, ha...  1.42 us
  transfers between devices with their start and end apart: 25, of which 12 were waited for; matrix products, arithmetic and copies ran while one was open for 0% of the time, Pallas kernels for 3%

profile of v1, /device:TPU:0, one launch (start us, length us, event | category | flops | bytes accessed | tf_op | source)
XLA Modules:
  0.0 56.2 jit_solution(17109895660503772437)
XLA Ops:
  0.0 2.4 %collective-permute-start = (s32[1,64]{1,0:T(1,128)}, s32[1,64]{1,0:T(1,128)S(1)}, u32[]{:S(2)}, u32[]{:S(2)}) collective-permute-start(s32[1,64]{1,0:T(1,128)} %bitcast.21), channel_id=1, source_target_pairs={{8,0},{16,8},{24,16},{0,24},{9,1},{17,9},{25,17},{1,25},{10,2},{18... | collective-permute-start | bytes 776 | tf_op jit(solution)/shard_map/ppermute | solution.py:193
  2.4 1.4 %collective-permute-done.skel_ref.refs_0_ = s32[1,64]{1,0:T(1,128)S(1)} collective-permute-done((s32[1,64]{1,0:T(1,128)}, s32[1,64]{1,0:T(1,128)S(1)}, u32[]{:S(2)}, u32[]{:S(2)}) %collective-permute-start) | collective-permute-done | bytes 288 | tf_op jit(solution)/shard_map/ppermute | solution.py:193
  3.8 0.9 %copy-done.1 = f32[1,2,1,16,768]{4,3,2,1,0:T(8,128)S(1)} copy-done((f32[1,2,1,16,768]{4,3,2,1,0:T(8,128)S(1)}, f32[1,2,1,16,768]{4,3,2,1,0:T(8,128)}, u32[]{:S(2)}) %copy-start.1) | copy-done | bytes 98328
  4.7 0.3 first.1
  5.0 4.7 %collective-permute-start.3 = (f32[32,896]{1,0:T(8,128)S(1)}, f32[32,896]{1,0:T(8,128)S(1)}, u32[]{:S(2)}, u32[]{:S(2)}) collective-permute-start(f32[32,896]{1,0:T(8,128)S(1)} %get-tuple-element.16.refs_1_), channel_id=1, source_target_pairs={{0,15},{1,8},{2,9},{3,10},{4,11},{5,12},{6,13},{7,14},{8,16},{9,17... | collective-permute-start | bytes 344072 | tf_op jit(solution)/shard_map/ppermute | solution.py:231
  9.7 0.4 collective-permute-start.7
  10.1 2.0 %collective-permute-done.3.refs_3_.refs_4_ = f32[32,896]{1,0:T(8,128)S(1)} collective-permute-done((f32[32,896]{1,0:T(8,128)S(1)}, f32[32,896]{1,0:T(8,128)S(1)}, u32[]{:S(2)}, u32[]{:S(2)}) %collective-permute-start.3) | collective-permute-done | bytes 114720 | tf_op jit(solution)/shard_map/ppermute | solution.py:231
  12.1 1.4 %collective-permute-start.6 = (f32[16,128]{1,0:T(8,128)S(1)}, f32[16,128]{1,0:T(8,128)S(1)}, u32[]{:S(2)}, u32[]{:S(2)}) collective-permute-start(f32[16,128]{1,0:T(8,128)S(1)} %get-tuple-element.19), channel_id=1, source_target_pairs={{0,12},{1,13},{2,14},{3,15},{4,8},{5,9},{6,10},{7,11},{8,16},{9,17... | collective-permute-start | bytes 24584 | tf_op jit(solution)/shard_map/ppermute | solution.py:231
  13.5 0.4 collective-permute-done.2.refs_2_.refs_3_
  14.0 0.6 %collective-permute-start.5 = (f32[16,128]{1,0:T(8,128)S(1)}, f32[16,128]{1,0:T(8,128)S(1)}, u32[]{:S(2)}, u32[]{:S(2)}) collective-permute-start(f32[16,128]{1,0:T(8,128)S(1)} %get-tuple-element.19), channel_id=1, source_target_pairs={{0,13},{1,14},{2,15},{3,8},{4,9},{5,10},{6,11},{7,12},{8,16},{9,17... | collective-permute-start | bytes 24584 | tf_op jit(solution)/shard_map/ppermute | solution.py:231
  14.5 0.6 %collective-permute-done.1.refs_1_ = f32[32,896]{1,0:T(8,128)S(1)} collective-permute-done((f32[32,896]{1,0:T(8,128)S(1)}, f32[32,896]{1,0:T(8,128)S(1)}, u32[]{:S(2)}, u32[]{:S(2)}) %collective-permute-start.1) | collective-permute-done | bytes 114720 | tf_op jit(solution)/shard_map/ppermute | solution.py:231
  15.2 0.0 collective-permute-start.4
  15.8 0.0 copy-start
  15.8 3.7 %copy-done = f32[1,2,2,768,768]{4,3,2,1,0:T(8,128)S(1)} copy-done((f32[1,2,2,768,768]{4,3,2,1,0:T(8,128)S(1)}, f32[1,2,2,768,768]{4,3,2,1,0:T(8,128)}, u32[]{:S(2)}) %copy-start) | copy-done | bytes 9437208
  19.5 1.4 %split_tiles.1 = (bf16[4,768,768]{2,1,0:T(8,128)(2,1)S(1)}, bf16[4,768,768]{2,1,0:T(8,128)(2,1)S(1)}) custom-call(f32[4,768,768]{2,1,0:T(8,128)S(1)} %bitcast.12), custom_call_target="tpu_custom_call" | custom-call | tf_op jit(solution)/shard_map/split_tiles/pallas_call | solution.py:207
  21.0 0.4 split_far.1
  21.4 0.0 collective-permute-done.8.refs_9_
  21.4 0.0 collective-permute-done.7.refs_8_
  21.4 0.0 collective-permute-done.5.refs_6_
  21.4 0.0 collective-permute-done.4.refs_5_
  21.4 0.1 far.3
  21.5 1.7 %collective-permute-start.11 = (f32[32,896]{1,0:T(8,128)S(1)}, f32[32,896]{1,0:T(8,128)S(1)}, u32[]{:S(2)}, u32[]{:S(2)}) collective-permute-start(f32[32,896]{1,0:T(8,128)S(1)} %get-tuple-element.22.refs_1_), channel_id=1, source_target_pairs={{8,23},{9,16},{10,17},{11,18},{12,19},{13,20},{14,21},{15,22},{16,... | collective-permute-start | bytes 344072 | tf_op jit(solution)/shard_map/ppermute | solution.py:231
  23.2 0.1 collective-permute-start.10
  23.3 0.7 %collective-permute-start.9 = (f32[32,896]{1,0:T(8,128)S(1)}, f32[32,896]{1,0:T(8,128)S(1)}, u32[]{:S(2)}, u32[]{:S(2)}) collective-permute-start(f32[32,896]{1,0:T(8,128)S(1)} %get-tuple-element.22.refs_1_), channel_id=1, source_target_pairs={{8,16},{9,17},{10,18},{11,19},{12,20},{13,21},{14,22},{15,23},{16,... | collective-permute-start | bytes 344072 | tf_op jit(solution)/shard_map/ppermute | solution.py:231
  24.1 1.4 %collective-permute-start.15 = (f32[16,128]{1,0:T(8,128)S(1)}, f32[16,128]{1,0:T(8,128)S(1)}, u32[]{:S(2)}, u32[]{:S(2)}) collective-permute-start(f32[16,128]{1,0:T(8,128)S(1)} %get-tuple-element.23), channel_id=1, source_target_pairs={{8,19},{9,20},{10,21},{11,22},{12,23},{13,16},{14,17},{15,18},{16,... | collective-permute-start | bytes 24584 | tf_op jit(solution)/shard_map/ppermute | solution.py:231
  25.5 0.3 collective-permute-done.11.refs_3_.refs_4_
  25.7 0.6 %collective-permute-start.14 = (f32[16,128]{1,0:T(8,128)S(1)}, f32[16,128]{1,0:T(8,128)S(1)}, u32[]{:S(2)}, u32[]{:S(2)}) collective-permute-start(f32[16,128]{1,0:T(8,128)S(1)} %get-tuple-element.23), channel_id=1, source_target_pairs={{8,20},{9,21},{10,22},{11,23},{12,16},{13,17},{14,18},{15,19},{16,... | collective-permute-start | bytes 24584 | tf_op jit(solution)/shard_map/ppermute | solution.py:231
  26.4 1.1 %collective-permute-done.10.refs_2_.refs_3_ = f32[32,896]{1,0:T(8,128)S(1)} collective-permute-done((f32[32,896]{1,0:T(8,128)S(1)}, f32[32,896]{1,0:T(8,128)S(1)}, u32[]{:S(2)}, u32[]{:S(2)}) %collective-permute-start.10) | collective-permute-done | bytes 114720 | tf_op jit(solution)/shard_map/ppermute | solution.py:231
  27.4 4.2 %collective-permute-start.13 = (f32[16,128]{1,0:T(8,128)S(1)}, f32[16,128]{1,0:T(8,128)S(1)}, u32[]{:S(2)}, u32[]{:S(2)}) collective-permute-start(f32[16,128]{1,0:T(8,128)S(1)} %get-tuple-element.23), channel_id=1, source_target_pairs={{8,21},{9,22},{10,23},{11,16},{12,17},{13,18},{14,19},{15,20},{16,... | collective-permute-start | bytes 24584 | tf_op jit(solution)/shard_map/ppermute | solution.py:231
  31.6 0.1 collective-permute-start.12
  31.7 0.8 %collective-permute-done.13.refs_6_ = f32[16,128]{1,0:T(8,128)S(1)} collective-permute-done((f32[16,128]{1,0:T(8,128)S(1)}, f32[16,128]{1,0:T(8,128)S(1)}, u32[]{:S(2)}, u32[]{:S(2)}) %collective-permute-start.13) | collective-permute-done | bytes 8224 | tf_op jit(solution)/shard_map/ppermute | solution.py:231
  32.4 2.3 %collective-permute-done.12.refs_5_ = f32[16,128]{1,0:T(8,128)S(1)} collective-permute-done((f32[16,128]{1,0:T(8,128)S(1)}, f32[16,128]{1,0:T(8,128)S(1)}, u32[]{:S(2)}, u32[]{:S(2)}) %collective-permute-start.12) | collective-permute-done | bytes 8224 | tf_op jit(solution)/shard_map/ppermute | solution.py:231
  34.7 0.1 far.4
  34.8 2.7 %collective-permute-start.18 = (f32[32,896]{1,0:T(8,128)S(1)}, f32[32,896]{1,0:T(8,128)S(1)}, u32[]{:S(2)}, u32[]{:S(2)}) collective-permute-start(f32[32,896]{1,0:T(8,128)S(1)} %get-tuple-element.24.refs_1_), channel_id=1, source_target_pairs={{16,25},{17,26},{18,27},{19,28},{20,29},{21,30},{22,31},{23,24},{2... | collective-permute-start | bytes 344072 | tf_op jit(solution)/shard_map/ppermute | solution.py:231
  37.5 0.1 collective-permute-start.17
  37.5 0.1 collective-permute-start.24
  37.6 0.1 collective-permute-start.23
  37.7 1.3 %collective-permute-done.19.refs_3_.refs_4_ = f32[32,896]{1,0:T(8,128)S(1)} collective-permute-done((f32[32,896]{1,0:T(8,128)S(1)}, f32[32,896]{1,0:T(8,128)S(1)}, u32[]{:S(2)}, u32[]{:S(2)}) %collective-permute-start.19) | collective-permute-done | bytes 114720 | tf_op jit(solution)/shard_map/ppermute | solution.py:231
  39.0 0.6 %collective-permute-start.22 = (f32[16,128]{1,0:T(8,128)S(1)}, f32[16,128]{1,0:T(8,128)S(1)}, u32[]{:S(2)}, u32[]{:S(2)}) collective-permute-start(f32[16,128]{1,0:T(8,128)S(1)} %get-tuple-element.25), channel_id=1, source_target_pairs={{16,28},{17,29},{18,30},{19,31},{20,24},{21,25},{22,26},{23,27},{2... | collective-permute-start | bytes 24584 | tf_op jit(solution)/shard_map/ppermute | solution.py:231
  39.6 0.6 %collective-permute-done.18.refs_2_.refs_3_ = f32[32,896]{1,0:T(8,128)S(1)} collective-permute-done((f32[32,896]{1,0:T(8,128)S(1)}, f32[32,896]{1,0:T(8,128)S(1)}, u32[]{:S(2)}, u32[]{:S(2)}) %collective-permute-start.18) | collective-permute-done | bytes 114720 | tf_op jit(solution)/shard_map/ppermute | solution.py:231
  40.2 1.5 %collective-permute-start.21 = (f32[16,128]{1,0:T(8,128)S(1)}, f32[16,128]{1,0:T(8,128)S(1)}, u32[]{:S(2)}, u32[]{:S(2)}) collective-permute-start(f32[16,128]{1,0:T(8,128)S(1)} %get-tuple-element.25), channel_id=1, source_target_pairs={{16,29},{17,30},{18,31},{19,24},{20,25},{21,26},{22,27},{23,28},{2... | collective-permute-start | bytes 24584 | tf_op jit(solution)/shard_map/ppermute | solution.py:231
  41.7 1.2 %collective-permute-start.20 = (f32[16,128]{1,0:T(8,128)S(1)}, f32[16,128]{1,0:T(8,128)S(1)}, u32[]{:S(2)}, u32[]{:S(2)}) collective-permute-start(f32[16,128]{1,0:T(8,128)S(1)} %get-tuple-element.25), channel_id=1, source_target_pairs={{16,30},{17,31},{18,24},{19,25},{20,26},{21,27},{22,28},{23,29},{2... | collective-permute-start | bytes 24584 | tf_op jit(solution)/shard_map/ppermute | solution.py:231
  43.0 1.8 %collective-permute-done.21.refs_6_ = f32[16,128]{1,0:T(8,128)S(1)} collective-permute-done((f32[16,128]{1,0:T(8,128)S(1)}, f32[16,128]{1,0:T(8,128)S(1)}, u32[]{:S(2)}, u32[]{:S(2)}) %collective-permute-start.21) | collective-permute-done | bytes 8224 | tf_op jit(solution)/shard_map/ppermute | solution.py:231
  44.7 0.1 collective-permute-done.20.refs_5_
  44.8 0.7 %far.5 = (f32[32,896]{1,0:T(8,128)S(1)}, f32[16,128]{1,0:T(8,128)}) custom-call(s32[1,64]{1,0:T(1,128)S(1)} %collective-permute-done.skel_ref.refs_0_, f32[32,896]{1,0:T(8,128)S(1)} %get-tuple-element.24.refs_1_, f32[32,768]{1,0:T(8,128)S(1)} %near.5.refs_2_, f32[32,896]{1,0:T(8,128)S(1)} %collective-permute-done.18.refs_2_.refs_3_, ...), custom_call_target="tpu_custom_call" | custom-call | tf_op jit(solution)/shard_map/far/pallas_call | solution.py:245
  45.5 0.2 energy.1
  45.7 9.7 %all_to_all.11 = f32[8,1,16]{2,1,0:T(1,128)S(1)} all-to-all(f32[8,1,16]{2,1,0:T(1,128)S(1)} %bitcast.20), channel_id=1, replica_groups=mesh['slab'=4,'trace'=8] {'trace'}, dimensions={0} | all-to-all | bytes 1024 | tf_op jit(solution)/shard_map/all_to_all | solution.py:262
  55.4 0.8 %norm.1 = f32[2,16,768]{2,1,0:T(8,128)} custom-call(f32[32,896]{1,0:T(8,128)S(1)} %get-tuple-element.26.state_ref.refs_0_, f32[8,16]{1,0:T(8,128)S(1)} %bitcast.19), custom_call_target="tpu_custom_call" | custom-call | tf_op jit(solution)/shard_map/norm/pallas_call | solution.py:263
  (24 shorter events, 0.1 us)
Async XLA Ops:
  0.0 3.8 %collective-permute-start = (s32[1,64]{1,0:T(1,128)}, s32[1,64]{1,0:T(1,128)S(1)}, u32[]{:S(2)}, u32[]{:S(2)}) collective-permute-start(s32[1,64]{1,0:T(1,128)} %bitcast.21), channel_id=1, source_target_pairs={{8,0},{16,8},{24,16},{0,24},{9,1},{17,9},{25,17},{1,25},{10,2},{18... | collective-permute-start | bytes 776 | tf_op jit(solution)/shard_map/ppermute | solution.py:193
  3.8 0.9 %copy-start.1 = (f32[1,2,1,16,768]{4,3,2,1,0:T(8,128)S(1)}, f32[1,2,1,16,768]{4,3,2,1,0:T(8,128)}, u32[]{:S(2)}) copy-start(f32[1,2,1,16,768]{4,3,2,1,0:T(8,128)} %param.11) | copy-start | bytes 294916
  5.0 7.1 %collective-permute-start.3 = (f32[32,896]{1,0:T(8,128)S(1)}, f32[32,896]{1,0:T(8,128)S(1)}, u32[]{:S(2)}, u32[]{:S(2)}) collective-permute-start(f32[32,896]{1,0:T(8,128)S(1)} %get-tuple-element.16.refs_1_), channel_id=1, source_target_pairs={{0,15},{1,8},{2,9},{3,10},{4,11},{5,12},{6,13},{7,14},{8,16},{9,17... | collective-permute-start | bytes 344072 | tf_op jit(solution)/shard_map/ppermute | solution.py:231
  9.7 4.2 %collective-permute-start.2 = (f32[32,896]{1,0:T(8,128)S(1)}, f32[32,896]{1,0:T(8,128)S(1)}, u32[]{:S(2)}, u32[]{:S(2)}) collective-permute-start(f32[32,896]{1,0:T(8,128)S(1)} %get-tuple-element.16.refs_1_), channel_id=1, source_target_pairs={{0,9},{1,10},{2,11},{3,12},{4,13},{5,14},{6,15},{7,8},{8,16},{9,17... | collective-permute-start | bytes 344072 | tf_op jit(solution)/shard_map/ppermute | solution.py:231
  9.7 5.4 %collective-permute-start.1 = (f32[32,896]{1,0:T(8,128)S(1)}, f32[32,896]{1,0:T(8,128)S(1)}, u32[]{:S(2)}, u32[]{:S(2)}) collective-permute-start(f32[32,896]{1,0:T(8,128)S(1)} %get-tuple-element.16.refs_1_), channel_id=1, source_target_pairs={{0,8},{1,9},{2,10},{3,11},{4,12},{5,13},{6,14},{7,15},{8,16},{9,17... | collective-permute-start | bytes 344072 | tf_op jit(solution)/shard_map/ppermute | solution.py:231
  9.7 11.6 %collective-permute-start.8 = (f32[16,128]{1,0:T(8,128)S(1)}, f32[16,128]{1,0:T(8,128)S(1)}, u32[]{:S(2)}, u32[]{:S(2)}) collective-permute-start(f32[16,128]{1,0:T(8,128)S(1)} %get-tuple-element.19), channel_id=1, source_target_pairs={{0,10},{1,11},{2,12},{3,13},{4,14},{5,15},{6,8},{7,9},{8,16},{9,17... | collective-permute-start | bytes 24584 | tf_op jit(solution)/shard_map/ppermute | solution.py:231
  9.7 11.6 %collective-permute-start.7 = (f32[16,128]{1,0:T(8,128)S(1)}, f32[16,128]{1,0:T(8,128)S(1)}, u32[]{:S(2)}, u32[]{:S(2)}) collective-permute-start(f32[16,128]{1,0:T(8,128)S(1)} %get-tuple-element.19), channel_id=1, source_target_pairs={{0,11},{1,12},{2,13},{3,14},{4,15},{5,8},{6,9},{7,10},{8,16},{9,17... | collective-permute-start | bytes 24584 | tf_op jit(solution)/shard_map/ppermute | solution.py:231
  12.1 9.3 %collective-permute-start.6 = (f32[16,128]{1,0:T(8,128)S(1)}, f32[16,128]{1,0:T(8,128)S(1)}, u32[]{:S(2)}, u32[]{:S(2)}) collective-permute-start(f32[16,128]{1,0:T(8,128)S(1)} %get-tuple-element.19), channel_id=1, source_target_pairs={{0,12},{1,13},{2,14},{3,15},{4,8},{5,9},{6,10},{7,11},{8,16},{9,17... | collective-permute-start | bytes 24584 | tf_op jit(solution)/shard_map/ppermute | solution.py:231
  14.0 7.5 %collective-permute-start.5 = (f32[16,128]{1,0:T(8,128)S(1)}, f32[16,128]{1,0:T(8,128)S(1)}, u32[]{:S(2)}, u32[]{:S(2)}) collective-permute-start(f32[16,128]{1,0:T(8,128)S(1)} %get-tuple-element.19), channel_id=1, source_target_pairs={{0,13},{1,14},{2,15},{3,8},{4,9},{5,10},{6,11},{7,12},{8,16},{9,17... | collective-permute-start | bytes 24584 | tf_op jit(solution)/shard_map/ppermute | solution.py:231
  15.2 6.2 %collective-permute-start.4 = (f32[16,128]{1,0:T(8,128)S(1)}, f32[16,128]{1,0:T(8,128)S(1)}, u32[]{:S(2)}, u32[]{:S(2)}) collective-permute-start(f32[16,128]{1,0:T(8,128)S(1)} %get-tuple-element.19), channel_id=1, source_target_pairs={{0,14},{1,15},{2,8},{3,9},{4,10},{5,11},{6,12},{7,13},{8,16},{9,17... | collective-permute-start | bytes 24584 | tf_op jit(solution)/shard_map/ppermute | solution.py:231
  15.8 3.7 %copy-start = (f32[1,2,2,768,768]{4,3,2,1,0:T(8,128)S(1)}, f32[1,2,2,768,768]{4,3,2,1,0:T(8,128)}, u32[]{:S(2)}) copy-start(f32[1,2,2,768,768]{4,3,2,1,0:T(8,128)} %param.6) | copy-start | bytes 28311556
  19.5 1.4 %copy-start.3 = (f32[1,2,64,768]{3,2,1,0:T(8,128)S(1)}, f32[1,2,64,768]{3,2,1,0:T(8,128)}, u32[]{:S(2)}) copy-start(f32[1,2,64,768]{3,2,1,0:T(8,128)} %param.10) | copy-start | bytes 1179652
  19.5 1.4 %copy-start.4 = (f32[1,2,64,512]{3,2,1,0:T(8,128)S(1)}, f32[1,2,64,512]{3,2,1,0:T(8,128)}, u32[]{:S(2)}) copy-start(f32[1,2,64,512]{3,2,1,0:T(8,128)} %param.9) | copy-start | bytes 786436
  19.5 1.8 %copy-start.2 = (f32[1,2,1,16,768]{4,3,2,1,0:T(8,128)S(1)}, f32[1,2,1,16,768]{4,3,2,1,0:T(8,128)}, u32[]{:S(2)}) copy-start(f32[1,2,1,16,768]{4,3,2,1,0:T(8,128)} %param.11) | copy-start | bytes 294916
  21.5 4.2 %collective-permute-start.11 = (f32[32,896]{1,0:T(8,128)S(1)}, f32[32,896]{1,0:T(8,128)S(1)}, u32[]{:S(2)}, u32[]{:S(2)}) collective-permute-start(f32[32,896]{1,0:T(8,128)S(1)} %get-tuple-element.22.refs_1_), channel_id=1, source_target_pairs={{8,23},{9,16},{10,17},{11,18},{12,19},{13,20},{14,21},{15,22},{16,... | collective-permute-start | bytes 344072 | tf_op jit(solution)/shard_map/ppermute | solution.py:231
  23.2 4.2 %collective-permute-start.10 = (f32[32,896]{1,0:T(8,128)S(1)}, f32[32,896]{1,0:T(8,128)S(1)}, u32[]{:S(2)}, u32[]{:S(2)}) collective-permute-start(f32[32,896]{1,0:T(8,128)S(1)} %get-tuple-element.22.refs_1_), channel_id=1, source_target_pairs={{8,17},{9,18},{10,19},{11,20},{12,21},{13,22},{14,23},{15,16},{16,... | collective-permute-start | bytes 344072 | tf_op jit(solution)/shard_map/ppermute | solution.py:231
  23.3 8.3 %collective-permute-start.9 = (f32[32,896]{1,0:T(8,128)S(1)}, f32[32,896]{1,0:T(8,128)S(1)}, u32[]{:S(2)}, u32[]{:S(2)}) collective-permute-start(f32[32,896]{1,0:T(8,128)S(1)} %get-tuple-element.22.refs_1_), channel_id=1, source_target_pairs={{8,16},{9,17},{10,18},{11,19},{12,20},{13,21},{14,22},{15,23},{16,... | collective-permute-start | bytes 344072 | tf_op jit(solution)/shard_map/ppermute | solution.py:231
  24.1 7.6 %collective-permute-start.16 = (f32[16,128]{1,0:T(8,128)S(1)}, f32[16,128]{1,0:T(8,128)S(1)}, u32[]{:S(2)}, u32[]{:S(2)}) collective-permute-start(f32[16,128]{1,0:T(8,128)S(1)} %get-tuple-element.23), channel_id=1, source_target_pairs={{8,18},{9,19},{10,20},{11,21},{12,22},{13,23},{14,16},{15,17},{16,... | collective-permute-start | bytes 24584 | tf_op jit(solution)/shard_map/ppermute | solution.py:231
  24.1 7.6 %collective-permute-start.15 = (f32[16,128]{1,0:T(8,128)S(1)}, f32[16,128]{1,0:T(8,128)S(1)}, u32[]{:S(2)}, u32[]{:S(2)}) collective-permute-start(f32[16,128]{1,0:T(8,128)S(1)} %get-tuple-element.23), channel_id=1, source_target_pairs={{8,19},{9,20},{10,21},{11,22},{12,23},{13,16},{14,17},{15,18},{16,... | collective-permute-start | bytes 24584 | tf_op jit(solution)/shard_map/ppermute | solution.py:231
  25.7 5.9 %collective-permute-start.14 = (f32[16,128]{1,0:T(8,128)S(1)}, f32[16,128]{1,0:T(8,128)S(1)}, u32[]{:S(2)}, u32[]{:S(2)}) collective-permute-start(f32[16,128]{1,0:T(8,128)S(1)} %get-tuple-element.23), channel_id=1, source_target_pairs={{8,20},{9,21},{10,22},{11,23},{12,16},{13,17},{14,18},{15,19},{16,... | collective-permute-start | bytes 24584 | tf_op jit(solution)/shard_map/ppermute | solution.py:231
  27.4 5.0 %collective-permute-start.13 = (f32[16,128]{1,0:T(8,128)S(1)}, f32[16,128]{1,0:T(8,128)S(1)}, u32[]{:S(2)}, u32[]{:S(2)}) collective-permute-start(f32[16,128]{1,0:T(8,128)S(1)} %get-tuple-element.23), channel_id=1, source_target_pairs={{8,21},{9,22},{10,23},{11,16},{12,17},{13,18},{14,19},{15,20},{16,... | collective-permute-start | bytes 24584 | tf_op jit(solution)/shard_map/ppermute | solution.py:231
  31.6 3.1 %collective-permute-start.12 = (f32[16,128]{1,0:T(8,128)S(1)}, f32[16,128]{1,0:T(8,128)S(1)}, u32[]{:S(2)}, u32[]{:S(2)}) collective-permute-start(f32[16,128]{1,0:T(8,128)S(1)} %get-tuple-element.23), channel_id=1, source_target_pairs={{8,22},{9,23},{10,16},{11,17},{12,18},{13,19},{14,20},{15,21},{16,... | collective-permute-start | bytes 24584 | tf_op jit(solution)/shard_map/ppermute | solution.py:231
  34.8 4.2 %collective-permute-start.19 = (f32[32,896]{1,0:T(8,128)S(1)}, f32[32,896]{1,0:T(8,128)S(1)}, u32[]{:S(2)}, u32[]{:S(2)}) collective-permute-start(f32[32,896]{1,0:T(8,128)S(1)} %get-tuple-element.24.refs_1_), channel_id=1, source_target_pairs={{16,31},{17,24},{18,25},{19,26},{20,27},{21,28},{22,29},{23,30},{2... | collective-permute-start | bytes 344072 | tf_op jit(solution)/shard_map/ppermute | solution.py:231
  34.8 5.4 %collective-permute-start.18 = (f32[32,896]{1,0:T(8,128)S(1)}, f32[32,896]{1,0:T(8,128)S(1)}, u32[]{:S(2)}, u32[]{:S(2)}) collective-permute-start(f32[32,896]{1,0:T(8,128)S(1)} %get-tuple-element.24.refs_1_), channel_id=1, source_target_pairs={{16,25},{17,26},{18,27},{19,28},{20,29},{21,30},{22,31},{23,24},{2... | collective-permute-start | bytes 344072 | tf_op jit(solution)/shard_map/ppermute | solution.py:231
  37.5 4.2 %collective-permute-start.17 = (f32[32,896]{1,0:T(8,128)S(1)}, f32[32,896]{1,0:T(8,128)S(1)}, u32[]{:S(2)}, u32[]{:S(2)}) collective-permute-start(f32[32,896]{1,0:T(8,128)S(1)} %get-tuple-element.24.refs_1_), channel_id=1, source_target_pairs={{16,24},{17,25},{18,26},{19,27},{20,28},{21,29},{22,30},{23,31},{2... | collective-permute-start | bytes 344072 | tf_op jit(solution)/shard_map/ppermute | solution.py:231
  37.5 5.4 %collective-permute-start.24 = (f32[16,128]{1,0:T(8,128)S(1)}, f32[16,128]{1,0:T(8,128)S(1)}, u32[]{:S(2)}, u32[]{:S(2)}) collective-permute-start(f32[16,128]{1,0:T(8,128)S(1)} %get-tuple-element.25), channel_id=1, source_target_pairs={{16,26},{17,27},{18,28},{19,29},{20,30},{21,31},{22,24},{23,25},{2... | collective-permute-start | bytes 24584 | tf_op jit(solution)/shard_map/ppermute | solution.py:231
  37.6 5.3 %collective-permute-start.23 = (f32[16,128]{1,0:T(8,128)S(1)}, f32[16,128]{1,0:T(8,128)S(1)}, u32[]{:S(2)}, u32[]{:S(2)}) collective-permute-start(f32[16,128]{1,0:T(8,128)S(1)} %get-tuple-element.25), channel_id=1, source_target_pairs={{16,27},{17,28},{18,29},{19,30},{20,31},{21,24},{22,25},{23,26},{2... | collective-permute-start | bytes 24584 | tf_op jit(solution)/shard_map/ppermute | solution.py:231
  39.0 4.0 %collective-permute-start.22 = (f32[16,128]{1,0:T(8,128)S(1)}, f32[16,128]{1,0:T(8,128)S(1)}, u32[]{:S(2)}, u32[]{:S(2)}) collective-permute-start(f32[16,128]{1,0:T(8,128)S(1)} %get-tuple-element.25), channel_id=1, source_target_pairs={{16,28},{17,29},{18,30},{19,31},{20,24},{21,25},{22,26},{23,27},{2... | collective-permute-start | bytes 24584 | tf_op jit(solution)/shard_map/ppermute | solution.py:231
  40.2 4.5 %collective-permute-start.21 = (f32[16,128]{1,0:T(8,128)S(1)}, f32[16,128]{1,0:T(8,128)S(1)}, u32[]{:S(2)}, u32[]{:S(2)}) collective-permute-start(f32[16,128]{1,0:T(8,128)S(1)} %get-tuple-element.25), channel_id=1, source_target_pairs={{16,29},{17,30},{18,31},{19,24},{20,25},{21,26},{22,27},{23,28},{2... | collective-permute-start | bytes 24584 | tf_op jit(solution)/shard_map/ppermute | solution.py:231
  41.7 3.1 %collective-permute-start.20 = (f32[16,128]{1,0:T(8,128)S(1)}, f32[16,128]{1,0:T(8,128)S(1)}, u32[]{:S(2)}, u32[]{:S(2)}) collective-permute-start(f32[16,128]{1,0:T(8,128)S(1)} %get-tuple-element.25), channel_id=1, source_target_pairs={{16,30},{17,31},{18,24},{19,25},{20,26},{21,27},{22,28},{23,29},{2... | collective-permute-start | bytes 24584 | tf_op jit(solution)/shard_map/ppermute | solution.py:231

commit v2 on v0

v2 whole, which is shorter than its diff:
```python
import jax
import jax.numpy as jnp
from jax import lax
from jax.experimental import pallas as pl
from jax.experimental.pallas import tpu as pltpu
from jax.sharding import PartitionSpec as P

f32 = jnp.float32
bf16 = jnp.bfloat16
small_eps = 1e-06
both_axes = ("slab", "trace")
in_vmem = pl.BlockSpec(memory_space=pltpu.VMEM)
in_smem = pl.BlockSpec(memory_space=pltpu.SMEM)

pieces = 4


def two_parts(x):
    high = x.astype(bf16)
    return high, (x - high.astype(f32)).astype(bf16)


def three_parts(x):
    high = x.astype(bf16)
    rest = x - high.astype(f32)
    middle = rest.astype(bf16)
    return high, middle, (rest - middle.astype(f32)).astype(bf16)


def dot(a, b):
    return jnp.dot(a, b, preferred_element_type=f32)


def times(stacked, high, weight_high, weight_low):
    rows = high.shape[0]
    both = dot(stacked, weight_high)
    return both[:rows] + both[rows:] + dot(high, weight_low)


def complex_times(x, weights):
    high, low = two_parts(x)
    stacked = jnp.concatenate([high, low], axis=0)
    by_re = times(stacked, high, *weights[0])
    by_im = times(stacked, high, *weights[1])
    half = x.shape[0] // 2
    return by_re[:half] - by_im[half:], by_im[:half] + by_re[half:]


def on_odd():
    return lax.rem(lax.axis_index("trace"), 2) == 1


def pick(x, skel_row):
    n, width = x.shape
    rank = skel_row.shape[1]
    rows = lax.broadcasted_iota(jnp.int32, (width, rank), 0)
    chosen = jnp.where(rows == skel_row, 1.0, 0.0).astype(bf16)
    out = dot(jnp.concatenate(three_parts(x), axis=0), chosen)
    out = out[:n] + (out[n : 2 * n] + out[2 * n :])
    lane = lax.broadcasted_iota(jnp.int32, (n, 2 * rank), 1)
    return jnp.where((lane >= rank) == on_odd(), jnp.concatenate([out, out], axis=1), 0.0)


def first_kernel(skel_ref, src_ref, small_ref):
    small_ref[...] = pick(src_ref[...], skel_ref[...])


def split_tiles(slot, tiles_ref, half_refs, held_ref, sems, meanwhile):
    pieces_all, rows, _ = held_ref.shape
    _, tile, _ = tiles_ref.shape
    per = tile // rows
    copies = [
        pltpu.make_async_copy(
            tiles_ref.at[slot * (pieces_all // per) + i // per, pl.ds(i % per * rows, rows)],
            held_ref.at[i],
            sems.at[i],
        )
        for i in range(pieces_all)
    ]
    for copy in copies:
        copy.start()
    meanwhile()
    high_ref, low_ref = half_refs
    for i, copy in enumerate(copies):
        copy.wait()
        high, low = two_parts(held_ref[i])
        place = pl.ds(i % per * rows, rows)
        high_ref[i // per, place] = high
        low_ref[i // per, place] = low


def split_far_kernel(side_ref, coupling_in, basis_in, tiles_ref, *refs):
    coef_ref, base_ref, *half_refs, coupling_ref, basis_ref, far_sems, held_ref, sems = refs
    far_copies = [
        pltpu.make_async_copy(coupling_in, coupling_ref, far_sems.at[0]),
        pltpu.make_async_copy(basis_in, basis_ref, far_sems.at[1]),
    ]
    for copy in far_copies:
        copy.start()

    def meanwhile():
        for copy in far_copies:
            copy.wait()
        split_far(side_ref, coupling_ref, basis_ref, coef_ref, base_ref)

    split_tiles(0, tiles_ref, half_refs, held_ref, sems, meanwhile)


def split_kernel(tiles_ref, high_ref, low_ref, held_ref, sems):
    split_tiles(1, tiles_ref, (high_ref, low_ref), held_ref, sems, lambda: None)


def split_far(side_ref, coupling_ref, basis_ref, coef_ref, base_ref):
    here = lax.axis_index("trace")
    _, rank, total = coupling_ref.shape
    width = 2 * rank
    half = lax.broadcasted_iota(jnp.int32, (rank, width), 1) // rank
    for j in range(total // width):
        group = (here // 2) ^ j
        block = group * 2 + half
        keep = (block != here) & (block != here + side_ref[0, 0])
        place = pl.ds(pl.multiple_of(group * width, width), width)
        for part in range(2):
            high, low = two_parts(jnp.where(keep, coupling_ref[part, :, place], 0.0).T)
            coef_ref[part, 0, j * width : (j + 1) * width] = high
            coef_ref[part, 1, j * width : (j + 1) * width] = low
    for part in range(2):
        high, low = two_parts(basis_ref[part])
        base_ref[part, 0] = high
        base_ref[part, 1] = low


def add_near(out_ref, start, x, high_ref, low_ref):
    half = x.shape[0] // 2
    re, im = complex_times(x, [(high_ref[p], low_ref[p]) for p in range(2)])
    out_ref[:half] = start[:half] + re
    out_ref[half:] = start[half:] + im


def own_kernel(step, own_ref, src_ref, high_ref, low_ref, out_ref):
    @pl.when(lax.axis_index("slab") == step)
    def _():
        add_near(out_ref, src_ref[...], own_ref[...], high_ref, low_ref)


def beside_kernel(step, side_ref, mate_ref, other_ref, start_ref, high_ref, low_ref, out_ref):
    @pl.when(lax.axis_index("slab") == step)
    def _():
        width = start_ref.shape[1]
        mate = (side_ref[0, 0] < 0) == on_odd()
        x = jnp.where(mate, mate_ref[:, :width], other_ref[:, :width])
        add_near(out_ref, start_ref[...], x, high_ref, low_ref)


def far_kernel(step, skel_ref, old_ref, near_ref, mate_ref, *refs):
    *pair_refs, coef_ref, base_ref, state_ref, small_ref = refs
    active = lax.axis_index("slab") == step
    width = near_ref.shape[1]

    @pl.when(active)
    def _():
        values = [ref[...] for ref in pair_refs]
        values = jnp.concatenate([mate_ref[:, width:]] + values, axis=1)
        weights = [(coef_ref[p, 0], coef_ref[p, 1]) for p in range(2)]
        coef = jnp.concatenate(complex_times(values, weights), axis=0)
        weights = [(base_ref[p, 0], base_ref[p, 1]) for p in range(2)]
        far = jnp.concatenate(complex_times(coef, weights), axis=0)
        new = near_ref[...] + far
        state_ref[...] = new
        small_ref[...] = pick(new, skel_ref[...])

    @pl.when(jnp.logical_not(active))
    def _():
        state_ref[...] = old_ref[...]
        small_ref[...] = jnp.zeros_like(small_ref)


def energy_kernel(state_ref, out_ref):
    half = state_ref.shape[0] // 2
    squares = state_ref[...] * state_ref[...]
    each = jnp.sum(squares[:half] + squares[half:], axis=1, keepdims=True)
    out_ref[...] = jnp.broadcast_to(jnp.broadcast_to(each, (half, 128)).T[:1], out_ref.shape)


def norm_kernel(count, state_ref, sums_ref, out_ref):
    half = state_ref.shape[0] // 2
    total = jnp.sum(sums_ref[...], axis=0, keepdims=True)
    scale = jnp.broadcast_to(1.0 / jnp.sqrt(total / count + small_eps), (128, half)).T[:, :1]
    out_ref[0] = state_ref[:half] * scale
    out_ref[1] = state_ref[half:] * scale


def about(us):
    return pl.CostEstimate(
        flops=int(us * 1.15e9), bytes_accessed=int(us * 3.69e6), transcendentals=0
    )


def across(c, blocks):
    return min(max((c ^ 1) + (2 if c % 2 else -2), 0), blocks - 1)


def call(kernel, name, outs, specs, args, room=6, **more):
    many = isinstance(outs, tuple)
    return pl.pallas_call(
        kernel,
        out_shape=outs,
        in_specs=specs,
        out_specs=[in_vmem] * len(outs) if many else in_vmem,
        compiler_params=pltpu.CompilerParams(vmem_limit_bytes=room << 20),
        name=name,
        **more,
    )(*args)


in_hbm = pl.BlockSpec(memory_space=pl.ANY)


def far_from(x):
    return pltpu.with_memory_space_constraint(x, pltpu.HBM)


def ring_pairs(step, move, slabs, blocks):
    pairs = []
    for place in range(slabs):
        source = (step - 1 + place) % slabs
        target = (source + 1) % slabs
        for c in range(blocks):
            pairs.append((source * blocks + c, target * blocks + (move(c) if place == 0 else c)))
    return pairs


def on_device(near_tiles, near_side, skeleton, far_coupling, far_basis, sources):
    slabs = lax.axis_size("slab")
    blocks = lax.axis_size("trace")
    _, slots, parts, tile, width = near_tiles.shape
    _, _, batches, shots, _ = sources.shape
    rank = skeleton.shape[2]
    rows = batches * shots
    n = parts * rows
    state_type = jax.ShapeDtypeStruct((n, width), f32)
    small_type = jax.ShapeDtypeStruct((n, 2 * rank), f32)

    src = sources.reshape(n, width)
    skel_next = lax.ppermute(
        skeleton.reshape(1, rank), "slab", [((s + 1) % slabs, s) for s in range(slabs)]
    )
    halves = jax.ShapeDtypeStruct((parts, tile, width), bf16)

    held = [
        pltpu.VMEM((parts * pieces, tile // pieces, width), f32),
        pltpu.SemaphoreType.DMA((parts * pieces,)),
    ]

    def split_first(planes):
        coef, base, *own_halves = call(
            split_far_kernel,
            "split_own",
            (
                jax.ShapeDtypeStruct((parts, 2, blocks * rank, rank), bf16),
                jax.ShapeDtypeStruct((parts, 2, rank, width), bf16),
                halves,
                halves,
            ),
            [in_smem] + [in_hbm] * 3,
            (near_side, far_from(far_coupling[0]), far_from(far_basis[0]), far_from(planes)),
            scratch_shapes=[
                pltpu.VMEM(far_coupling.shape[1:], f32),
                pltpu.VMEM(far_basis.shape[1:], f32),
                pltpu.SemaphoreType.DMA((2,)),
                *held,
            ],
            cost_estimate=about(2.5),
            room=12,
        )
        return coef, base, own_halves

    def split_second(planes):
        return call(
            split_kernel,
            "split_beside",
            (halves, halves),
            [in_hbm],
            (far_from(planes),),
            scratch_shapes=held,
            cost_estimate=about(2.5),
            room=12,
        )

    planes = near_tiles.reshape(slots * parts, tile, width)
    coef, base, own_halves = split_first(planes)
    skel_next, coef = lax.optimization_barrier((skel_next, coef))
    state = src
    small = call(first_kernel, "first", small_type, [in_vmem] * 2, (skel_next, src))
    state, small = lax.optimization_barrier((state, small))

    for step in range(1, slabs):

        def send(x, move):
            return lax.ppermute(x, both_axes, ring_pairs(step, move, slabs, blocks))

        def send_pair(x, j):
            return send(x, lambda c: c ^ (2 * j))

        swapped = lax.ppermute(small, "trace", [(c, c ^ 1) for c in range(blocks)])
        pair = small + swapped
        own = send(state, lambda c: c)
        if step == 1:
            own, planes = lax.optimization_barrier((own, planes))
            beside_halves = split_second(planes)
        wide = jnp.concatenate([state, small], axis=1)
        ways = range(1, blocks // 2)
        mate = send(wide, lambda c: c ^ 1)
        other = send(state, lambda c: across(c, blocks))
        by_way = {j: send_pair(pair, j) for j in reversed(ways)}
        pairs = [by_way[j] for j in ways]
        near = call(
            lambda *refs, step=step: own_kernel(step, *refs),
            "own",
            state_type,
            [in_vmem] * 4,
            (own, src, *own_halves),
            cost_estimate=about(5),
        )
        near = call(
            lambda *refs, step=step: beside_kernel(step, *refs),
            "beside",
            state_type,
            [in_smem] + [in_vmem] * 5,
            (near_side, mate, other, near, *beside_halves),
            cost_estimate=about(0.85),
        )
        args = (skel_next, state, near, mate, *pairs, coef, base)
        state, small = call(
            lambda *refs, step=step: far_kernel(step, *refs),
            "far",
            (state_type, small_type),
            [in_vmem] * len(args),
            args,
            cost_estimate=about(0.7),
        )

    partial = call(
        energy_kernel, "energy", jax.ShapeDtypeStruct((blocks, rows), f32), [in_vmem], (state,)
    )
    sums = lax.all_to_all(partial, "trace", 0, 0)
    normed = call(
        lambda *refs: norm_kernel(float(parts * width * blocks), *refs),
        "norm",
        jax.ShapeDtypeStruct((parts, rows, width), f32),
        [in_vmem] * 2,
        (state, sums),
    )
    return normed.reshape(sources.shape)


def solution(mesh):
    placed = (
        P("slab", None, None, None, "trace"),
        P("slab", "trace"),
        P("slab", "trace", None),
        P("slab", None, "trace", None),
        P("slab", None, None, "trace"),
        P("slab", None, None, None, "trace"),
    )
    return jax.shard_map(
        on_device,
        mesh=mesh,
        in_specs=placed,
        out_specs=P("slab", None, None, None, "trace"),
        check_vma=False,
    )
```

time: 295 us -> 51.7 us (0.18)
  the two profiles are of different devices: /device:TPU:4 before, /device:TPU:0 now
where the time goes in v2:
time: 51.7 us; the launch traced here: 51.5 us
  starting transfers between devices  21.6 us (42%)
  blocking collectives  12.3 us (24%)
  waiting for transfers between devices  8.85 us (17%)
  Pallas kernels  7.93 us (15%)
  between operations  0.8 us (2%)
    ppermute x18, starting transfers between devices, send(): return lax.ppermute(x, both_axes, ring_pairs(step, move, slabs, blocks))  15.7 us
    all_to_all x1, blocking collectives, on_device(): sums = lax.all_to_all(partial, 'trace', 0, 0)  12.3 us
    pallas_call x14, Pallas kernels, call(): pl.pallas_call(kernel, out_shape=outs, in_specs=specs, out_specs=[in_vmem...  7.93 us
    ppermute x18, waiting for transfers between devices, send(): return lax.ppermute(x, both_axes, ring_pairs(step, move, slabs, blocks))  6.03 us
    ppermute x3, starting transfers between devices, on_device(): swapped = lax.ppermute(small, 'trace', [(c, c ^ 1) for c in range(blocks)])  3.53 us
    ppermute x3, waiting for transfers between devices, on_device(): swapped = lax.ppermute(small, 'trace', [(c, c ^ 1) for c in range(blocks)])  2.81 us
    ppermute x1, starting transfers between devices, on_device(): lax.ppermute(skeleton.reshape(1, rank), 'slab', [((s + 1) % slabs, s) for...  2.41 us
  transfers between devices with their start and end apart: 22, of which 11 were waited for; matrix products, arithmetic and copies ran while one was open for 0% of the time, Pallas kernels for 12%

profile of v2, /device:TPU:0, one launch (start us, length us, event | category | flops | bytes accessed | tf_op | source)
XLA Modules:
  0.0 51.5 jit_solution(9479336175948440661)
XLA Ops:
  0.0 2.4 %collective-permute-start = (s32[1,64]{1,0:T(1,128)}, s32[1,64]{1,0:T(1,128)S(1)}, u32[]{:S(2)}, u32[]{:S(2)}) collective-permute-start(s32[1,64]{1,0:T(1,128)} %bitcast.26), channel_id=1, source_target_pairs={{8,0},{16,8},{24,16},{0,24},{9,1},{17,9},{25,17},{1,25},{10,2},{18... | collective-permute-start | bytes 776 | tf_op jit(solution)/shard_map/ppermute | solution.py:245
  3.1 3.6 %split_own.1 = (bf16[2,2,512,64]{3,2,1,0:T(8,128)(2,1)S(1)}, bf16[2,2,64,768]{3,2,1,0:T(8,128)(2,1)S(1)}, bf16[2,768,768]{2,1,0:T(8,128)(2,1)S(1)}, bf16[2,768,768]{2,1,0:T(8,128)(2,1)S(1)}) custom-call(s32[1,1]{1,0:T(1,128)S(6)} %copy.10.side_ref.refs_0_, f32[2,64,512]{2,1,0:T(8,128)} %bitcast.25, f32[2,64,768]{2,1,0:T(8,128)} %bitcast.24, ...), custom_call_target="tpu_custom_call" | custom-call | flops 2875000064 | bytes 9225000 | tf_op jit(solution)/shard_map/split_own/pallas_call | solution.py:205
  6.6 0.0 collective-permute-done.skel_ref.refs_0_
  6.7 0.3 first.1
  6.9 0.0 collective-permute-start.3
  6.9 1.6 %collective-permute-start.4 = (f32[32,128]{1,0:T(8,128)S(1)}, f32[32,128]{1,0:T(8,128)S(1)}, u32[]{:S(2)}, u32[]{:S(2)}) collective-permute-start(f32[32,128]{1,0:T(8,128)S(1)} %first.1), channel_id=1, source_target_pairs={{0,1},{1,0},{2,3},{3,2},{4,5},{5,4},{6,7},{7,6},{8,9},{9,8},{10,11... | collective-permute-start | bytes 49160 | tf_op jit(solution)/shard_map/ppermute | solution.py:305
  8.5 0.4 collective-permute-start.2
  8.9 0.9 %collective-permute-start.1 = (f32[32,896]{1,0:T(8,128)S(1)}, f32[32,896]{1,0:T(8,128)S(1)}, u32[]{:S(2)}, u32[]{:S(2)}) collective-permute-start(f32[32,896]{1,0:T(8,128)S(1)} %pad_maximum_fusion), channel_id=1, source_target_pairs={{0,9},{1,8},{2,11},{3,10},{4,13},{5,12},{6,15},{7,14},{8,16},{9,17... | collective-permute-start | bytes 344072 | tf_op jit(solution)/shard_map/ppermute | solution.py:300
  9.8 0.9 %collective-permute-done.4 = f32[32,128]{1,0:T(8,128)S(1)} collective-permute-done((f32[32,128]{1,0:T(8,128)S(1)}, f32[32,128]{1,0:T(8,128)S(1)}, u32[]{:S(2)}, u32[]{:S(2)}) %collective-permute-start.4) | collective-permute-done | bytes 16416 | tf_op jit(solution)/shard_map/ppermute | solution.py:305
  10.7 1.0 %collective-permute-start.5 = (f32[32,128]{1,0:T(8,128)S(1)}, f32[32,128]{1,0:T(8,128)S(1)}, u32[]{:S(2)}, u32[]{:S(2)}) collective-permute-start(f32[32,128]{1,0:T(8,128)S(1)} %add.9), channel_id=1, source_target_pairs={{0,10},{1,11},{2,8},{3,9},{4,14},{5,15},{6,12},{7,13},{8,16},{9,17... | collective-permute-start | bytes 49160 | tf_op jit(solution)/shard_map/ppermute | solution.py:300
  11.7 2.4 %collective-permute-start.6 = (f32[32,128]{1,0:T(8,128)S(1)}, f32[32,128]{1,0:T(8,128)S(1)}, u32[]{:S(2)}, u32[]{:S(2)}) collective-permute-start(f32[32,128]{1,0:T(8,128)S(1)} %add.9), channel_id=1, source_target_pairs={{0,12},{1,13},{2,14},{3,15},{4,8},{5,9},{6,10},{7,11},{8,16},{9,17... | collective-permute-start | bytes 49160 | tf_op jit(solution)/shard_map/ppermute | solution.py:300
  14.1 0.0 collective-permute-done.3.refs_0_
  14.1 1.1 %collective-permute-start.7 = (f32[32,128]{1,0:T(8,128)S(1)}, f32[32,128]{1,0:T(8,128)S(1)}, u32[]{:S(2)}, u32[]{:S(2)}) collective-permute-start(f32[32,128]{1,0:T(8,128)S(1)} %add.9), channel_id=1, source_target_pairs={{0,14},{1,15},{2,12},{3,13},{4,10},{5,11},{6,8},{7,9},{8,16},{9,17... | collective-permute-start | bytes 49160 | tf_op jit(solution)/shard_map/ppermute | solution.py:300
  15.3 2.5 %split_beside.1 = (bf16[2,768,768]{2,1,0:T(8,128)(2,1)S(1)}, bf16[2,768,768]{2,1,0:T(8,128)(2,1)S(1)}) custom-call(f32[4,768,768]{2,1,0:T(8,128)} %bitcast.23), custom_call_target="tpu_custom_call" | custom-call | flops 2875000064 | bytes 9225000 | tf_op jit(solution)/shard_map/split_beside/pallas_call | solution.py:205
  17.7 0.0 collective-permute-done.2.refs_2_
  17.8 0.0 collective-permute-done.1.refs_1_.refs_3_
  17.8 0.0 collective-permute-done.5.refs_4_
  17.8 0.0 collective-permute-done.7.refs_6_
  17.9 0.2 collective-permute-start.10
  18.1 1.5 %collective-permute-start.11 = (f32[32,128]{1,0:T(8,128)S(1)}, f32[32,128]{1,0:T(8,128)S(1)}, u32[]{:S(2)}, u32[]{:S(2)}) collective-permute-start(f32[32,128]{1,0:T(8,128)S(1)} %get-tuple-element.35), channel_id=1, source_target_pairs={{0,1},{1,0},{2,3},{3,2},{4,5},{5,4},{6,7},{7,6},{8,9},{9,8},{10,11... | collective-permute-start | bytes 49160 | tf_op jit(solution)/shard_map/ppermute | solution.py:305
  19.6 0.1 collective-permute-start.9
  19.7 0.9 %collective-permute-start.8 = (f32[32,896]{1,0:T(8,128)S(1)}, f32[32,896]{1,0:T(8,128)S(1)}, u32[]{:S(2)}, u32[]{:S(2)}) collective-permute-start(f32[32,896]{1,0:T(8,128)S(1)} %pad_maximum_fusion.1), channel_id=1, source_target_pairs={{8,17},{9,16},{10,19},{11,18},{12,21},{13,20},{14,23},{15,22},{16,... | collective-permute-start | bytes 344072 | tf_op jit(solution)/shard_map/ppermute | solution.py:300
  20.6 1.2 %collective-permute-done.11 = f32[32,128]{1,0:T(8,128)S(1)} collective-permute-done((f32[32,128]{1,0:T(8,128)S(1)}, f32[32,128]{1,0:T(8,128)S(1)}, u32[]{:S(2)}, u32[]{:S(2)}) %collective-permute-start.11) | collective-permute-done | bytes 16416 | tf_op jit(solution)/shard_map/ppermute | solution.py:305
  21.8 0.0 collective-permute-start.12
  21.8 2.0 %collective-permute-start.13 = (f32[32,128]{1,0:T(8,128)S(1)}, f32[32,128]{1,0:T(8,128)S(1)}, u32[]{:S(2)}, u32[]{:S(2)}) collective-permute-start(f32[32,128]{1,0:T(8,128)S(1)} %add.10), channel_id=1, source_target_pairs={{8,20},{9,21},{10,22},{11,23},{12,16},{13,17},{14,18},{15,19},{16,... | collective-permute-start | bytes 49160 | tf_op jit(solution)/shard_map/ppermute | solution.py:300
  23.8 0.3 collective-permute-start.14
  24.1 0.0 collective-permute-done.9.refs_2_
  24.1 0.9 %collective-permute-done.8.refs_1_.refs_3_ = f32[32,896]{1,0:T(8,128)S(1)} collective-permute-done((f32[32,896]{1,0:T(8,128)S(1)}, f32[32,896]{1,0:T(8,128)S(1)}, u32[]{:S(2)}, u32[]{:S(2)}) %collective-permute-start.8) | collective-permute-done | bytes 114720 | tf_op jit(solution)/shard_map/ppermute | solution.py:300
  24.9 0.2 collective-permute-done.12.refs_4_
  25.1 0.2 collective-permute-done.13.refs_5_
  25.3 1.7 %collective-permute-done.14.refs_6_ = f32[32,128]{1,0:T(8,128)S(1)} collective-permute-done((f32[32,128]{1,0:T(8,128)S(1)}, f32[32,128]{1,0:T(8,128)S(1)}, u32[]{:S(2)}, u32[]{:S(2)}) %collective-permute-start.14) | collective-permute-done | bytes 16416 | tf_op jit(solution)/shard_map/ppermute | solution.py:300
  27.0 2.3 %collective-permute-start.17 = (f32[32,768]{1,0:T(8,128)S(1)}, f32[32,768]{1,0:T(8,128)S(1)}, u32[]{:S(2)}, u32[]{:S(2)}) collective-permute-start(f32[32,768]{1,0:T(8,128)S(1)} %get-tuple-element.36.refs_1_), channel_id=1, source_target_pairs={{16,24},{17,25},{18,26},{19,27},{20,28},{21,29},{22,30},{23,31},{2... | collective-permute-start | bytes 294920 | tf_op jit(solution)/shard_map/ppermute | solution.py:300
  29.2 0.5 collective-permute-start.18
  29.7 2.2 %collective-permute-start.16 = (f32[32,768]{1,0:T(8,128)S(1)}, f32[32,768]{1,0:T(8,128)S(1)}, u32[]{:S(2)}, u32[]{:S(2)}) collective-permute-start(f32[32,768]{1,0:T(8,128)S(1)} %get-tuple-element.36.refs_1_), channel_id=1, source_target_pairs={{16,24},{17,26},{18,25},{19,28},{20,27},{21,30},{22,29},{23,31},{2... | collective-permute-start | bytes 294920 | tf_op jit(solution)/shard_map/ppermute | solution.py:300
  32.0 0.4 collective-permute-start.15
  32.3 0.7 %collective-permute-done.18 = f32[32,128]{1,0:T(8,128)S(1)} collective-permute-done((f32[32,128]{1,0:T(8,128)S(1)}, f32[32,128]{1,0:T(8,128)S(1)}, u32[]{:S(2)}, u32[]{:S(2)}) %collective-permute-start.18) | collective-permute-done | bytes 16416 | tf_op jit(solution)/shard_map/ppermute | solution.py:305
  33.0 0.6 %collective-permute-start.19 = (f32[32,128]{1,0:T(8,128)S(1)}, f32[32,128]{1,0:T(8,128)S(1)}, u32[]{:S(2)}, u32[]{:S(2)}) collective-permute-start(f32[32,128]{1,0:T(8,128)S(1)} %add.11), channel_id=1, source_target_pairs={{16,26},{17,27},{18,24},{19,25},{20,30},{21,31},{22,28},{23,29},{2... | collective-permute-start | bytes 49160 | tf_op jit(solution)/shard_map/ppermute | solution.py:300
  33.6 0.9 %collective-permute-start.20 = (f32[32,128]{1,0:T(8,128)S(1)}, f32[32,128]{1,0:T(8,128)S(1)}, u32[]{:S(2)}, u32[]{:S(2)}) collective-permute-start(f32[32,128]{1,0:T(8,128)S(1)} %add.11), channel_id=1, source_target_pairs={{16,28},{17,29},{18,30},{19,31},{20,24},{21,25},{22,26},{23,27},{2... | collective-permute-start | bytes 49160 | tf_op jit(solution)/shard_map/ppermute | solution.py:300
  34.5 0.0 collective-permute-done.17.refs_0_
  34.5 0.1 collective-permute-start.21
  34.6 1.6 %collective-permute-done.15.refs_1_.refs_3_ = f32[32,896]{1,0:T(8,128)S(1)} collective-permute-done((f32[32,896]{1,0:T(8,128)S(1)}, f32[32,896]{1,0:T(8,128)S(1)}, u32[]{:S(2)}, u32[]{:S(2)}) %collective-permute-start.15) | collective-permute-done | bytes 114720 | tf_op jit(solution)/shard_map/ppermute | solution.py:300
  36.2 0.2 collective-permute-done.19.refs_4_
  36.4 0.4 collective-permute-done.20.refs_5_
  36.7 0.9 %collective-permute-done.21.refs_6_ = f32[32,128]{1,0:T(8,128)S(1)} collective-permute-done((f32[32,128]{1,0:T(8,128)S(1)}, f32[32,128]{1,0:T(8,128)S(1)}, u32[]{:S(2)}, u32[]{:S(2)}) %collective-permute-start.21) | collective-permute-done | bytes 16416 | tf_op jit(solution)/shard_map/ppermute | solution.py:300
  37.7 0.6 %far.5 = (f32[32,768]{1,0:T(8,128)S(1)}, f32[32,128]{1,0:T(8,128)}) custom-call(s32[1,64]{1,0:T(1,128)S(1)} %collective-permute-done.skel_ref.refs_0_, f32[32,768]{1,0:T(8,128)S(1)} %get-tuple-element.36.refs_1_, f32[32,768]{1,0:T(8,128)S(1)} %beside.5.refs_2_, f32[32,896]{1,0:T(8,128)S(1)} %collective-permute-done.15.refs_1_.refs_3_, ...), custom_call_target="tpu_custom_call" | custom-call | flops 805000000 | bytes 2583000 | tf_op jit(solution)/shard_map/far/pallas_call | solution.py:205
  38.3 0.2 energy.1
  38.4 12.3 %all_to_all.11 = f32[8,1,16]{2,1,0:T(1,128)S(1)} all-to-all(f32[8,1,16]{2,1,0:T(1,128)S(1)} %bitcast.21), channel_id=1, replica_groups=mesh['slab'=4,'trace'=8] {'trace'}, dimensions={0} | all-to-all | bytes 1024 | tf_op jit(solution)/shard_map/all_to_all | solution.py:346
  50.7 0.8 %norm.1 = f32[2,16,768]{2,1,0:T(8,128)} custom-call(f32[32,768]{1,0:T(8,128)S(1)} %get-tuple-element.38.state_ref.refs_0_, f32[8,16]{1,0:T(8,128)S(1)} %bitcast.20), custom_call_target="tpu_custom_call" | custom-call | tf_op jit(solution)/shard_map/norm/pallas_call | solution.py:205
  (19 shorter events, 0.1 us)
Async XLA Ops:
  0.0 6.6 %collective-permute-start = (s32[1,64]{1,0:T(1,128)}, s32[1,64]{1,0:T(1,128)S(1)}, u32[]{:S(2)}, u32[]{:S(2)}) collective-permute-start(s32[1,64]{1,0:T(1,128)} %bitcast.26), channel_id=1, source_target_pairs={{8,0},{16,8},{24,16},{0,24},{9,1},{17,9},{25,17},{1,25},{10,2},{18... | collective-permute-start | bytes 776 | tf_op jit(solution)/shard_map/ppermute | solution.py:245
  3.1 3.6 %copy-start = (f32[1,2,1,16,768]{4,3,2,1,0:T(8,128)S(1)}, f32[1,2,1,16,768]{4,3,2,1,0:T(8,128)}, u32[]{:S(2)}) copy-start(f32[1,2,1,16,768]{4,3,2,1,0:T(8,128)} %param.11) | copy-start | bytes 294916
  6.9 7.2 %collective-permute-start.3 = (f32[32,768]{1,0:T(8,128)S(1)}, f32[32,768]{1,0:T(8,128)S(1)}, u32[]{:S(2)}, u32[]{:S(2)}) collective-permute-start(f32[32,768]{1,0:T(8,128)S(1)} %bitcast.13), channel_id=1, source_target_pairs={{0,8},{1,9},{2,10},{3,11},{4,12},{5,13},{6,14},{7,15},{8,16},{9,17... | collective-permute-start | bytes 294920 | tf_op jit(solution)/shard_map/ppermute | solution.py:300
  6.9 3.8 %collective-permute-start.4 = (f32[32,128]{1,0:T(8,128)S(1)}, f32[32,128]{1,0:T(8,128)S(1)}, u32[]{:S(2)}, u32[]{:S(2)}) collective-permute-start(f32[32,128]{1,0:T(8,128)S(1)} %first.1), channel_id=1, source_target_pairs={{0,1},{1,0},{2,3},{3,2},{4,5},{5,4},{6,7},{7,6},{8,9},{9,8},{10,11... | collective-permute-start | bytes 49160 | tf_op jit(solution)/shard_map/ppermute | solution.py:305
  8.5 9.2 %collective-permute-start.2 = (f32[32,768]{1,0:T(8,128)S(1)}, f32[32,768]{1,0:T(8,128)S(1)}, u32[]{:S(2)}, u32[]{:S(2)}) collective-permute-start(f32[32,768]{1,0:T(8,128)S(1)} %bitcast.15), channel_id=1, source_target_pairs={{0,8},{1,10},{2,9},{3,12},{4,11},{5,14},{6,13},{7,15},{8,16},{9,17... | collective-permute-start | bytes 294920 | tf_op jit(solution)/shard_map/ppermute | solution.py:300
  8.9 8.9 %collective-permute-start.1 = (f32[32,896]{1,0:T(8,128)S(1)}, f32[32,896]{1,0:T(8,128)S(1)}, u32[]{:S(2)}, u32[]{:S(2)}) collective-permute-start(f32[32,896]{1,0:T(8,128)S(1)} %pad_maximum_fusion), channel_id=1, source_target_pairs={{0,9},{1,8},{2,11},{3,10},{4,13},{5,12},{6,15},{7,14},{8,16},{9,17... | collective-permute-start | bytes 344072 | tf_op jit(solution)/shard_map/ppermute | solution.py:300
  10.7 7.1 %collective-permute-start.5 = (f32[32,128]{1,0:T(8,128)S(1)}, f32[32,128]{1,0:T(8,128)S(1)}, u32[]{:S(2)}, u32[]{:S(2)}) collective-permute-start(f32[32,128]{1,0:T(8,128)S(1)} %add.9), channel_id=1, source_target_pairs={{0,10},{1,11},{2,8},{3,9},{4,14},{5,15},{6,12},{7,13},{8,16},{9,17... | collective-permute-start | bytes 49160 | tf_op jit(solution)/shard_map/ppermute | solution.py:300
  11.7 6.1 %collective-permute-start.6 = (f32[32,128]{1,0:T(8,128)S(1)}, f32[32,128]{1,0:T(8,128)S(1)}, u32[]{:S(2)}, u32[]{:S(2)}) collective-permute-start(f32[32,128]{1,0:T(8,128)S(1)} %add.9), channel_id=1, source_target_pairs={{0,12},{1,13},{2,14},{3,15},{4,8},{5,9},{6,10},{7,11},{8,16},{9,17... | collective-permute-start | bytes 49160 | tf_op jit(solution)/shard_map/ppermute | solution.py:300
  14.1 3.7 %collective-permute-start.7 = (f32[32,128]{1,0:T(8,128)S(1)}, f32[32,128]{1,0:T(8,128)S(1)}, u32[]{:S(2)}, u32[]{:S(2)}) collective-permute-start(f32[32,128]{1,0:T(8,128)S(1)} %add.9), channel_id=1, source_target_pairs={{0,14},{1,15},{2,12},{3,13},{4,10},{5,11},{6,8},{7,9},{8,16},{9,17... | collective-permute-start | bytes 49160 | tf_op jit(solution)/shard_map/ppermute | solution.py:300
  17.9 5.9 %collective-permute-start.10 = (f32[32,768]{1,0:T(8,128)S(1)}, f32[32,768]{1,0:T(8,128)S(1)}, u32[]{:S(2)}, u32[]{:S(2)}) collective-permute-start(f32[32,768]{1,0:T(8,128)S(1)} %get-tuple-element.34.refs_1_), channel_id=1, source_target_pairs={{8,16},{9,17},{10,18},{11,19},{12,20},{13,21},{14,22},{15,23},{16,... | collective-permute-start | bytes 294920 | tf_op jit(solution)/shard_map/ppermute | solution.py:300
  18.1 3.7 %collective-permute-start.11 = (f32[32,128]{1,0:T(8,128)S(1)}, f32[32,128]{1,0:T(8,128)S(1)}, u32[]{:S(2)}, u32[]{:S(2)}) collective-permute-start(f32[32,128]{1,0:T(8,128)S(1)} %get-tuple-element.35), channel_id=1, source_target_pairs={{0,1},{1,0},{2,3},{3,2},{4,5},{5,4},{6,7},{7,6},{8,9},{9,8},{10,11... | collective-permute-start | bytes 49160 | tf_op jit(solution)/shard_map/ppermute | solution.py:305
  19.6 4.5 %collective-permute-start.9 = (f32[32,768]{1,0:T(8,128)S(1)}, f32[32,768]{1,0:T(8,128)S(1)}, u32[]{:S(2)}, u32[]{:S(2)}) collective-permute-start(f32[32,768]{1,0:T(8,128)S(1)} %get-tuple-element.34.refs_1_), channel_id=1, source_target_pairs={{8,16},{9,18},{10,17},{11,20},{12,19},{13,22},{14,21},{15,23},{16,... | collective-permute-start | bytes 294920 | tf_op jit(solution)/shard_map/ppermute | solution.py:300
  19.7 5.3 %collective-permute-start.8 = (f32[32,896]{1,0:T(8,128)S(1)}, f32[32,896]{1,0:T(8,128)S(1)}, u32[]{:S(2)}, u32[]{:S(2)}) collective-permute-start(f32[32,896]{1,0:T(8,128)S(1)} %pad_maximum_fusion.1), channel_id=1, source_target_pairs={{8,17},{9,16},{10,19},{11,18},{12,21},{13,20},{14,23},{15,22},{16,... | collective-permute-start | bytes 344072 | tf_op jit(solution)/shard_map/ppermute | solution.py:300
  21.8 3.3 %collective-permute-start.12 = (f32[32,128]{1,0:T(8,128)S(1)}, f32[32,128]{1,0:T(8,128)S(1)}, u32[]{:S(2)}, u32[]{:S(2)}) collective-permute-start(f32[32,128]{1,0:T(8,128)S(1)} %add.10), channel_id=1, source_target_pairs={{8,18},{9,19},{10,16},{11,17},{12,22},{13,23},{14,20},{15,21},{16,... | collective-permute-start | bytes 49160 | tf_op jit(solution)/shard_map/ppermute | solution.py:300
  21.8 3.4 %collective-permute-start.13 = (f32[32,128]{1,0:T(8,128)S(1)}, f32[32,128]{1,0:T(8,128)S(1)}, u32[]{:S(2)}, u32[]{:S(2)}) collective-permute-start(f32[32,128]{1,0:T(8,128)S(1)} %add.10), channel_id=1, source_target_pairs={{8,20},{9,21},{10,22},{11,23},{12,16},{13,17},{14,18},{15,19},{16,... | collective-permute-start | bytes 49160 | tf_op jit(solution)/shard_map/ppermute | solution.py:300
  23.8 3.2 %collective-permute-start.14 = (f32[32,128]{1,0:T(8,128)S(1)}, f32[32,128]{1,0:T(8,128)S(1)}, u32[]{:S(2)}, u32[]{:S(2)}) collective-permute-start(f32[32,128]{1,0:T(8,128)S(1)} %add.10), channel_id=1, source_target_pairs={{8,22},{9,23},{10,20},{11,21},{12,18},{13,19},{14,16},{15,17},{16,... | collective-permute-start | bytes 49160 | tf_op jit(solution)/shard_map/ppermute | solution.py:300
  27.0 7.5 %collective-permute-start.17 = (f32[32,768]{1,0:T(8,128)S(1)}, f32[32,768]{1,0:T(8,128)S(1)}, u32[]{:S(2)}, u32[]{:S(2)}) collective-permute-start(f32[32,768]{1,0:T(8,128)S(1)} %get-tuple-element.36.refs_1_), channel_id=1, source_target_pairs={{16,24},{17,25},{18,26},{19,27},{20,28},{21,29},{22,30},{23,31},{2... | collective-permute-start | bytes 294920 | tf_op jit(solution)/shard_map/ppermute | solution.py:300
  29.2 3.7 %collective-permute-start.18 = (f32[32,128]{1,0:T(8,128)S(1)}, f32[32,128]{1,0:T(8,128)S(1)}, u32[]{:S(2)}, u32[]{:S(2)}) collective-permute-start(f32[32,128]{1,0:T(8,128)S(1)} %get-tuple-element.37), channel_id=1, source_target_pairs={{0,1},{1,0},{2,3},{3,2},{4,5},{5,4},{6,7},{7,6},{8,9},{9,8},{10,11... | collective-permute-start | bytes 49160 | tf_op jit(solution)/shard_map/ppermute | solution.py:305
  29.7 4.8 %collective-permute-start.16 = (f32[32,768]{1,0:T(8,128)S(1)}, f32[32,768]{1,0:T(8,128)S(1)}, u32[]{:S(2)}, u32[]{:S(2)}) collective-permute-start(f32[32,768]{1,0:T(8,128)S(1)} %get-tuple-element.36.refs_1_), channel_id=1, source_target_pairs={{16,24},{17,26},{18,25},{19,28},{20,27},{21,30},{22,29},{23,31},{2... | collective-permute-start | bytes 294920 | tf_op jit(solution)/shard_map/ppermute | solution.py:300
  32.0 4.2 %collective-permute-start.15 = (f32[32,896]{1,0:T(8,128)S(1)}, f32[32,896]{1,0:T(8,128)S(1)}, u32[]{:S(2)}, u32[]{:S(2)}) collective-permute-start(f32[32,896]{1,0:T(8,128)S(1)} %pad_maximum_fusion.2), channel_id=1, source_target_pairs={{16,25},{17,24},{18,27},{19,26},{20,29},{21,28},{22,31},{23,30},{2... | collective-permute-start | bytes 344072 | tf_op jit(solution)/shard_map/ppermute | solution.py:300
  33.0 3.4 %collective-permute-start.19 = (f32[32,128]{1,0:T(8,128)S(1)}, f32[32,128]{1,0:T(8,128)S(1)}, u32[]{:S(2)}, u32[]{:S(2)}) collective-permute-start(f32[32,128]{1,0:T(8,128)S(1)} %add.11), channel_id=1, source_target_pairs={{16,26},{17,27},{18,24},{19,25},{20,30},{21,31},{22,28},{23,29},{2... | collective-permute-start | bytes 49160 | tf_op jit(solution)/shard_map/ppermute | solution.py:300
  33.6 3.2 %collective-permute-start.20 = (f32[32,128]{1,0:T(8,128)S(1)}, f32[32,128]{1,0:T(8,128)S(1)}, u32[]{:S(2)}, u32[]{:S(2)}) collective-permute-start(f32[32,128]{1,0:T(8,128)S(1)} %add.11), channel_id=1, source_target_pairs={{16,28},{17,29},{18,30},{19,31},{20,24},{21,25},{22,26},{23,27},{2... | collective-permute-start | bytes 49160 | tf_op jit(solution)/shard_map/ppermute | solution.py:300
  34.5 3.2 %collective-permute-start.21 = (f32[32,128]{1,0:T(8,128)S(1)}, f32[32,128]{1,0:T(8,128)S(1)}, u32[]{:S(2)}, u32[]{:S(2)}) collective-permute-start(f32[32,128]{1,0:T(8,128)S(1)} %add.11), channel_id=1, source_target_pairs={{16,30},{17,31},{18,28},{19,29},{20,26},{21,27},{22,24},{23,25},{2... | collective-permute-start | bytes 49160 | tf_op jit(solution)/shard_map/ppermute | solution.py:300

commit v3 on v2

--- a/solution.py
+++ b/solution.py
@@ -89,25 +89,29 @@
         low_ref[i // per, place] = low
 
 
+def split_kernel(tiles_ref, high_ref, low_ref, held_ref, sems):
+    split_tiles(0, tiles_ref, (high_ref, low_ref), held_ref, sems, lambda: None)
+
+
 def split_far_kernel(side_ref, coupling_in, basis_in, tiles_ref, *refs):
     coef_ref, base_ref, *half_refs, coupling_ref, basis_ref, far_sems, held_ref, sems = refs
     far_copies = [
         pltpu.make_async_copy(coupling_in, coupling_ref, far_sems.at[0]),
         pltpu.make_async_copy(basis_in, basis_ref, far_sems.at[1]),
     ]
-    for copy in far_copies:
-        copy.start()
 
     def meanwhile():
         for copy in far_copies:
-            copy.wait()
-        split_far(side_ref, coupling_ref, basis_ref, coef_ref, base_ref)
-
-    split_tiles(0, tiles_ref, half_refs, held_ref, sems, meanwhile)
-
-
-def split_kernel(tiles_ref, high_ref, low_ref, held_ref, sems):
-    split_tiles(1, tiles_ref, (high_ref, low_ref), held_ref, sems, lambda: None)
+            copy.start()
+
+    split_tiles(1, tiles_ref, half_refs, held_ref, sems, meanwhile)
+    for copy in far_copies:
+        copy.wait()
+    split_far(side_ref, coupling_ref, basis_ref, coef_ref, base_ref)
+
+
+def pair_ways(count):
+    return [0, *range(count - 1, 0, -1)]
 
 
 def split_far(side_ref, coupling_ref, basis_ref, coef_ref, base_ref):
@@ -115,8 +119,8 @@
     _, rank, total = coupling_ref.shape
     width = 2 * rank
     half = lax.broadcasted_iota(jnp.int32, (rank, width), 1) // rank
-    for j in range(total // width):
-        group = (here // 2) ^ j
+    for j, way in enumerate(pair_ways(total // width)):
+        group = (here // 2) ^ way
         block = group * 2 + half
         keep = (block != here) & (block != here + side_ref[0, 0])
         place = pl.ds(pl.multiple_of(group * width, width), width)
@@ -152,20 +156,40 @@
         add_near(out_ref, start_ref[...], x, high_ref, low_ref)
 
 
+def add_far(near_ref, mate_ref, pair_refs, coef_ref, base_ref):
+    width = near_ref.shape[1]
+    values = jnp.concatenate([mate_ref[:, width:]] + [ref[...] for ref in pair_refs], axis=1)
+    weights = [(coef_ref[p, 0], coef_ref[p, 1]) for p in range(2)]
+    coef = jnp.concatenate(complex_times(values, weights), axis=0)
+    weights = [(base_ref[p, 0], base_ref[p, 1]) for p in range(2)]
+    return near_ref[...] + jnp.concatenate(complex_times(coef, weights), axis=0)
+
+
+def last_kernel(step, old_ref, near_ref, mate_ref, *refs):
+    *pair_refs, coef_ref, base_ref, state_ref, energy_ref = refs
+    active = lax.axis_index("slab") == step
+
+    @pl.when(active)
+    def _():
+        state_ref[...] = add_far(near_ref, mate_ref, pair_refs, coef_ref, base_ref)
+
+    @pl.when(jnp.logical_not(active))
+    def _():
+        state_ref[...] = old_ref[...]
+
+    half = state_ref.shape[0] // 2
+    squares = state_ref[...] * state_ref[...]
+    each = jnp.sum(squares[:half] + squares[half:], axis=1, keepdims=True)
+    energy_ref[...] = jnp.broadcast_to(jnp.broadcast_to(each, (half, 128)).T[:1], energy_ref.shape)
+
+
 def far_kernel(step, skel_ref, old_ref, near_ref, mate_ref, *refs):
     *pair_refs, coef_ref, base_ref, state_ref, small_ref = refs
     active = lax.axis_index("slab") == step
-    width = near_ref.shape[1]
 
     @pl.when(active)
     def _():
-        values = [ref[...] for ref in pair_refs]
-        values = jnp.concatenate([mate_ref[:, width:]] + values, axis=1)
-        weights = [(coef_ref[p, 0], coef_ref[p, 1]) for p in range(2)]
-        coef = jnp.concatenate(complex_times(values, weights), axis=0)
-        weights = [(base_ref[p, 0], base_ref[p, 1]) for p in range(2)]
-        far = jnp.concatenate(complex_times(coef, weights), axis=0)
-        new = near_ref[...] + far
+        new = add_far(near_ref, mate_ref, pair_refs, coef_ref, base_ref)
         state_ref[...] = new
         small_ref[...] = pick(new, skel_ref[...])
 
@@ -173,13 +197,6 @@
     def _():
         state_ref[...] = old_ref[...]
         small_ref[...] = jnp.zeros_like(small_ref)
-
-
-def energy_kernel(state_ref, out_ref):
-    half = state_ref.shape[0] // 2
-    squares = state_ref[...] * state_ref[...]
-    each = jnp.sum(squares[:half] + squares[half:], axis=1, keepdims=True)
-    out_ref[...] = jnp.broadcast_to(jnp.broadcast_to(each, (half, 128)).T[:1], out_ref.shape)
 
 
 def norm_kernel(count, state_ref, sums_ref, out_ref):
@@ -252,10 +269,22 @@
         pltpu.SemaphoreType.DMA((parts * pieces,)),
     ]
 
-    def split_first(planes):
-        coef, base, *own_halves = call(
+    planes = far_from(near_tiles.reshape(slots * parts, tile, width))
+    own_halves = call(
+        split_kernel,
+        "split_own",
+        (halves, halves),
+        [in_hbm],
+        (planes,),
+        scratch_shapes=held,
+        cost_estimate=about(2.5),
+        room=12,
+    )
+
+    def split_rest(planes):
+        coef, base, *beside_halves = call(
             split_far_kernel,
-            "split_own",
+            "split_beside",
             (
                 jax.ShapeDtypeStruct((parts, 2, blocks * rank, rank), bf16),
                 jax.ShapeDtypeStruct((parts, 2, rank, width), bf16),
@@ -263,7 +292,7 @@
                 halves,
             ),
             [in_smem] + [in_hbm] * 3,
-            (near_side, far_from(far_coupling[0]), far_from(far_basis[0]), far_from(planes)),
+            (near_side, far_from(far_coupling[0]), far_from(far_basis[0]), planes),
             scratch_shapes=[
                 pltpu.VMEM(far_coupling.shape[1:], f32),
                 pltpu.VMEM(far_basis.shape[1:], f32),
@@ -273,23 +302,9 @@
             cost_estimate=about(2.5),
             room=12,
         )
-        return coef, base, own_halves
-
-    def split_second(planes):
-        return call(
-            split_kernel,
-            "split_beside",
-            (halves, halves),
-            [in_hbm],
-            (far_from(planes),),
-            scratch_shapes=held,
-            cost_estimate=about(2.5),
-            room=12,
-        )
-
-    planes = near_tiles.reshape(slots * parts, tile, width)
-    coef, base, own_halves = split_first(planes)
-    skel_next, coef = lax.optimization_barrier((skel_next, coef))
+        return coef, base, beside_halves
+
+    skel_next, *own_halves = lax.optimization_barrier((skel_next, *own_halves))
     state = src
     small = call(first_kernel, "first", small_type, [in_vmem] * 2, (skel_next, src))
     state, small = lax.optimization_barrier((state, small))
@@ -307,13 +322,11 @@
         own = send(state, lambda c: c)
         if step == 1:
             own, planes = lax.optimization_barrier((own, planes))
-            beside_halves = split_second(planes)
+            coef, base, beside_halves = split_rest(planes)
         wide = jnp.concatenate([state, small], axis=1)
-        ways = range(1, blocks // 2)
         mate = send(wide, lambda c: c ^ 1)
         other = send(state, lambda c: across(c, blocks))
-        by_way = {j: send_pair(pair, j) for j in reversed(ways)}
-        pairs = [by_way[j] for j in ways]
+        pairs = [send_pair(pair, way) for way in pair_ways(blocks // 2)[1:]]
         near = call(
             lambda *refs, step=step: own_kernel(step, *refs),
             "own",
@@ -330,19 +343,26 @@
             (near_side, mate, other, near, *beside_halves),
             cost_estimate=about(0.85),
         )
-        args = (skel_next, state, near, mate, *pairs, coef, base)
-        state, small = call(
-            lambda *refs, step=step: far_kernel(step, *refs),
-            "far",
-            (state_type, small_type),
-            [in_vmem] * len(args),
-            args,
-            cost_estimate=about(0.7),
-        )
-
-    partial = call(
-        energy_kernel, "energy", jax.ShapeDtypeStruct((blocks, rows), f32), [in_vmem], (state,)
-    )
+        args = (state, near, mate, *pairs, coef, base)
+        if step + 1 < slabs:
+            state, small = call(
+                lambda *refs, step=step: far_kernel(step, *refs),
+                "far",
+                (state_type, small_type),
+                [in_vmem] * (1 + len(args)),
+                (skel_next, *args),
+                cost_estimate=about(0.7),
+            )
+        else:
+            state, partial = call(
+                lambda *refs, step=step: last_kernel(step, *refs),
+                "last",
+                (state_type, jax.ShapeDtypeStruct((blocks, rows), f32)),
+                [in_vmem] * len(args),
+                args,
+                cost_estimate=about(0.7),
+            )
+
     sums = lax.all_to_all(partial, "trace", 0, 0)
     normed = call(
         lambda *refs: norm_kernel(float(parts * width * blocks), *refs),

time: 51.7 us -> 49.6 us (0.959)
  waiting for transfers between devices: 8.85 us -> 7.45 us
  Pallas kernels: 7.93 us -> 6.66 us
    ppermute x18, waiting for transfers between devices: 6.03 us -> 4.18 us  [send(): return lax.ppermute(x, both_axes, ring_pairs(step, move, slabs, blocks))]
    pallas_call x14 -> x13, Pallas kernels: 7.93 us -> 6.66 us  [call(): pl.pallas_call(kernel, out_shape=outs, in_specs=specs, out_specs=[in_vmem...]
  transfers between devices with their start and end apart: 22 -> 22, of which waited for: 11 -> 7; matrix products, arithmetic and copies ran while one was open for 0% -> 0% of each run, Pallas kernels for 12% -> 11%
where the time goes in v3:
time: 49.6 us; the launch traced here: 49.4 us
  starting transfers between devices  22 us (44%)
  blocking collectives  12.4 us (25%)
  waiting for transfers between devices  7.45 us (15%)
  Pallas kernels  6.66 us (13%)
  between operations  0.81 us (2%)
    ppermute x18, starting transfers between devices, send(): return lax.ppermute(x, both_axes, ring_pairs(step, move, slabs, blocks))  15.9 us
    all_to_all x1, blocking collectives, on_device(): sums = lax.all_to_all(partial, 'trace', 0, 0)  12.4 us
    pallas_call x13, Pallas kernels, call(): pl.pallas_call(kernel, out_shape=outs, in_specs=specs, out_specs=[in_vmem...  6.66 us
    ppermute x18, waiting for transfers between devices, send(): return lax.ppermute(x, both_axes, ring_pairs(step, move, slabs, blocks))  4.18 us
    ppermute x3, starting transfers between devices, on_device(): swapped = lax.ppermute(small, 'trace', [(c, c ^ 1) for c in range(blocks)])  3.65 us
    ppermute x3, waiting for transfers between devices, on_device(): swapped = lax.ppermute(small, 'trace', [(c, c ^ 1) for c in range(blocks)])  3.27 us
    ppermute x1, starting transfers between devices, on_device(): lax.ppermute(skeleton.reshape(1, rank), 'slab', [((s + 1) % slabs, s) for...  2.41 us
  transfers between devices with their start and end apart: 22, of which 7 were waited for; matrix products, arithmetic and copies ran while one was open for 0% of the time, Pallas kernels for 11%

profile of v3, /device:TPU:0, one launch (start us, length us, event | category | flops | bytes accessed | tf_op | source)
XLA Modules:
  0.0 49.4 jit_solution(16597337091272247755)
XLA Ops:
  0.0 2.4 %collective-permute-start = (s32[1,64]{1,0:T(1,128)}, s32[1,64]{1,0:T(1,128)S(1)}, u32[]{:S(2)}, u32[]{:S(2)}) collective-permute-start(s32[1,64]{1,0:T(1,128)} %bitcast.26), channel_id=1, source_target_pairs={{8,0},{16,8},{24,16},{0,24},{9,1},{17,9},{25,17},{1,25},{10,2},{18... | collective-permute-start | bytes 776 | tf_op jit(solution)/shard_map/ppermute | solution.py:262
  2.4 2.5 %split_own.1 = (bf16[2,768,768]{2,1,0:T(8,128)(2,1)S(1)}, bf16[2,768,768]{2,1,0:T(8,128)(2,1)S(1)}) custom-call(f32[4,768,768]{2,1,0:T(8,128)} %bitcast.22), custom_call_target="tpu_custom_call" | custom-call | flops 2875000064 | bytes 9225000 | tf_op jit(solution)/shard_map/split_own/pallas_call | solution.py:222
  5.6 0.0 collective-permute-done.skel_ref.refs_0_
  5.6 0.3 first.1
  5.9 0.0 collective-permute-start.3
  5.9 1.6 %collective-permute-start.4 = (f32[32,128]{1,0:T(8,128)S(1)}, f32[32,128]{1,0:T(8,128)S(1)}, u32[]{:S(2)}, u32[]{:S(2)}) collective-permute-start(f32[32,128]{1,0:T(8,128)S(1)} %first.1), channel_id=1, source_target_pairs={{0,1},{1,0},{2,3},{3,2},{4,5},{5,4},{6,7},{7,6},{8,9},{9,8},{10,11... | collective-permute-start | bytes 49160 | tf_op jit(solution)/shard_map/ppermute | solution.py:320
  7.4 0.4 collective-permute-start.2
  7.8 0.9 %collective-permute-start.1 = (f32[32,896]{1,0:T(8,128)S(1)}, f32[32,896]{1,0:T(8,128)S(1)}, u32[]{:S(2)}, u32[]{:S(2)}) collective-permute-start(f32[32,896]{1,0:T(8,128)S(1)} %pad_maximum_fusion), channel_id=1, source_target_pairs={{0,9},{1,8},{2,11},{3,10},{4,13},{5,12},{6,15},{7,14},{8,16},{9,17... | collective-permute-start | bytes 344072 | tf_op jit(solution)/shard_map/ppermute | solution.py:315
  8.7 0.9 %collective-permute-done.4 = f32[32,128]{1,0:T(8,128)S(1)} collective-permute-done((f32[32,128]{1,0:T(8,128)S(1)}, f32[32,128]{1,0:T(8,128)S(1)}, u32[]{:S(2)}, u32[]{:S(2)}) %collective-permute-start.4) | collective-permute-done | bytes 16416 | tf_op jit(solution)/shard_map/ppermute | solution.py:320
  9.7 3.0 %collective-permute-start.5 = (f32[32,128]{1,0:T(8,128)S(1)}, f32[32,128]{1,0:T(8,128)S(1)}, u32[]{:S(2)}, u32[]{:S(2)}) collective-permute-start(f32[32,128]{1,0:T(8,128)S(1)} %add.9), channel_id=1, source_target_pairs={{0,14},{1,15},{2,12},{3,13},{4,10},{5,11},{6,8},{7,9},{8,16},{9,17... | collective-permute-start | bytes 49160 | tf_op jit(solution)/shard_map/ppermute | solution.py:315
  12.7 0.4 collective-permute-start.6
  13.1 0.0 collective-permute-done.3.refs_0_
  13.1 0.0 collective-permute-start.7
  13.1 2.9 %split_beside.1 = (bf16[2,2,512,64]{3,2,1,0:T(8,128)(2,1)S(1)}, bf16[2,2,64,768]{3,2,1,0:T(8,128)(2,1)S(1)}, bf16[2,768,768]{2,1,0:T(8,128)(2,1)S(1)}, bf16[2,768,768]{2,1,0:T(8,128)(2,1)S(1)}) custom-call(s32[1,1]{1,0:T(1,128)S(6)} %copy.10.side_ref.refs_0_, f32[2,64,512]{2,1,0:T(8,128)} %bitcast.25, f32[2,64,768]{2,1,0:T(8,128)} %bitcast.24, ...), custom_call_target="tpu_custom_call" | custom-call | flops 2875000064 | bytes 9225000 | tf_op jit(solution)/shard_map/split_beside/pallas_call | solution.py:222
  15.9 0.0 collective-permute-done.2.refs_2_
  16.0 0.0 collective-permute-done.1.refs_1_.refs_3_
  16.0 0.0 collective-permute-done.5.refs_4_
  16.0 0.0 collective-permute-done.6.refs_5_
  16.0 0.2 collective-permute-done.7.refs_6_
  16.2 1.2 %collective-permute-start.10 = (f32[32,768]{1,0:T(8,128)S(1)}, f32[32,768]{1,0:T(8,128)S(1)}, u32[]{:S(2)}, u32[]{:S(2)}) collective-permute-start(f32[32,768]{1,0:T(8,128)S(1)} %get-tuple-element.37.refs_1_), channel_id=1, source_target_pairs={{8,16},{9,17},{10,18},{11,19},{12,20},{13,21},{14,22},{15,23},{16,... | collective-permute-start | bytes 294920 | tf_op jit(solution)/shard_map/ppermute | solution.py:315
  17.4 1.5 %collective-permute-start.11 = (f32[32,128]{1,0:T(8,128)S(1)}, f32[32,128]{1,0:T(8,128)S(1)}, u32[]{:S(2)}, u32[]{:S(2)}) collective-permute-start(f32[32,128]{1,0:T(8,128)S(1)} %get-tuple-element.38), channel_id=1, source_target_pairs={{0,1},{1,0},{2,3},{3,2},{4,5},{5,4},{6,7},{7,6},{8,9},{9,8},{10,11... | collective-permute-start | bytes 49160 | tf_op jit(solution)/shard_map/ppermute | solution.py:320
  18.9 0.3 collective-permute-start.9
  19.2 0.7 %collective-permute-start.8 = (f32[32,896]{1,0:T(8,128)S(1)}, f32[32,896]{1,0:T(8,128)S(1)}, u32[]{:S(2)}, u32[]{:S(2)}) collective-permute-start(f32[32,896]{1,0:T(8,128)S(1)} %pad_maximum_fusion.1), channel_id=1, source_target_pairs={{8,17},{9,16},{10,19},{11,18},{12,21},{13,20},{14,23},{15,22},{16,... | collective-permute-start | bytes 344072 | tf_op jit(solution)/shard_map/ppermute | solution.py:315
  19.9 1.2 %collective-permute-done.11 = f32[32,128]{1,0:T(8,128)S(1)} collective-permute-done((f32[32,128]{1,0:T(8,128)S(1)}, f32[32,128]{1,0:T(8,128)S(1)}, u32[]{:S(2)}, u32[]{:S(2)}) %collective-permute-start.11) | collective-permute-done | bytes 16416 | tf_op jit(solution)/shard_map/ppermute | solution.py:320
  21.2 0.0 collective-permute-start.12
  21.2 3.2 %collective-permute-start.13 = (f32[32,128]{1,0:T(8,128)S(1)}, f32[32,128]{1,0:T(8,128)S(1)}, u32[]{:S(2)}, u32[]{:S(2)}) collective-permute-start(f32[32,128]{1,0:T(8,128)S(1)} %add.10), channel_id=1, source_target_pairs={{8,20},{9,21},{10,22},{11,23},{12,16},{13,17},{14,18},{15,19},{16,... | collective-permute-start | bytes 49160 | tf_op jit(solution)/shard_map/ppermute | solution.py:315
  24.3 0.0 collective-permute-done.10.refs_0_
  24.3 0.0 collective-permute-start.14
  24.3 0.0 collective-permute-done.9.refs_2_
  24.3 0.0 collective-permute-done.8.refs_1_.refs_3_
  24.4 0.0 collective-permute-done.12.refs_4_
  24.4 0.7 %collective-permute-done.13.refs_5_ = f32[32,128]{1,0:T(8,128)S(1)} collective-permute-done((f32[32,128]{1,0:T(8,128)S(1)}, f32[32,128]{1,0:T(8,128)S(1)}, u32[]{:S(2)}, u32[]{:S(2)}) %collective-permute-start.13) | collective-permute-done | bytes 16416 | tf_op jit(solution)/shard_map/ppermute | solution.py:315
  25.2 2.3 %collective-permute-done.14.refs_6_ = f32[32,128]{1,0:T(8,128)S(1)} collective-permute-done((f32[32,128]{1,0:T(8,128)S(1)}, f32[32,128]{1,0:T(8,128)S(1)}, u32[]{:S(2)}, u32[]{:S(2)}) %collective-permute-start.14) | collective-permute-done | bytes 16416 | tf_op jit(solution)/shard_map/ppermute | solution.py:315
  27.5 0.1 collective-permute-start.17
  27.6 0.6 %collective-permute-start.18 = (f32[32,128]{1,0:T(8,128)S(1)}, f32[32,128]{1,0:T(8,128)S(1)}, u32[]{:S(2)}, u32[]{:S(2)}) collective-permute-start(f32[32,128]{1,0:T(8,128)S(1)} %get-tuple-element.40), channel_id=1, source_target_pairs={{0,1},{1,0},{2,3},{3,2},{4,5},{5,4},{6,7},{7,6},{8,9},{9,8},{10,11... | collective-permute-start | bytes 49160 | tf_op jit(solution)/shard_map/ppermute | solution.py:320
  28.2 1.8 %collective-permute-start.16 = (f32[32,768]{1,0:T(8,128)S(1)}, f32[32,768]{1,0:T(8,128)S(1)}, u32[]{:S(2)}, u32[]{:S(2)}) collective-permute-start(f32[32,768]{1,0:T(8,128)S(1)} %get-tuple-element.39.refs_0_), channel_id=1, source_target_pairs={{16,24},{17,26},{18,25},{19,28},{20,27},{21,30},{22,29},{23,31},{2... | collective-permute-start | bytes 294920 | tf_op jit(solution)/shard_map/ppermute | solution.py:315
  30.0 0.4 collective-permute-start.15
  30.3 1.1 %collective-permute-done.18 = f32[32,128]{1,0:T(8,128)S(1)} collective-permute-done((f32[32,128]{1,0:T(8,128)S(1)}, f32[32,128]{1,0:T(8,128)S(1)}, u32[]{:S(2)}, u32[]{:S(2)}) %collective-permute-start.18) | collective-permute-done | bytes 16416 | tf_op jit(solution)/shard_map/ppermute | solution.py:320
  31.5 0.2 collective-permute-start.19
  31.7 1.0 %collective-permute-start.20 = (f32[32,128]{1,0:T(8,128)S(1)}, f32[32,128]{1,0:T(8,128)S(1)}, u32[]{:S(2)}, u32[]{:S(2)}) collective-permute-start(f32[32,128]{1,0:T(8,128)S(1)} %add.11), channel_id=1, source_target_pairs={{16,28},{17,29},{18,30},{19,31},{20,24},{21,25},{22,26},{23,27},{2... | collective-permute-start | bytes 49160 | tf_op jit(solution)/shard_map/ppermute | solution.py:315
  32.6 0.0 collective-permute-done.17.refs_0_
  32.6 2.5 %collective-permute-start.21 = (f32[32,128]{1,0:T(8,128)S(1)}, f32[32,128]{1,0:T(8,128)S(1)}, u32[]{:S(2)}, u32[]{:S(2)}) collective-permute-start(f32[32,128]{1,0:T(8,128)S(1)} %add.11), channel_id=1, source_target_pairs={{16,26},{17,27},{18,24},{19,25},{20,30},{21,31},{22,28},{23,29},{2... | collective-permute-start | bytes 49160 | tf_op jit(solution)/shard_map/ppermute | solution.py:315
  35.2 0.0 collective-permute-done.16.refs_2_
  35.2 0.0 collective-permute-done.20.refs_4_
  35.2 0.8 %collective-permute-done.21.refs_5_ = f32[32,128]{1,0:T(8,128)S(1)} collective-permute-done((f32[32,128]{1,0:T(8,128)S(1)}, f32[32,128]{1,0:T(8,128)S(1)}, u32[]{:S(2)}, u32[]{:S(2)}) %collective-permute-start.21) | collective-permute-done | bytes 16416 | tf_op jit(solution)/shard_map/ppermute | solution.py:315
  36.0 0.2 last.1
  36.2 12.4 %all_to_all.11 = f32[8,1,16]{2,1,0:T(1,128)S(1)} all-to-all(f32[8,1,16]{2,1,0:T(1,128)S(1)} %bitcast.21), channel_id=1, replica_groups=mesh['slab'=4,'trace'=8] {'trace'}, dimensions={0} | all-to-all | bytes 1024 | tf_op jit(solution)/shard_map/all_to_all | solution.py:366
  48.6 0.8 %norm.1 = f32[2,16,768]{2,1,0:T(8,128)} custom-call(f32[32,768]{1,0:T(8,128)S(1)} %get-tuple-element.41.refs_0_, f32[8,16]{1,0:T(8,128)S(1)} %bitcast.20), custom_call_target="tpu_custom_call" | custom-call | tf_op jit(solution)/shard_map/norm/pallas_call | solution.py:222
  (18 shorter events, 0.1 us)
Async XLA Ops:
  0.0 5.6 %collective-permute-start = (s32[1,64]{1,0:T(1,128)}, s32[1,64]{1,0:T(1,128)S(1)}, u32[]{:S(2)}, u32[]{:S(2)}) collective-permute-start(s32[1,64]{1,0:T(1,128)} %bitcast.26), channel_id=1, source_target_pairs={{8,0},{16,8},{24,16},{0,24},{9,1},{17,9},{25,17},{1,25},{10,2},{18... | collective-permute-start | bytes 776 | tf_op jit(solution)/shard_map/ppermute | solution.py:262
  2.4 3.2 %copy-start = (f32[1,2,1,16,768]{4,3,2,1,0:T(8,128)S(1)}, f32[1,2,1,16,768]{4,3,2,1,0:T(8,128)}, u32[]{:S(2)}) copy-start(f32[1,2,1,16,768]{4,3,2,1,0:T(8,128)} %param.11) | copy-start | bytes 294916
  5.9 7.2 %collective-permute-start.3 = (f32[32,768]{1,0:T(8,128)S(1)}, f32[32,768]{1,0:T(8,128)S(1)}, u32[]{:S(2)}, u32[]{:S(2)}) collective-permute-start(f32[32,768]{1,0:T(8,128)S(1)} %bitcast.13), channel_id=1, source_target_pairs={{0,8},{1,9},{2,10},{3,11},{4,12},{5,13},{6,14},{7,15},{8,16},{9,17... | collective-permute-start | bytes 294920 | tf_op jit(solution)/shard_map/ppermute | solution.py:315
  5.9 3.8 %collective-permute-start.4 = (f32[32,128]{1,0:T(8,128)S(1)}, f32[32,128]{1,0:T(8,128)S(1)}, u32[]{:S(2)}, u32[]{:S(2)}) collective-permute-start(f32[32,128]{1,0:T(8,128)S(1)} %first.1), channel_id=1, source_target_pairs={{0,1},{1,0},{2,3},{3,2},{4,5},{5,4},{6,7},{7,6},{8,9},{9,8},{10,11... | collective-permute-start | bytes 49160 | tf_op jit(solution)/shard_map/ppermute | solution.py:320
  7.4 8.5 %collective-permute-start.2 = (f32[32,768]{1,0:T(8,128)S(1)}, f32[32,768]{1,0:T(8,128)S(1)}, u32[]{:S(2)}, u32[]{:S(2)}) collective-permute-start(f32[32,768]{1,0:T(8,128)S(1)} %bitcast.15), channel_id=1, source_target_pairs={{0,8},{1,10},{2,9},{3,12},{4,11},{5,14},{6,13},{7,15},{8,16},{9,17... | collective-permute-start | bytes 294920 | tf_op jit(solution)/shard_map/ppermute | solution.py:315
  7.8 8.1 %collective-permute-start.1 = (f32[32,896]{1,0:T(8,128)S(1)}, f32[32,896]{1,0:T(8,128)S(1)}, u32[]{:S(2)}, u32[]{:S(2)}) collective-permute-start(f32[32,896]{1,0:T(8,128)S(1)} %pad_maximum_fusion), channel_id=1, source_target_pairs={{0,9},{1,8},{2,11},{3,10},{4,13},{5,12},{6,15},{7,14},{8,16},{9,17... | collective-permute-start | bytes 344072 | tf_op jit(solution)/shard_map/ppermute | solution.py:315
  9.7 6.3 %collective-permute-start.5 = (f32[32,128]{1,0:T(8,128)S(1)}, f32[32,128]{1,0:T(8,128)S(1)}, u32[]{:S(2)}, u32[]{:S(2)}) collective-permute-start(f32[32,128]{1,0:T(8,128)S(1)} %add.9), channel_id=1, source_target_pairs={{0,14},{1,15},{2,12},{3,13},{4,10},{5,11},{6,8},{7,9},{8,16},{9,17... | collective-permute-start | bytes 49160 | tf_op jit(solution)/shard_map/ppermute | solution.py:315
  12.7 3.3 %collective-permute-start.6 = (f32[32,128]{1,0:T(8,128)S(1)}, f32[32,128]{1,0:T(8,128)S(1)}, u32[]{:S(2)}, u32[]{:S(2)}) collective-permute-start(f32[32,128]{1,0:T(8,128)S(1)} %add.9), channel_id=1, source_target_pairs={{0,12},{1,13},{2,14},{3,15},{4,8},{5,9},{6,10},{7,11},{8,16},{9,17... | collective-permute-start | bytes 49160 | tf_op jit(solution)/shard_map/ppermute | solution.py:315
  13.1 3.2 %collective-permute-start.7 = (f32[32,128]{1,0:T(8,128)S(1)}, f32[32,128]{1,0:T(8,128)S(1)}, u32[]{:S(2)}, u32[]{:S(2)}) collective-permute-start(f32[32,128]{1,0:T(8,128)S(1)} %add.9), channel_id=1, source_target_pairs={{0,10},{1,11},{2,8},{3,9},{4,14},{5,15},{6,12},{7,13},{8,16},{9,17... | collective-permute-start | bytes 49160 | tf_op jit(solution)/shard_map/ppermute | solution.py:315
  16.2 8.1 %collective-permute-start.10 = (f32[32,768]{1,0:T(8,128)S(1)}, f32[32,768]{1,0:T(8,128)S(1)}, u32[]{:S(2)}, u32[]{:S(2)}) collective-permute-start(f32[32,768]{1,0:T(8,128)S(1)} %get-tuple-element.37.refs_1_), channel_id=1, source_target_pairs={{8,16},{9,17},{10,18},{11,19},{12,20},{13,21},{14,22},{15,23},{16,... | collective-permute-start | bytes 294920 | tf_op jit(solution)/shard_map/ppermute | solution.py:315
  17.4 3.7 %collective-permute-start.11 = (f32[32,128]{1,0:T(8,128)S(1)}, f32[32,128]{1,0:T(8,128)S(1)}, u32[]{:S(2)}, u32[]{:S(2)}) collective-permute-start(f32[32,128]{1,0:T(8,128)S(1)} %get-tuple-element.38), channel_id=1, source_target_pairs={{0,1},{1,0},{2,3},{3,2},{4,5},{5,4},{6,7},{7,6},{8,9},{9,8},{10,11... | collective-permute-start | bytes 49160 | tf_op jit(solution)/shard_map/ppermute | solution.py:320
  18.9 5.4 %collective-permute-start.9 = (f32[32,768]{1,0:T(8,128)S(1)}, f32[32,768]{1,0:T(8,128)S(1)}, u32[]{:S(2)}, u32[]{:S(2)}) collective-permute-start(f32[32,768]{1,0:T(8,128)S(1)} %get-tuple-element.37.refs_1_), channel_id=1, source_target_pairs={{8,16},{9,18},{10,17},{11,20},{12,19},{13,22},{14,21},{15,23},{16,... | collective-permute-start | bytes 294920 | tf_op jit(solution)/shard_map/ppermute | solution.py:315
  19.2 5.1 %collective-permute-start.8 = (f32[32,896]{1,0:T(8,128)S(1)}, f32[32,896]{1,0:T(8,128)S(1)}, u32[]{:S(2)}, u32[]{:S(2)}) collective-permute-start(f32[32,896]{1,0:T(8,128)S(1)} %pad_maximum_fusion.1), channel_id=1, source_target_pairs={{8,17},{9,16},{10,19},{11,18},{12,21},{13,20},{14,23},{15,22},{16,... | collective-permute-start | bytes 344072 | tf_op jit(solution)/shard_map/ppermute | solution.py:315
  21.2 3.3 %collective-permute-start.12 = (f32[32,128]{1,0:T(8,128)S(1)}, f32[32,128]{1,0:T(8,128)S(1)}, u32[]{:S(2)}, u32[]{:S(2)}) collective-permute-start(f32[32,128]{1,0:T(8,128)S(1)} %add.10), channel_id=1, source_target_pairs={{8,22},{9,23},{10,20},{11,21},{12,18},{13,19},{14,16},{15,17},{16,... | collective-permute-start | bytes 49160 | tf_op jit(solution)/shard_map/ppermute | solution.py:315
  21.2 4.0 %collective-permute-start.13 = (f32[32,128]{1,0:T(8,128)S(1)}, f32[32,128]{1,0:T(8,128)S(1)}, u32[]{:S(2)}, u32[]{:S(2)}) collective-permute-start(f32[32,128]{1,0:T(8,128)S(1)} %add.10), channel_id=1, source_target_pairs={{8,20},{9,21},{10,22},{11,23},{12,16},{13,17},{14,18},{15,19},{16,... | collective-permute-start | bytes 49160 | tf_op jit(solution)/shard_map/ppermute | solution.py:315
  24.3 3.2 %collective-permute-start.14 = (f32[32,128]{1,0:T(8,128)S(1)}, f32[32,128]{1,0:T(8,128)S(1)}, u32[]{:S(2)}, u32[]{:S(2)}) collective-permute-start(f32[32,128]{1,0:T(8,128)S(1)} %add.10), channel_id=1, source_target_pairs={{8,18},{9,19},{10,16},{11,17},{12,22},{13,23},{14,20},{15,21},{16,... | collective-permute-start | bytes 49160 | tf_op jit(solution)/shard_map/ppermute | solution.py:315
  27.5 5.1 %collective-permute-start.17 = (f32[32,768]{1,0:T(8,128)S(1)}, f32[32,768]{1,0:T(8,128)S(1)}, u32[]{:S(2)}, u32[]{:S(2)}) collective-permute-start(f32[32,768]{1,0:T(8,128)S(1)} %get-tuple-element.39.refs_0_), channel_id=1, source_target_pairs={{16,24},{17,25},{18,26},{19,27},{20,28},{21,29},{22,30},{23,31},{2... | collective-permute-start | bytes 294920 | tf_op jit(solution)/shard_map/ppermute | solution.py:315
  27.6 3.9 %collective-permute-start.18 = (f32[32,128]{1,0:T(8,128)S(1)}, f32[32,128]{1,0:T(8,128)S(1)}, u32[]{:S(2)}, u32[]{:S(2)}) collective-permute-start(f32[32,128]{1,0:T(8,128)S(1)} %get-tuple-element.40), channel_id=1, source_target_pairs={{0,1},{1,0},{2,3},{3,2},{4,5},{5,4},{6,7},{7,6},{8,9},{9,8},{10,11... | collective-permute-start | bytes 49160 | tf_op jit(solution)/shard_map/ppermute | solution.py:320
  28.2 7.0 %collective-permute-start.16 = (f32[32,768]{1,0:T(8,128)S(1)}, f32[32,768]{1,0:T(8,128)S(1)}, u32[]{:S(2)}, u32[]{:S(2)}) collective-permute-start(f32[32,768]{1,0:T(8,128)S(1)} %get-tuple-element.39.refs_0_), channel_id=1, source_target_pairs={{16,24},{17,26},{18,25},{19,28},{20,27},{21,30},{22,29},{23,31},{2... | collective-permute-start | bytes 294920 | tf_op jit(solution)/shard_map/ppermute | solution.py:315
  30.0 5.2 %collective-permute-start.15 = (f32[32,896]{1,0:T(8,128)S(1)}, f32[32,896]{1,0:T(8,128)S(1)}, u32[]{:S(2)}, u32[]{:S(2)}) collective-permute-start(f32[32,896]{1,0:T(8,128)S(1)} %pad_maximum_fusion.2), channel_id=1, source_target_pairs={{16,25},{17,24},{18,27},{19,26},{20,29},{21,28},{22,31},{23,30},{2... | collective-permute-start | bytes 344072 | tf_op jit(solution)/shard_map/ppermute | solution.py:315
  31.5 3.7 %collective-permute-start.19 = (f32[32,128]{1,0:T(8,128)S(1)}, f32[32,128]{1,0:T(8,128)S(1)}, u32[]{:S(2)}, u32[]{:S(2)}) collective-permute-start(f32[32,128]{1,0:T(8,128)S(1)} %add.11), channel_id=1, source_target_pairs={{16,30},{17,31},{18,28},{19,29},{20,26},{21,27},{22,24},{23,25},{2... | collective-permute-start | bytes 49160 | tf_op jit(solution)/shard_map/ppermute | solution.py:315
  31.7 3.5 %collective-permute-start.20 = (f32[32,128]{1,0:T(8,128)S(1)}, f32[32,128]{1,0:T(8,128)S(1)}, u32[]{:S(2)}, u32[]{:S(2)}) collective-permute-start(f32[32,128]{1,0:T(8,128)S(1)} %add.11), channel_id=1, source_target_pairs={{16,28},{17,29},{18,30},{19,31},{20,24},{21,25},{22,26},{23,27},{2... | collective-permute-start | bytes 49160 | tf_op jit(solution)/shard_map/ppermute | solution.py:315
  32.6 3.4 %collective-permute-start.21 = (f32[32,128]{1,0:T(8,128)S(1)}, f32[32,128]{1,0:T(8,128)S(1)}, u32[]{:S(2)}, u32[]{:S(2)}) collective-permute-start(f32[32,128]{1,0:T(8,128)S(1)} %add.11), channel_id=1, source_target_pairs={{16,26},{17,27},{18,24},{19,25},{20,30},{21,31},{22,28},{23,29},{2... | collective-permute-start | bytes 49160 | tf_op jit(solution)/shard_map/ppermute | solution.py:315

commit v4 on v3

--- a/solution.py
+++ b/solution.py
@@ -239,9 +239,9 @@
 
 def ring_pairs(step, move, slabs, blocks):
     pairs = []
+    order = [step - 1, step] + [(step - 2 - i) % slabs for i in range(slabs - 2)]
     for place in range(slabs):
-        source = (step - 1 + place) % slabs
-        target = (source + 1) % slabs
+        source, target = order[place], order[(place + 1) % slabs]
         for c in range(blocks):
             pairs.append((source * blocks + c, target * blocks + (move(c) if place == 0 else c)))
     return pairs

time: 49.6 us -> 47.7 us (0.962)
  blocking collectives: 12.4 us -> 9.42 us
  waiting for transfers between devices: 7.45 us -> 9.41 us
  starting transfers between devices: 22 us -> 21.2 us
    all_to_all x1, blocking collectives: 12.4 us -> 9.42 us  [on_device(): sums = lax.all_to_all(partial, 'trace', 0, 0)]
    ppermute x3, waiting for transfers between devices: 3.27 us -> 5.52 us  [on_device(): swapped = lax.ppermute(small, 'trace', [(c, c ^ 1) for c in range(blocks)])]
    ppermute x18, starting transfers between devices: 15.9 us -> 15.3 us  [send(): return lax.ppermute(x, both_axes, ring_pairs(step, move, slabs, blocks))]
  transfers between devices with their start and end apart: 22 -> 22, of which waited for: 7 -> 11; matrix products, arithmetic and copies ran while one was open for 0% -> 0% of each run, Pallas kernels for 11% -> 11%
where the time goes in v4:
time: 47.7 us; the launch traced here: 47.5 us
  starting transfers between devices  21.2 us (44%)
  blocking collectives  9.42 us (20%)
  waiting for transfers between devices  9.41 us (20%)
  Pallas kernels  6.65 us (14%)
  between operations  0.77 us (2%)
    ppermute x18, starting transfers between devices, send(): return lax.ppermute(x, both_axes, ring_pairs(step, move, slabs, blocks))  15.3 us
    all_to_all x1, blocking collectives, on_device(): sums = lax.all_to_all(partial, 'trace', 0, 0)  9.42 us
    pallas_call x13, Pallas kernels, call(): pl.pallas_call(kernel, out_shape=outs, in_specs=specs, out_specs=[in_vmem...  6.65 us
    ppermute x3, waiting for transfers between devices, on_device(): swapped = lax.ppermute(small, 'trace', [(c, c ^ 1) for c in range(blocks)])  5.52 us
    ppermute x18, waiting for transfers between devices, send(): return lax.ppermute(x, both_axes, ring_pairs(step, move, slabs, blocks))  3.88 us
    ppermute x3, starting transfers between devices, on_device(): swapped = lax.ppermute(small, 'trace', [(c, c ^ 1) for c in range(blocks)])  3.51 us
    ppermute x1, starting transfers between devices, on_device(): lax.ppermute(skeleton.reshape(1, rank), 'slab', [((s + 1) % slabs, s) for...  2.41 us
  transfers between devices with their start and end apart: 22, of which 11 were waited for; matrix products, arithmetic and copies ran while one was open for 0% of the time, Pallas kernels for 11%

profile of v4, /device:TPU:0, one launch (start us, length us, event | category | flops | bytes accessed | tf_op | source)
XLA Modules:
  0.0 47.5 jit_solution(7757682601120511498)
XLA Ops:
  0.0 2.4 %collective-permute-start = (s32[1,64]{1,0:T(1,128)}, s32[1,64]{1,0:T(1,128)S(1)}, u32[]{:S(2)}, u32[]{:S(2)}) collective-permute-start(s32[1,64]{1,0:T(1,128)} %bitcast.26), channel_id=1, source_target_pairs={{8,0},{16,8},{24,16},{0,24},{9,1},{17,9},{25,17},{1,25},{10,2},{18... | collective-permute-start | bytes 776 | tf_op jit(solution)/shard_map/ppermute | solution.py:262
  2.4 2.5 %split_own.1 = (bf16[2,768,768]{2,1,0:T(8,128)(2,1)S(1)}, bf16[2,768,768]{2,1,0:T(8,128)(2,1)S(1)}) custom-call(f32[4,768,768]{2,1,0:T(8,128)} %bitcast.22), custom_call_target="tpu_custom_call" | custom-call | flops 2875000064 | bytes 9225000 | tf_op jit(solution)/shard_map/split_own/pallas_call | solution.py:222
  5.6 0.0 collective-permute-done.skel_ref.refs_0_
  5.6 0.3 first.1
  5.9 0.0 collective-permute-start.3
  5.9 1.5 %collective-permute-start.4 = (f32[32,128]{1,0:T(8,128)S(1)}, f32[32,128]{1,0:T(8,128)S(1)}, u32[]{:S(2)}, u32[]{:S(2)}) collective-permute-start(f32[32,128]{1,0:T(8,128)S(1)} %first.1), channel_id=1, source_target_pairs={{0,1},{1,0},{2,3},{3,2},{4,5},{5,4},{6,7},{7,6},{8,9},{9,8},{10,11... | collective-permute-start | bytes 49160 | tf_op jit(solution)/shard_map/ppermute | solution.py:320
  7.4 0.5 %collective-permute-start.2 = (f32[32,768]{1,0:T(8,128)S(1)}, f32[32,768]{1,0:T(8,128)S(1)}, u32[]{:S(2)}, u32[]{:S(2)}) collective-permute-start(f32[32,768]{1,0:T(8,128)S(1)} %bitcast.15), channel_id=1, source_target_pairs={{0,8},{1,10},{2,9},{3,12},{4,11},{5,14},{6,13},{7,15},{8,24},{9,25... | collective-permute-start | bytes 294920 | tf_op jit(solution)/shard_map/ppermute | solution.py:315
  7.9 0.2 collective-permute-start.1
  8.2 1.5 %collective-permute-done.4 = f32[32,128]{1,0:T(8,128)S(1)} collective-permute-done((f32[32,128]{1,0:T(8,128)S(1)}, f32[32,128]{1,0:T(8,128)S(1)}, u32[]{:S(2)}, u32[]{:S(2)}) %collective-permute-start.4) | collective-permute-done | bytes 16416 | tf_op jit(solution)/shard_map/ppermute | solution.py:320
  9.6 3.3 %collective-permute-start.5 = (f32[32,128]{1,0:T(8,128)S(1)}, f32[32,128]{1,0:T(8,128)S(1)}, u32[]{:S(2)}, u32[]{:S(2)}) collective-permute-start(f32[32,128]{1,0:T(8,128)S(1)} %add.9), channel_id=1, source_target_pairs={{0,14},{1,15},{2,12},{3,13},{4,10},{5,11},{6,8},{7,9},{8,24},{9,25... | collective-permute-start | bytes 49160 | tf_op jit(solution)/shard_map/ppermute | solution.py:315
  13.0 0.0 collective-permute-start.6
  13.0 0.0 collective-permute-done.3.refs_0_
  13.0 0.1 collective-permute-start.7
  13.1 2.9 %split_beside.1 = (bf16[2,2,512,64]{3,2,1,0:T(8,128)(2,1)S(1)}, bf16[2,2,64,768]{3,2,1,0:T(8,128)(2,1)S(1)}, bf16[2,768,768]{2,1,0:T(8,128)(2,1)S(1)}, bf16[2,768,768]{2,1,0:T(8,128)(2,1)S(1)}) custom-call(s32[1,1]{1,0:T(1,128)S(6)} %copy.10.side_ref.refs_0_, f32[2,64,512]{2,1,0:T(8,128)} %bitcast.25, f32[2,64,768]{2,1,0:T(8,128)} %bitcast.24, ...), custom_call_target="tpu_custom_call" | custom-call | flops 2875000064 | bytes 9225000 | tf_op jit(solution)/shard_map/split_beside/pallas_call | solution.py:222
  15.9 0.0 collective-permute-done.2.refs_2_
  15.9 0.0 collective-permute-done.1.refs_1_.refs_3_
  16.0 0.0 collective-permute-done.5.refs_4_
  16.0 0.7 %collective-permute-done.6.refs_5_ = f32[32,128]{1,0:T(8,128)S(1)} collective-permute-done((f32[32,128]{1,0:T(8,128)S(1)}, f32[32,128]{1,0:T(8,128)S(1)}, u32[]{:S(2)}, u32[]{:S(2)}) %collective-permute-start.6) | collective-permute-done | bytes 16416 | tf_op jit(solution)/shard_map/ppermute | solution.py:315
  16.7 0.2 collective-permute-done.7.refs_6_
  16.9 1.3 %collective-permute-start.10 = (f32[32,768]{1,0:T(8,128)S(1)}, f32[32,768]{1,0:T(8,128)S(1)}, u32[]{:S(2)}, u32[]{:S(2)}) collective-permute-start(f32[32,768]{1,0:T(8,128)S(1)} %get-tuple-element.37.refs_1_), channel_id=1, source_target_pairs={{8,16},{9,17},{10,18},{11,19},{12,20},{13,21},{14,22},{15,23},{16,... | collective-permute-start | bytes 294920 | tf_op jit(solution)/shard_map/ppermute | solution.py:315
  18.1 1.0 %collective-permute-start.11 = (f32[32,128]{1,0:T(8,128)S(1)}, f32[32,128]{1,0:T(8,128)S(1)}, u32[]{:S(2)}, u32[]{:S(2)}) collective-permute-start(f32[32,128]{1,0:T(8,128)S(1)} %get-tuple-element.38), channel_id=1, source_target_pairs={{0,1},{1,0},{2,3},{3,2},{4,5},{5,4},{6,7},{7,6},{8,9},{9,8},{10,11... | collective-permute-start | bytes 49160 | tf_op jit(solution)/shard_map/ppermute | solution.py:320
  19.1 0.9 %collective-permute-start.9 = (f32[32,768]{1,0:T(8,128)S(1)}, f32[32,768]{1,0:T(8,128)S(1)}, u32[]{:S(2)}, u32[]{:S(2)}) collective-permute-start(f32[32,768]{1,0:T(8,128)S(1)} %get-tuple-element.37.refs_1_), channel_id=1, source_target_pairs={{8,16},{9,18},{10,17},{11,20},{12,19},{13,22},{14,21},{15,23},{16,... | collective-permute-start | bytes 294920 | tf_op jit(solution)/shard_map/ppermute | solution.py:315
  20.1 0.2 collective-permute-start.8
  20.3 1.6 %collective-permute-done.11 = f32[32,128]{1,0:T(8,128)S(1)} collective-permute-done((f32[32,128]{1,0:T(8,128)S(1)}, f32[32,128]{1,0:T(8,128)S(1)}, u32[]{:S(2)}, u32[]{:S(2)}) %collective-permute-start.11) | collective-permute-done | bytes 16416 | tf_op jit(solution)/shard_map/ppermute | solution.py:320
  21.9 0.0 collective-permute-start.12
  21.9 1.3 %collective-permute-start.13 = (f32[32,128]{1,0:T(8,128)S(1)}, f32[32,128]{1,0:T(8,128)S(1)}, u32[]{:S(2)}, u32[]{:S(2)}) collective-permute-start(f32[32,128]{1,0:T(8,128)S(1)} %add.10), channel_id=1, source_target_pairs={{8,20},{9,21},{10,22},{11,23},{12,16},{13,17},{14,18},{15,19},{16,... | collective-permute-start | bytes 49160 | tf_op jit(solution)/shard_map/ppermute | solution.py:315
  23.2 0.0 collective-permute-done.10.refs_0_
  23.2 3.4 %collective-permute-start.14 = (f32[32,128]{1,0:T(8,128)S(1)}, f32[32,128]{1,0:T(8,128)S(1)}, u32[]{:S(2)}, u32[]{:S(2)}) collective-permute-start(f32[32,128]{1,0:T(8,128)S(1)} %add.10), channel_id=1, source_target_pairs={{8,18},{9,19},{10,16},{11,17},{12,22},{13,23},{14,20},{15,21},{16,... | collective-permute-start | bytes 49160 | tf_op jit(solution)/shard_map/ppermute | solution.py:315
  26.6 0.0 collective-permute-done.9.refs_2_
  26.7 0.2 collective-permute-done.8.refs_1_.refs_3_
  26.9 0.2 collective-permute-done.12.refs_4_
  27.0 0.2 collective-permute-done.13.refs_5_
  27.2 0.9 %collective-permute-done.14.refs_6_ = f32[32,128]{1,0:T(8,128)S(1)} collective-permute-done((f32[32,128]{1,0:T(8,128)S(1)}, f32[32,128]{1,0:T(8,128)S(1)}, u32[]{:S(2)}, u32[]{:S(2)}) %collective-permute-start.14) | collective-permute-done | bytes 16416 | tf_op jit(solution)/shard_map/ppermute | solution.py:315
  28.1 1.5 %collective-permute-start.17 = (f32[32,768]{1,0:T(8,128)S(1)}, f32[32,768]{1,0:T(8,128)S(1)}, u32[]{:S(2)}, u32[]{:S(2)}) collective-permute-start(f32[32,768]{1,0:T(8,128)S(1)} %get-tuple-element.39.refs_0_), channel_id=1, source_target_pairs={{16,24},{17,25},{18,26},{19,27},{20,28},{21,29},{22,30},{23,31},{2... | collective-permute-start | bytes 294920 | tf_op jit(solution)/shard_map/ppermute | solution.py:315
  29.6 1.0 %collective-permute-start.18 = (f32[32,128]{1,0:T(8,128)S(1)}, f32[32,128]{1,0:T(8,128)S(1)}, u32[]{:S(2)}, u32[]{:S(2)}) collective-permute-start(f32[32,128]{1,0:T(8,128)S(1)} %get-tuple-element.40), channel_id=1, source_target_pairs={{0,1},{1,0},{2,3},{3,2},{4,5},{5,4},{6,7},{7,6},{8,9},{9,8},{10,11... | collective-permute-start | bytes 49160 | tf_op jit(solution)/shard_map/ppermute | solution.py:320
  30.6 0.2 collective-permute-start.16
  30.8 0.1 collective-permute-start.15
  30.9 2.5 %collective-permute-done.18 = f32[32,128]{1,0:T(8,128)S(1)} collective-permute-done((f32[32,128]{1,0:T(8,128)S(1)}, f32[32,128]{1,0:T(8,128)S(1)}, u32[]{:S(2)}, u32[]{:S(2)}) %collective-permute-start.18) | collective-permute-done | bytes 16416 | tf_op jit(solution)/shard_map/ppermute | solution.py:320
  33.4 0.6 %collective-permute-start.19 = (f32[32,128]{1,0:T(8,128)S(1)}, f32[32,128]{1,0:T(8,128)S(1)}, u32[]{:S(2)}, u32[]{:S(2)}) collective-permute-start(f32[32,128]{1,0:T(8,128)S(1)} %add.11), channel_id=1, source_target_pairs={{16,30},{17,31},{18,28},{19,29},{20,26},{21,27},{22,24},{23,25},{2... | collective-permute-start | bytes 49160 | tf_op jit(solution)/shard_map/ppermute | solution.py:315
  34.0 1.6 %collective-permute-start.20 = (f32[32,128]{1,0:T(8,128)S(1)}, f32[32,128]{1,0:T(8,128)S(1)}, u32[]{:S(2)}, u32[]{:S(2)}) collective-permute-start(f32[32,128]{1,0:T(8,128)S(1)} %add.11), channel_id=1, source_target_pairs={{16,28},{17,29},{18,30},{19,31},{20,24},{21,25},{22,26},{23,27},{2... | collective-permute-start | bytes 49160 | tf_op jit(solution)/shard_map/ppermute | solution.py:315
  35.5 0.0 collective-permute-done.17.refs_0_
  35.5 0.0 collective-permute-start.21
  35.6 0.0 collective-permute-done.16.refs_2_
  35.6 1.4 %collective-permute-done.20.refs_4_ = f32[32,128]{1,0:T(8,128)S(1)} collective-permute-done((f32[32,128]{1,0:T(8,128)S(1)}, f32[32,128]{1,0:T(8,128)S(1)}, u32[]{:S(2)}, u32[]{:S(2)}) %collective-permute-start.20) | collective-permute-done | bytes 16416 | tf_op jit(solution)/shard_map/ppermute | solution.py:315
  37.0 0.2 collective-permute-done.21.refs_5_
  37.1 0.2 last.1
  37.3 9.4 %all_to_all.11 = f32[8,1,16]{2,1,0:T(1,128)S(1)} all-to-all(f32[8,1,16]{2,1,0:T(1,128)S(1)} %bitcast.21), channel_id=1, replica_groups=mesh['slab'=4,'trace'=8] {'trace'}, dimensions={0} | all-to-all | bytes 1024 | tf_op jit(solution)/shard_map/all_to_all | solution.py:366
  46.7 0.8 %norm.1 = f32[2,16,768]{2,1,0:T(8,128)} custom-call(f32[32,768]{1,0:T(8,128)S(1)} %get-tuple-element.41.refs_0_, f32[8,16]{1,0:T(8,128)S(1)} %bitcast.20), custom_call_target="tpu_custom_call" | custom-call | tf_op jit(solution)/shard_map/norm/pallas_call | solution.py:222
  (18 shorter events, 0.1 us)
Async XLA Ops:
  0.0 5.6 %collective-permute-start = (s32[1,64]{1,0:T(1,128)}, s32[1,64]{1,0:T(1,128)S(1)}, u32[]{:S(2)}, u32[]{:S(2)}) collective-permute-start(s32[1,64]{1,0:T(1,128)} %bitcast.26), channel_id=1, source_target_pairs={{8,0},{16,8},{24,16},{0,24},{9,1},{17,9},{25,17},{1,25},{10,2},{18... | collective-permute-start | bytes 776 | tf_op jit(solution)/shard_map/ppermute | solution.py:262
  2.4 3.2 %copy-start = (f32[1,2,1,16,768]{4,3,2,1,0:T(8,128)S(1)}, f32[1,2,1,16,768]{4,3,2,1,0:T(8,128)}, u32[]{:S(2)}) copy-start(f32[1,2,1,16,768]{4,3,2,1,0:T(8,128)} %param.11) | copy-start | bytes 294916
  5.9 7.1 %collective-permute-start.3 = (f32[32,768]{1,0:T(8,128)S(1)}, f32[32,768]{1,0:T(8,128)S(1)}, u32[]{:S(2)}, u32[]{:S(2)}) collective-permute-start(f32[32,768]{1,0:T(8,128)S(1)} %bitcast.13), channel_id=1, source_target_pairs={{0,8},{1,9},{2,10},{3,11},{4,12},{5,13},{6,14},{7,15},{8,24},{9,25... | collective-permute-start | bytes 294920 | tf_op jit(solution)/shard_map/ppermute | solution.py:315
  5.9 3.8 %collective-permute-start.4 = (f32[32,128]{1,0:T(8,128)S(1)}, f32[32,128]{1,0:T(8,128)S(1)}, u32[]{:S(2)}, u32[]{:S(2)}) collective-permute-start(f32[32,128]{1,0:T(8,128)S(1)} %first.1), channel_id=1, source_target_pairs={{0,1},{1,0},{2,3},{3,2},{4,5},{5,4},{6,7},{7,6},{8,9},{9,8},{10,11... | collective-permute-start | bytes 49160 | tf_op jit(solution)/shard_map/ppermute | solution.py:320
  7.4 8.5 %collective-permute-start.2 = (f32[32,768]{1,0:T(8,128)S(1)}, f32[32,768]{1,0:T(8,128)S(1)}, u32[]{:S(2)}, u32[]{:S(2)}) collective-permute-start(f32[32,768]{1,0:T(8,128)S(1)} %bitcast.15), channel_id=1, source_target_pairs={{0,8},{1,10},{2,9},{3,12},{4,11},{5,14},{6,13},{7,15},{8,24},{9,25... | collective-permute-start | bytes 294920 | tf_op jit(solution)/shard_map/ppermute | solution.py:315
  7.9 8.0 %collective-permute-start.1 = (f32[32,896]{1,0:T(8,128)S(1)}, f32[32,896]{1,0:T(8,128)S(1)}, u32[]{:S(2)}, u32[]{:S(2)}) collective-permute-start(f32[32,896]{1,0:T(8,128)S(1)} %pad_maximum_fusion), channel_id=1, source_target_pairs={{0,9},{1,8},{2,11},{3,10},{4,13},{5,12},{6,15},{7,14},{8,24},{9,25... | collective-permute-start | bytes 344072 | tf_op jit(solution)/shard_map/ppermute | solution.py:315
  9.6 6.3 %collective-permute-start.5 = (f32[32,128]{1,0:T(8,128)S(1)}, f32[32,128]{1,0:T(8,128)S(1)}, u32[]{:S(2)}, u32[]{:S(2)}) collective-permute-start(f32[32,128]{1,0:T(8,128)S(1)} %add.9), channel_id=1, source_target_pairs={{0,14},{1,15},{2,12},{3,13},{4,10},{5,11},{6,8},{7,9},{8,24},{9,25... | collective-permute-start | bytes 49160 | tf_op jit(solution)/shard_map/ppermute | solution.py:315
  13.0 3.7 %collective-permute-start.6 = (f32[32,128]{1,0:T(8,128)S(1)}, f32[32,128]{1,0:T(8,128)S(1)}, u32[]{:S(2)}, u32[]{:S(2)}) collective-permute-start(f32[32,128]{1,0:T(8,128)S(1)} %add.9), channel_id=1, source_target_pairs={{0,12},{1,13},{2,14},{3,15},{4,8},{5,9},{6,10},{7,11},{8,24},{9,25... | collective-permute-start | bytes 49160 | tf_op jit(solution)/shard_map/ppermute | solution.py:315
  13.0 3.9 %collective-permute-start.7 = (f32[32,128]{1,0:T(8,128)S(1)}, f32[32,128]{1,0:T(8,128)S(1)}, u32[]{:S(2)}, u32[]{:S(2)}) collective-permute-start(f32[32,128]{1,0:T(8,128)S(1)} %add.9), channel_id=1, source_target_pairs={{0,10},{1,11},{2,8},{3,9},{4,14},{5,15},{6,12},{7,13},{8,24},{9,25... | collective-permute-start | bytes 49160 | tf_op jit(solution)/shard_map/ppermute | solution.py:315
  16.9 6.4 %collective-permute-start.10 = (f32[32,768]{1,0:T(8,128)S(1)}, f32[32,768]{1,0:T(8,128)S(1)}, u32[]{:S(2)}, u32[]{:S(2)}) collective-permute-start(f32[32,768]{1,0:T(8,128)S(1)} %get-tuple-element.37.refs_1_), channel_id=1, source_target_pairs={{8,16},{9,17},{10,18},{11,19},{12,20},{13,21},{14,22},{15,23},{16,... | collective-permute-start | bytes 294920 | tf_op jit(solution)/shard_map/ppermute | solution.py:315
  18.1 3.7 %collective-permute-start.11 = (f32[32,128]{1,0:T(8,128)S(1)}, f32[32,128]{1,0:T(8,128)S(1)}, u32[]{:S(2)}, u32[]{:S(2)}) collective-permute-start(f32[32,128]{1,0:T(8,128)S(1)} %get-tuple-element.38), channel_id=1, source_target_pairs={{0,1},{1,0},{2,3},{3,2},{4,5},{5,4},{6,7},{7,6},{8,9},{9,8},{10,11... | collective-permute-start | bytes 49160 | tf_op jit(solution)/shard_map/ppermute | solution.py:320
  19.1 7.5 %collective-permute-start.9 = (f32[32,768]{1,0:T(8,128)S(1)}, f32[32,768]{1,0:T(8,128)S(1)}, u32[]{:S(2)}, u32[]{:S(2)}) collective-permute-start(f32[32,768]{1,0:T(8,128)S(1)} %get-tuple-element.37.refs_1_), channel_id=1, source_target_pairs={{8,16},{9,18},{10,17},{11,20},{12,19},{13,22},{14,21},{15,23},{16,... | collective-permute-start | bytes 294920 | tf_op jit(solution)/shard_map/ppermute | solution.py:315
  20.1 6.8 %collective-permute-start.8 = (f32[32,896]{1,0:T(8,128)S(1)}, f32[32,896]{1,0:T(8,128)S(1)}, u32[]{:S(2)}, u32[]{:S(2)}) collective-permute-start(f32[32,896]{1,0:T(8,128)S(1)} %pad_maximum_fusion.1), channel_id=1, source_target_pairs={{8,17},{9,16},{10,19},{11,18},{12,21},{13,20},{14,23},{15,22},{16,... | collective-permute-start | bytes 344072 | tf_op jit(solution)/shard_map/ppermute | solution.py:315
  21.9 5.1 %collective-permute-start.12 = (f32[32,128]{1,0:T(8,128)S(1)}, f32[32,128]{1,0:T(8,128)S(1)}, u32[]{:S(2)}, u32[]{:S(2)}) collective-permute-start(f32[32,128]{1,0:T(8,128)S(1)} %add.10), channel_id=1, source_target_pairs={{8,22},{9,23},{10,20},{11,21},{12,18},{13,19},{14,16},{15,17},{16,... | collective-permute-start | bytes 49160 | tf_op jit(solution)/shard_map/ppermute | solution.py:315
  21.9 5.3 %collective-permute-start.13 = (f32[32,128]{1,0:T(8,128)S(1)}, f32[32,128]{1,0:T(8,128)S(1)}, u32[]{:S(2)}, u32[]{:S(2)}) collective-permute-start(f32[32,128]{1,0:T(8,128)S(1)} %add.10), channel_id=1, source_target_pairs={{8,20},{9,21},{10,22},{11,23},{12,16},{13,17},{14,18},{15,19},{16,... | collective-permute-start | bytes 49160 | tf_op jit(solution)/shard_map/ppermute | solution.py:315
  23.2 4.9 %collective-permute-start.14 = (f32[32,128]{1,0:T(8,128)S(1)}, f32[32,128]{1,0:T(8,128)S(1)}, u32[]{:S(2)}, u32[]{:S(2)}) collective-permute-start(f32[32,128]{1,0:T(8,128)S(1)} %add.10), channel_id=1, source_target_pairs={{8,18},{9,19},{10,16},{11,17},{12,22},{13,23},{14,20},{15,21},{16,... | collective-permute-start | bytes 49160 | tf_op jit(solution)/shard_map/ppermute | solution.py:315
  28.1 7.4 %collective-permute-start.17 = (f32[32,768]{1,0:T(8,128)S(1)}, f32[32,768]{1,0:T(8,128)S(1)}, u32[]{:S(2)}, u32[]{:S(2)}) collective-permute-start(f32[32,768]{1,0:T(8,128)S(1)} %get-tuple-element.39.refs_0_), channel_id=1, source_target_pairs={{16,24},{17,25},{18,26},{19,27},{20,28},{21,29},{22,30},{23,31},{2... | collective-permute-start | bytes 294920 | tf_op jit(solution)/shard_map/ppermute | solution.py:315
  29.6 3.7 %collective-permute-start.18 = (f32[32,128]{1,0:T(8,128)S(1)}, f32[32,128]{1,0:T(8,128)S(1)}, u32[]{:S(2)}, u32[]{:S(2)}) collective-permute-start(f32[32,128]{1,0:T(8,128)S(1)} %get-tuple-element.40), channel_id=1, source_target_pairs={{0,1},{1,0},{2,3},{3,2},{4,5},{5,4},{6,7},{7,6},{8,9},{9,8},{10,11... | collective-permute-start | bytes 49160 | tf_op jit(solution)/shard_map/ppermute | solution.py:320
  30.6 5.0 %collective-permute-start.16 = (f32[32,768]{1,0:T(8,128)S(1)}, f32[32,768]{1,0:T(8,128)S(1)}, u32[]{:S(2)}, u32[]{:S(2)}) collective-permute-start(f32[32,768]{1,0:T(8,128)S(1)} %get-tuple-element.39.refs_0_), channel_id=1, source_target_pairs={{16,24},{17,26},{18,25},{19,28},{20,27},{21,30},{22,29},{23,31},{2... | collective-permute-start | bytes 294920 | tf_op jit(solution)/shard_map/ppermute | solution.py:315
  30.8 4.7 %collective-permute-start.15 = (f32[32,896]{1,0:T(8,128)S(1)}, f32[32,896]{1,0:T(8,128)S(1)}, u32[]{:S(2)}, u32[]{:S(2)}) collective-permute-start(f32[32,896]{1,0:T(8,128)S(1)} %pad_maximum_fusion.2), channel_id=1, source_target_pairs={{16,25},{17,24},{18,27},{19,26},{20,29},{21,28},{22,31},{23,30},{2... | collective-permute-start | bytes 344072 | tf_op jit(solution)/shard_map/ppermute | solution.py:315
  33.4 2.2 %collective-permute-start.19 = (f32[32,128]{1,0:T(8,128)S(1)}, f32[32,128]{1,0:T(8,128)S(1)}, u32[]{:S(2)}, u32[]{:S(2)}) collective-permute-start(f32[32,128]{1,0:T(8,128)S(1)} %add.11), channel_id=1, source_target_pairs={{16,30},{17,31},{18,28},{19,29},{20,26},{21,27},{22,24},{23,25},{2... | collective-permute-start | bytes 49160 | tf_op jit(solution)/shard_map/ppermute | solution.py:315
  34.0 3.0 %collective-permute-start.20 = (f32[32,128]{1,0:T(8,128)S(1)}, f32[32,128]{1,0:T(8,128)S(1)}, u32[]{:S(2)}, u32[]{:S(2)}) collective-permute-start(f32[32,128]{1,0:T(8,128)S(1)} %add.11), channel_id=1, source_target_pairs={{16,28},{17,29},{18,30},{19,31},{20,24},{21,25},{22,26},{23,27},{2... | collective-permute-start | bytes 49160 | tf_op jit(solution)/shard_map/ppermute | solution.py:315
  35.5 1.6 %collective-permute-start.21 = (f32[32,128]{1,0:T(8,128)S(1)}, f32[32,128]{1,0:T(8,128)S(1)}, u32[]{:S(2)}, u32[]{:S(2)}) collective-permute-start(f32[32,128]{1,0:T(8,128)S(1)} %add.11), channel_id=1, source_target_pairs={{16,26},{17,27},{18,24},{19,25},{20,30},{21,31},{22,28},{23,29},{2... | collective-permute-start | bytes 49160 | tf_op jit(solution)/shard_map/ppermute | solution.py:315

commit v5 on v4

--- a/solution.py
+++ b/solution.py
@@ -247,6 +247,16 @@
     return pairs
 
 
+def swap_pairs(step, move, slabs, blocks):
+    rest = [(step + 1 + i) % slabs for i in range(slabs - 2)]
+    pairs = []
+    for place, (one, two) in enumerate([(step - 1, step), *zip(rest[::2], rest[1::2])]):
+        for c in range(blocks):
+            to = move(c) if place == 0 else c
+            pairs += [(one * blocks + c, two * blocks + to), (two * blocks + to, one * blocks + c)]
+    return pairs
+
+
 def on_device(near_tiles, near_side, skeleton, far_coupling, far_basis, sources):
     slabs = lax.axis_size("slab")
     blocks = lax.axis_size("trace")
@@ -314,17 +324,20 @@
         def send(x, move):
             return lax.ppermute(x, both_axes, ring_pairs(step, move, slabs, blocks))
 
+        def trade(x, move):
+            return lax.ppermute(x, both_axes, swap_pairs(step, move, slabs, blocks))
+
         def send_pair(x, j):
             return send(x, lambda c: c ^ (2 * j))
 
         swapped = lax.ppermute(small, "trace", [(c, c ^ 1) for c in range(blocks)])
         pair = small + swapped
-        own = send(state, lambda c: c)
+        own = (trade if step % 2 else send)(state, lambda c: c)
         if step == 1:
             own, planes = lax.optimization_barrier((own, planes))
             coef, base, beside_halves = split_rest(planes)
         wide = jnp.concatenate([state, small], axis=1)
-        mate = send(wide, lambda c: c ^ 1)
+        mate = (trade if step % 2 else send)(wide, lambda c: c ^ 1)
         other = send(state, lambda c: across(c, blocks))
         pairs = [send_pair(pair, way) for way in pair_ways(blocks // 2)[1:]]
         near = call(

time: 47.7 us -> 47.3 us (level)
  waiting for transfers between devices: 9.41 us -> 7.29 us
  starting transfers between devices: 21.2 us -> 23.1 us
    ppermute x3, waiting for transfers between devices: 5.52 us -> 3.59 us  [on_device(): swapped = lax.ppermute(small, 'trace', [(c, c ^ 1) for c in range(blocks)])]
    ppermute x18 -> x14, starting transfers between devices: 15.3 us -> 16.3 us  [send(): return lax.ppermute(x, both_axes, ring_pairs(step, move, slabs, blocks))]
    ppermute x0 -> x4, starting transfers between devices: none -> 0.57 us  [trade(): return lax.ppermute(x, both_axes, swap_pairs(step, move, slabs, blocks))]
    ppermute x18 -> x14, waiting for transfers between devices: 3.88 us -> 3.68 us  [send(): return lax.ppermute(x, both_axes, ring_pairs(step, move, slabs, blocks))]
  transfers between devices with their start and end apart: 22 -> 22, of which waited for: 11 -> 12; matrix products, arithmetic and copies ran while one was open for 0% -> 0% of each run, Pallas kernels for 11% -> 11%
where the time goes in v5:
time: 47.3 us; the launch traced here: 47.1 us
  starting transfers between devices  23.1 us (49%)
  blocking collectives  9.28 us (20%)
  waiting for transfers between devices  7.29 us (15%)
  Pallas kernels  6.64 us (14%)
  between operations  0.77 us (2%)
    ppermute x14, starting transfers between devices, send(): return lax.ppermute(x, both_axes, ring_pairs(step, move, slabs, blocks))  16.3 us
    all_to_all x1, blocking collectives, on_device(): sums = lax.all_to_all(partial, 'trace', 0, 0)  9.28 us
    pallas_call x13, Pallas kernels, call(): pl.pallas_call(kernel, out_shape=outs, in_specs=specs, out_specs=[in_vmem...  6.64 us
    ppermute x3, starting transfers between devices, on_device(): swapped = lax.ppermute(small, 'trace', [(c, c ^ 1) for c in range(blocks)])  3.75 us
    ppermute x14, waiting for transfers between devices, send(): return lax.ppermute(x, both_axes, ring_pairs(step, move, slabs, blocks))  3.68 us
    ppermute x3, waiting for transfers between devices, on_device(): swapped = lax.ppermute(small, 'trace', [(c, c ^ 1) for c in range(blocks)])  3.59 us
    ppermute x1, starting transfers between devices, on_device(): lax.ppermute(skeleton.reshape(1, rank), 'slab', [((s + 1) % slabs, s) for...  2.41 us
  transfers between devices with their start and end apart: 22, of which 12 were waited for; matrix products, arithmetic and copies ran while one was open for 0% of the time, Pallas kernels for 11%

profile of v5, /device:TPU:0, one launch (start us, length us, event | category | flops | bytes accessed | tf_op | source)
XLA Modules:
  0.0 47.1 jit_solution(9195173209948169951)
XLA Ops:
  0.0 2.4 %collective-permute-start = (s32[1,64]{1,0:T(1,128)}, s32[1,64]{1,0:T(1,128)S(1)}, u32[]{:S(2)}, u32[]{:S(2)}) collective-permute-start(s32[1,64]{1,0:T(1,128)} %bitcast.26), channel_id=1, source_target_pairs={{8,0},{16,8},{24,16},{0,24},{9,1},{17,9},{25,17},{1,25},{10,2},{18... | collective-permute-start | bytes 776 | tf_op jit(solution)/shard_map/ppermute | solution.py:272
  2.4 2.5 %split_own.1 = (bf16[2,768,768]{2,1,0:T(8,128)(2,1)S(1)}, bf16[2,768,768]{2,1,0:T(8,128)(2,1)S(1)}) custom-call(f32[4,768,768]{2,1,0:T(8,128)} %bitcast.22), custom_call_target="tpu_custom_call" | custom-call | flops 2875000064 | bytes 9225000 | tf_op jit(solution)/shard_map/split_own/pallas_call | solution.py:222
  5.6 0.0 collective-permute-done.skel_ref.refs_0_
  5.6 0.3 first.1
  5.9 0.0 collective-permute-start.3
  5.9 1.6 %collective-permute-start.4 = (f32[32,128]{1,0:T(8,128)S(1)}, f32[32,128]{1,0:T(8,128)S(1)}, u32[]{:S(2)}, u32[]{:S(2)}) collective-permute-start(f32[32,128]{1,0:T(8,128)S(1)} %first.1), channel_id=1, source_target_pairs={{0,1},{1,0},{2,3},{3,2},{4,5},{5,4},{6,7},{7,6},{8,9},{9,8},{10,11... | collective-permute-start | bytes 49160 | tf_op jit(solution)/shard_map/ppermute | solution.py:333
  7.4 0.2 collective-permute-start.2
  7.7 0.5 %collective-permute-start.1 = (f32[32,896]{1,0:T(8,128)S(1)}, f32[32,896]{1,0:T(8,128)S(1)}, u32[]{:S(2)}, u32[]{:S(2)}) collective-permute-start(f32[32,896]{1,0:T(8,128)S(1)} %pad_maximum_fusion), channel_id=1, source_target_pairs={{0,9},{9,0},{1,8},{8,1},{2,11},{11,2},{3,10},{10,3},{4,13},{13,4},... | collective-permute-start | bytes 344072 | tf_op jit(solution)/shard_map/ppermute | solution.py:328
  8.2 1.5 %collective-permute-done.4 = f32[32,128]{1,0:T(8,128)S(1)} collective-permute-done((f32[32,128]{1,0:T(8,128)S(1)}, f32[32,128]{1,0:T(8,128)S(1)}, u32[]{:S(2)}, u32[]{:S(2)}) %collective-permute-start.4) | collective-permute-done | bytes 16416 | tf_op jit(solution)/shard_map/ppermute | solution.py:333
  9.7 2.5 %collective-permute-start.5 = (f32[32,128]{1,0:T(8,128)S(1)}, f32[32,128]{1,0:T(8,128)S(1)}, u32[]{:S(2)}, u32[]{:S(2)}) collective-permute-start(f32[32,128]{1,0:T(8,128)S(1)} %add.9), channel_id=1, source_target_pairs={{0,14},{1,15},{2,12},{3,13},{4,10},{5,11},{6,8},{7,9},{8,24},{9,25... | collective-permute-start | bytes 49160 | tf_op jit(solution)/shard_map/ppermute | solution.py:325
  12.2 0.6 %collective-permute-start.6 = (f32[32,128]{1,0:T(8,128)S(1)}, f32[32,128]{1,0:T(8,128)S(1)}, u32[]{:S(2)}, u32[]{:S(2)}) collective-permute-start(f32[32,128]{1,0:T(8,128)S(1)} %add.9), channel_id=1, source_target_pairs={{0,12},{1,13},{2,14},{3,15},{4,8},{5,9},{6,10},{7,11},{8,24},{9,25... | collective-permute-start | bytes 49160 | tf_op jit(solution)/shard_map/ppermute | solution.py:325
  12.8 0.0 collective-permute-done.3.refs_0_
  12.8 0.0 collective-permute-start.7
  12.8 2.9 %split_beside.1 = (bf16[2,2,512,64]{3,2,1,0:T(8,128)(2,1)S(1)}, bf16[2,2,64,768]{3,2,1,0:T(8,128)(2,1)S(1)}, bf16[2,768,768]{2,1,0:T(8,128)(2,1)S(1)}, bf16[2,768,768]{2,1,0:T(8,128)(2,1)S(1)}) custom-call(s32[1,1]{1,0:T(1,128)S(6)} %copy.10.side_ref.refs_0_, f32[2,64,512]{2,1,0:T(8,128)} %bitcast.25, f32[2,64,768]{2,1,0:T(8,128)} %bitcast.24, ...), custom_call_target="tpu_custom_call" | custom-call | flops 2875000064 | bytes 9225000 | tf_op jit(solution)/shard_map/split_beside/pallas_call | solution.py:222
  15.7 0.0 collective-permute-done.2.refs_2_
  15.7 0.0 collective-permute-done.1.refs_1_.refs_3_
  15.7 0.0 collective-permute-done.5.refs_4_
  15.7 0.2 collective-permute-done.6.refs_5_
  15.9 0.6 %collective-permute-done.7.refs_6_ = f32[32,128]{1,0:T(8,128)S(1)} collective-permute-done((f32[32,128]{1,0:T(8,128)S(1)}, f32[32,128]{1,0:T(8,128)S(1)}, u32[]{:S(2)}, u32[]{:S(2)}) %collective-permute-start.7) | collective-permute-done | bytes 16416 | tf_op jit(solution)/shard_map/ppermute | solution.py:325
  16.5 0.8 %collective-permute-start.10 = (f32[32,768]{1,0:T(8,128)S(1)}, f32[32,768]{1,0:T(8,128)S(1)}, u32[]{:S(2)}, u32[]{:S(2)}) collective-permute-start(f32[32,768]{1,0:T(8,128)S(1)} %get-tuple-element.37.refs_1_), channel_id=1, source_target_pairs={{8,16},{9,17},{10,18},{11,19},{12,20},{13,21},{14,22},{15,23},{16,... | collective-permute-start | bytes 294920 | tf_op jit(solution)/shard_map/ppermute | solution.py:325
  17.4 1.5 %collective-permute-start.11 = (f32[32,128]{1,0:T(8,128)S(1)}, f32[32,128]{1,0:T(8,128)S(1)}, u32[]{:S(2)}, u32[]{:S(2)}) collective-permute-start(f32[32,128]{1,0:T(8,128)S(1)} %get-tuple-element.38), channel_id=1, source_target_pairs={{0,1},{1,0},{2,3},{3,2},{4,5},{5,4},{6,7},{7,6},{8,9},{9,8},{10,11... | collective-permute-start | bytes 49160 | tf_op jit(solution)/shard_map/ppermute | solution.py:333
  18.9 1.2 %collective-permute-start.9 = (f32[32,768]{1,0:T(8,128)S(1)}, f32[32,768]{1,0:T(8,128)S(1)}, u32[]{:S(2)}, u32[]{:S(2)}) collective-permute-start(f32[32,768]{1,0:T(8,128)S(1)} %get-tuple-element.37.refs_1_), channel_id=1, source_target_pairs={{8,16},{9,18},{10,17},{11,20},{12,19},{13,22},{14,21},{15,23},{16,... | collective-permute-start | bytes 294920 | tf_op jit(solution)/shard_map/ppermute | solution.py:325
  20.1 0.1 collective-permute-start.8
  20.1 1.0 %collective-permute-done.11 = f32[32,128]{1,0:T(8,128)S(1)} collective-permute-done((f32[32,128]{1,0:T(8,128)S(1)}, f32[32,128]{1,0:T(8,128)S(1)}, u32[]{:S(2)}, u32[]{:S(2)}) %collective-permute-start.11) | collective-permute-done | bytes 16416 | tf_op jit(solution)/shard_map/ppermute | solution.py:333
  21.1 0.5 %collective-permute-start.12 = (f32[32,128]{1,0:T(8,128)S(1)}, f32[32,128]{1,0:T(8,128)S(1)}, u32[]{:S(2)}, u32[]{:S(2)}) collective-permute-start(f32[32,128]{1,0:T(8,128)S(1)} %add.10), channel_id=1, source_target_pairs={{8,22},{9,23},{10,20},{11,21},{12,18},{13,19},{14,16},{15,17},{16,... | collective-permute-start | bytes 49160 | tf_op jit(solution)/shard_map/ppermute | solution.py:325
  21.7 0.8 %collective-permute-start.13 = (f32[32,128]{1,0:T(8,128)S(1)}, f32[32,128]{1,0:T(8,128)S(1)}, u32[]{:S(2)}, u32[]{:S(2)}) collective-permute-start(f32[32,128]{1,0:T(8,128)S(1)} %add.10), channel_id=1, source_target_pairs={{8,20},{9,21},{10,22},{11,23},{12,16},{13,17},{14,18},{15,19},{16,... | collective-permute-start | bytes 49160 | tf_op jit(solution)/shard_map/ppermute | solution.py:325
  22.5 0.0 collective-permute-done.10.refs_0_
  22.5 4.2 %collective-permute-start.14 = (f32[32,128]{1,0:T(8,128)S(1)}, f32[32,128]{1,0:T(8,128)S(1)}, u32[]{:S(2)}, u32[]{:S(2)}) collective-permute-start(f32[32,128]{1,0:T(8,128)S(1)} %add.10), channel_id=1, source_target_pairs={{8,18},{9,19},{10,16},{11,17},{12,22},{13,23},{14,20},{15,21},{16,... | collective-permute-start | bytes 49160 | tf_op jit(solution)/shard_map/ppermute | solution.py:325
  26.7 0.0 collective-permute-done.9.refs_2_
  26.7 0.2 collective-permute-done.8.refs_1_.refs_3_
  26.9 0.2 collective-permute-done.12.refs_4_
  27.0 0.2 collective-permute-done.13.refs_5_
  27.2 0.9 %collective-permute-done.14.refs_6_ = f32[32,128]{1,0:T(8,128)S(1)} collective-permute-done((f32[32,128]{1,0:T(8,128)S(1)}, f32[32,128]{1,0:T(8,128)S(1)}, u32[]{:S(2)}, u32[]{:S(2)}) %collective-permute-start.14) | collective-permute-done | bytes 16416 | tf_op jit(solution)/shard_map/ppermute | solution.py:325
  28.1 0.1 collective-permute-start.17
  28.2 0.7 %collective-permute-start.18 = (f32[32,128]{1,0:T(8,128)S(1)}, f32[32,128]{1,0:T(8,128)S(1)}, u32[]{:S(2)}, u32[]{:S(2)}) collective-permute-start(f32[32,128]{1,0:T(8,128)S(1)} %get-tuple-element.40), channel_id=1, source_target_pairs={{0,1},{1,0},{2,3},{3,2},{4,5},{5,4},{6,7},{7,6},{8,9},{9,8},{10,11... | collective-permute-start | bytes 49160 | tf_op jit(solution)/shard_map/ppermute | solution.py:333
  28.9 2.0 %collective-permute-start.16 = (f32[32,768]{1,0:T(8,128)S(1)}, f32[32,768]{1,0:T(8,128)S(1)}, u32[]{:S(2)}, u32[]{:S(2)}) collective-permute-start(f32[32,768]{1,0:T(8,128)S(1)} %get-tuple-element.39.refs_0_), channel_id=1, source_target_pairs={{16,24},{17,26},{18,25},{19,28},{20,27},{21,30},{22,29},{23,31},{2... | collective-permute-start | bytes 294920 | tf_op jit(solution)/shard_map/ppermute | solution.py:325
  30.9 0.0 collective-permute-start.15
  30.9 1.1 %collective-permute-done.18 = f32[32,128]{1,0:T(8,128)S(1)} collective-permute-done((f32[32,128]{1,0:T(8,128)S(1)}, f32[32,128]{1,0:T(8,128)S(1)}, u32[]{:S(2)}, u32[]{:S(2)}) %collective-permute-start.18) | collective-permute-done | bytes 16416 | tf_op jit(solution)/shard_map/ppermute | solution.py:333
  32.0 2.1 %collective-permute-start.19 = (f32[32,128]{1,0:T(8,128)S(1)}, f32[32,128]{1,0:T(8,128)S(1)}, u32[]{:S(2)}, u32[]{:S(2)}) collective-permute-start(f32[32,128]{1,0:T(8,128)S(1)} %add.11), channel_id=1, source_target_pairs={{16,30},{17,31},{18,28},{19,29},{20,26},{21,27},{22,24},{23,25},{2... | collective-permute-start | bytes 49160 | tf_op jit(solution)/shard_map/ppermute | solution.py:325
  34.1 1.0 %collective-permute-start.20 = (f32[32,128]{1,0:T(8,128)S(1)}, f32[32,128]{1,0:T(8,128)S(1)}, u32[]{:S(2)}, u32[]{:S(2)}) collective-permute-start(f32[32,128]{1,0:T(8,128)S(1)} %add.11), channel_id=1, source_target_pairs={{16,28},{17,29},{18,30},{19,31},{20,24},{21,25},{22,26},{23,27},{2... | collective-permute-start | bytes 49160 | tf_op jit(solution)/shard_map/ppermute | solution.py:325
  35.1 0.0 collective-permute-done.17.refs_0_
  35.1 0.3 collective-permute-start.21
  35.4 0.1 collective-permute-done.19.refs_3_
  35.5 1.0 %collective-permute-done.20.refs_4_ = f32[32,128]{1,0:T(8,128)S(1)} collective-permute-done((f32[32,128]{1,0:T(8,128)S(1)}, f32[32,128]{1,0:T(8,128)S(1)}, u32[]{:S(2)}, u32[]{:S(2)}) %collective-permute-start.20) | collective-permute-done | bytes 16416 | tf_op jit(solution)/shard_map/ppermute | solution.py:325
  36.5 0.3 collective-permute-done.21.refs_5_
  36.8 0.2 last.1
  37.0 9.3 %all_to_all.11 = f32[8,1,16]{2,1,0:T(1,128)S(1)} all-to-all(f32[8,1,16]{2,1,0:T(1,128)S(1)} %bitcast.21), channel_id=1, replica_groups=mesh['slab'=4,'trace'=8] {'trace'}, dimensions={0} | all-to-all | bytes 1024 | tf_op jit(solution)/shard_map/all_to_all | solution.py:379
  46.3 0.8 %norm.1 = f32[2,16,768]{2,1,0:T(8,128)} custom-call(f32[32,768]{1,0:T(8,128)S(1)} %get-tuple-element.41.refs_0_, f32[8,16]{1,0:T(8,128)S(1)} %bitcast.20), custom_call_target="tpu_custom_call" | custom-call | tf_op jit(solution)/shard_map/norm/pallas_call | solution.py:222
  (18 shorter events, 0.1 us)
Async XLA Ops:
  0.0 5.6 %collective-permute-start = (s32[1,64]{1,0:T(1,128)}, s32[1,64]{1,0:T(1,128)S(1)}, u32[]{:S(2)}, u32[]{:S(2)}) collective-permute-start(s32[1,64]{1,0:T(1,128)} %bitcast.26), channel_id=1, source_target_pairs={{8,0},{16,8},{24,16},{0,24},{9,1},{17,9},{25,17},{1,25},{10,2},{18... | collective-permute-start | bytes 776 | tf_op jit(solution)/shard_map/ppermute | solution.py:272
  2.4 3.2 %copy-start = (f32[1,2,1,16,768]{4,3,2,1,0:T(8,128)S(1)}, f32[1,2,1,16,768]{4,3,2,1,0:T(8,128)}, u32[]{:S(2)}) copy-start(f32[1,2,1,16,768]{4,3,2,1,0:T(8,128)} %param.11) | copy-start | bytes 294916
  5.9 6.9 %collective-permute-start.3 = (f32[32,768]{1,0:T(8,128)S(1)}, f32[32,768]{1,0:T(8,128)S(1)}, u32[]{:S(2)}, u32[]{:S(2)}) collective-permute-start(f32[32,768]{1,0:T(8,128)S(1)} %bitcast.13), channel_id=1, source_target_pairs={{0,8},{8,0},{1,9},{9,1},{2,10},{10,2},{3,11},{11,3},{4,12},{12,4},... | collective-permute-start | bytes 294920 | tf_op jit(solution)/shard_map/ppermute | solution.py:328
  5.9 3.8 %collective-permute-start.4 = (f32[32,128]{1,0:T(8,128)S(1)}, f32[32,128]{1,0:T(8,128)S(1)}, u32[]{:S(2)}, u32[]{:S(2)}) collective-permute-start(f32[32,128]{1,0:T(8,128)S(1)} %first.1), channel_id=1, source_target_pairs={{0,1},{1,0},{2,3},{3,2},{4,5},{5,4},{6,7},{7,6},{8,9},{9,8},{10,11... | collective-permute-start | bytes 49160 | tf_op jit(solution)/shard_map/ppermute | solution.py:333
  7.4 8.2 %collective-permute-start.2 = (f32[32,768]{1,0:T(8,128)S(1)}, f32[32,768]{1,0:T(8,128)S(1)}, u32[]{:S(2)}, u32[]{:S(2)}) collective-permute-start(f32[32,768]{1,0:T(8,128)S(1)} %bitcast.15), channel_id=1, source_target_pairs={{0,8},{1,10},{2,9},{3,12},{4,11},{5,14},{6,13},{7,15},{8,24},{9,25... | collective-permute-start | bytes 294920 | tf_op jit(solution)/shard_map/ppermute | solution.py:325
  7.7 8.0 %collective-permute-start.1 = (f32[32,896]{1,0:T(8,128)S(1)}, f32[32,896]{1,0:T(8,128)S(1)}, u32[]{:S(2)}, u32[]{:S(2)}) collective-permute-start(f32[32,896]{1,0:T(8,128)S(1)} %pad_maximum_fusion), channel_id=1, source_target_pairs={{0,9},{9,0},{1,8},{8,1},{2,11},{11,2},{3,10},{10,3},{4,13},{13,4},... | collective-permute-start | bytes 344072 | tf_op jit(solution)/shard_map/ppermute | solution.py:328
  9.7 6.0 %collective-permute-start.5 = (f32[32,128]{1,0:T(8,128)S(1)}, f32[32,128]{1,0:T(8,128)S(1)}, u32[]{:S(2)}, u32[]{:S(2)}) collective-permute-start(f32[32,128]{1,0:T(8,128)S(1)} %add.9), channel_id=1, source_target_pairs={{0,14},{1,15},{2,12},{3,13},{4,10},{5,11},{6,8},{7,9},{8,24},{9,25... | collective-permute-start | bytes 49160 | tf_op jit(solution)/shard_map/ppermute | solution.py:325
  12.2 3.7 %collective-permute-start.6 = (f32[32,128]{1,0:T(8,128)S(1)}, f32[32,128]{1,0:T(8,128)S(1)}, u32[]{:S(2)}, u32[]{:S(2)}) collective-permute-start(f32[32,128]{1,0:T(8,128)S(1)} %add.9), channel_id=1, source_target_pairs={{0,12},{1,13},{2,14},{3,15},{4,8},{5,9},{6,10},{7,11},{8,24},{9,25... | collective-permute-start | bytes 49160 | tf_op jit(solution)/shard_map/ppermute | solution.py:325
  12.8 3.7 %collective-permute-start.7 = (f32[32,128]{1,0:T(8,128)S(1)}, f32[32,128]{1,0:T(8,128)S(1)}, u32[]{:S(2)}, u32[]{:S(2)}) collective-permute-start(f32[32,128]{1,0:T(8,128)S(1)} %add.9), channel_id=1, source_target_pairs={{0,10},{1,11},{2,8},{3,9},{4,14},{5,15},{6,12},{7,13},{8,24},{9,25... | collective-permute-start | bytes 49160 | tf_op jit(solution)/shard_map/ppermute | solution.py:325
  16.5 5.9 %collective-permute-start.10 = (f32[32,768]{1,0:T(8,128)S(1)}, f32[32,768]{1,0:T(8,128)S(1)}, u32[]{:S(2)}, u32[]{:S(2)}) collective-permute-start(f32[32,768]{1,0:T(8,128)S(1)} %get-tuple-element.37.refs_1_), channel_id=1, source_target_pairs={{8,16},{9,17},{10,18},{11,19},{12,20},{13,21},{14,22},{15,23},{16,... | collective-permute-start | bytes 294920 | tf_op jit(solution)/shard_map/ppermute | solution.py:325
  17.4 3.7 %collective-permute-start.11 = (f32[32,128]{1,0:T(8,128)S(1)}, f32[32,128]{1,0:T(8,128)S(1)}, u32[]{:S(2)}, u32[]{:S(2)}) collective-permute-start(f32[32,128]{1,0:T(8,128)S(1)} %get-tuple-element.38), channel_id=1, source_target_pairs={{0,1},{1,0},{2,3},{3,2},{4,5},{5,4},{6,7},{7,6},{8,9},{9,8},{10,11... | collective-permute-start | bytes 49160 | tf_op jit(solution)/shard_map/ppermute | solution.py:333
  18.9 7.8 %collective-permute-start.9 = (f32[32,768]{1,0:T(8,128)S(1)}, f32[32,768]{1,0:T(8,128)S(1)}, u32[]{:S(2)}, u32[]{:S(2)}) collective-permute-start(f32[32,768]{1,0:T(8,128)S(1)} %get-tuple-element.37.refs_1_), channel_id=1, source_target_pairs={{8,16},{9,18},{10,17},{11,20},{12,19},{13,22},{14,21},{15,23},{16,... | collective-permute-start | bytes 294920 | tf_op jit(solution)/shard_map/ppermute | solution.py:325
  20.1 6.8 %collective-permute-start.8 = (f32[32,896]{1,0:T(8,128)S(1)}, f32[32,896]{1,0:T(8,128)S(1)}, u32[]{:S(2)}, u32[]{:S(2)}) collective-permute-start(f32[32,896]{1,0:T(8,128)S(1)} %pad_maximum_fusion.1), channel_id=1, source_target_pairs={{8,17},{9,16},{10,19},{11,18},{12,21},{13,20},{14,23},{15,22},{16,... | collective-permute-start | bytes 344072 | tf_op jit(solution)/shard_map/ppermute | solution.py:325
  21.1 5.9 %collective-permute-start.12 = (f32[32,128]{1,0:T(8,128)S(1)}, f32[32,128]{1,0:T(8,128)S(1)}, u32[]{:S(2)}, u32[]{:S(2)}) collective-permute-start(f32[32,128]{1,0:T(8,128)S(1)} %add.10), channel_id=1, source_target_pairs={{8,22},{9,23},{10,20},{11,21},{12,18},{13,19},{14,16},{15,17},{16,... | collective-permute-start | bytes 49160 | tf_op jit(solution)/shard_map/ppermute | solution.py:325
  21.7 5.5 %collective-permute-start.13 = (f32[32,128]{1,0:T(8,128)S(1)}, f32[32,128]{1,0:T(8,128)S(1)}, u32[]{:S(2)}, u32[]{:S(2)}) collective-permute-start(f32[32,128]{1,0:T(8,128)S(1)} %add.10), channel_id=1, source_target_pairs={{8,20},{9,21},{10,22},{11,23},{12,16},{13,17},{14,18},{15,19},{16,... | collective-permute-start | bytes 49160 | tf_op jit(solution)/shard_map/ppermute | solution.py:325
  22.5 5.6 %collective-permute-start.14 = (f32[32,128]{1,0:T(8,128)S(1)}, f32[32,128]{1,0:T(8,128)S(1)}, u32[]{:S(2)}, u32[]{:S(2)}) collective-permute-start(f32[32,128]{1,0:T(8,128)S(1)} %add.10), channel_id=1, source_target_pairs={{8,18},{9,19},{10,16},{11,17},{12,22},{13,23},{14,20},{15,21},{16,... | collective-permute-start | bytes 49160 | tf_op jit(solution)/shard_map/ppermute | solution.py:325
  28.1 7.0 %collective-permute-start.17 = (f32[32,768]{1,0:T(8,128)S(1)}, f32[32,768]{1,0:T(8,128)S(1)}, u32[]{:S(2)}, u32[]{:S(2)}) collective-permute-start(f32[32,768]{1,0:T(8,128)S(1)} %get-tuple-element.39.refs_0_), channel_id=1, source_target_pairs={{16,24},{24,16},{17,25},{25,17},{18,26},{26,18},{19,27},{27,19},{2... | collective-permute-start | bytes 294920 | tf_op jit(solution)/shard_map/ppermute | solution.py:328
  28.2 3.8 %collective-permute-start.18 = (f32[32,128]{1,0:T(8,128)S(1)}, f32[32,128]{1,0:T(8,128)S(1)}, u32[]{:S(2)}, u32[]{:S(2)}) collective-permute-start(f32[32,128]{1,0:T(8,128)S(1)} %get-tuple-element.40), channel_id=1, source_target_pairs={{0,1},{1,0},{2,3},{3,2},{4,5},{5,4},{6,7},{7,6},{8,9},{9,8},{10,11... | collective-permute-start | bytes 49160 | tf_op jit(solution)/shard_map/ppermute | solution.py:333
  28.9 6.5 %collective-permute-start.16 = (f32[32,768]{1,0:T(8,128)S(1)}, f32[32,768]{1,0:T(8,128)S(1)}, u32[]{:S(2)}, u32[]{:S(2)}) collective-permute-start(f32[32,768]{1,0:T(8,128)S(1)} %get-tuple-element.39.refs_0_), channel_id=1, source_target_pairs={{16,24},{17,26},{18,25},{19,28},{20,27},{21,30},{22,29},{23,31},{2... | collective-permute-start | bytes 294920 | tf_op jit(solution)/shard_map/ppermute | solution.py:325
  30.9 4.5 %collective-permute-start.15 = (f32[32,896]{1,0:T(8,128)S(1)}, f32[32,896]{1,0:T(8,128)S(1)}, u32[]{:S(2)}, u32[]{:S(2)}) collective-permute-start(f32[32,896]{1,0:T(8,128)S(1)} %pad_maximum_fusion.2), channel_id=1, source_target_pairs={{16,25},{25,16},{17,24},{24,17},{18,27},{27,18},{19,26},{26,19},{2... | collective-permute-start | bytes 344072 | tf_op jit(solution)/shard_map/ppermute | solution.py:328
  32.0 3.5 %collective-permute-start.19 = (f32[32,128]{1,0:T(8,128)S(1)}, f32[32,128]{1,0:T(8,128)S(1)}, u32[]{:S(2)}, u32[]{:S(2)}) collective-permute-start(f32[32,128]{1,0:T(8,128)S(1)} %add.11), channel_id=1, source_target_pairs={{16,30},{17,31},{18,28},{19,29},{20,26},{21,27},{22,24},{23,25},{2... | collective-permute-start | bytes 49160 | tf_op jit(solution)/shard_map/ppermute | solution.py:325
  34.1 2.4 %collective-permute-start.20 = (f32[32,128]{1,0:T(8,128)S(1)}, f32[32,128]{1,0:T(8,128)S(1)}, u32[]{:S(2)}, u32[]{:S(2)}) collective-permute-start(f32[32,128]{1,0:T(8,128)S(1)} %add.11), channel_id=1, source_target_pairs={{16,28},{17,29},{18,30},{19,31},{20,24},{21,25},{22,26},{23,27},{2... | collective-permute-start | bytes 49160 | tf_op jit(solution)/shard_map/ppermute | solution.py:325
  35.1 1.8 %collective-permute-start.21 = (f32[32,128]{1,0:T(8,128)S(1)}, f32[32,128]{1,0:T(8,128)S(1)}, u32[]{:S(2)}, u32[]{:S(2)}) collective-permute-start(f32[32,128]{1,0:T(8,128)S(1)} %add.11), channel_id=1, source_target_pairs={{16,26},{17,27},{18,24},{19,25},{20,30},{21,31},{22,28},{23,29},{2... | collective-permute-start | bytes 49160 | tf_op jit(solution)/shard_map/ppermute | solution.py:325
